TPU v7x, 512 devices: a whole 4x4x16 slice. The times are simulated.
512 devices in a mesh: cuts: 64 (over z, x_lo, core), event: 8 (over y, x_hi).
Axes of the slice: x: 4 (x_hi: 2, x_lo: 2; x = x_hi * 2 + x_lo), y: 4, z: 16, core: 2. Of those that a mesh axis runs over, the one named last changes fastest.
Arguments:
- adjoint_now: float32 [8, 17, 33, 8192], P('event', None, None, 'cuts'), may hold values from -6 to 6
- adjoint_prev: float32 [8, 17, 33, 8192], P('event', None, None, 'cuts'), may hold values from -6 to 6
- backward_now: float32 [8, 17, 33, 8192], P('event', None, None, 'cuts'), may hold values from -6 to 6
- backward_prev: float32 [8, 17, 33, 8192], P('event', None, None, 'cuts'), may hold values from -6 to 6
- kappa: float32 [17, 33, 8192], P(None, None, 'cuts'), may hold values from 1 to 4
- density: float32 [17, 33, 8192], P(None, None, 'cuts'), may hold values from 1 to 2
- edge_flip: int32 [64], P('cuts'), may hold values 0 or 1
- receiver_index: int32 [1024], P('cuts'), may hold values from 0 to 71807
- adjoint_source: float32 [8, 2, 1024], P('event', None, 'cuts'), may hold values from -150 to 150
Outputs:
- adjoint_final: float32 [8, 17, 33, 8192], P('event', None, None, 'cuts')
- adjoint_last: float32 [8, 17, 33, 8192], P('event', None, None, 'cuts')
- backward_final: float32 [8, 17, 33, 8192], P('event', None, None, 'cuts')
- backward_last: float32 [8, 17, 33, 8192], P('event', None, None, 'cuts')
- smoothed_kernel: float32 [17, 33, 8192], P(None, None, 'cuts')
Inputs may be any that keep to these rules, and one draw needn't show every extreme that they name: receiver_index[r] names a point of slice r // 16; several receivers may share a point. `edge_flip`: 1 where the interface after a slice reverses the second dimension.
All inputs are finite; a program needn't handle non-finite values. No bound on the sum of `edge_flip` on one device may be relied on, other than what follows from the above.
Results may differ from a plain program's by a relative error of at most 0.00012.
Values sent between devices are 32-bit elements; how exact they have to be, the bound alone decides.
No kernel may reach another device: no remote copies, remote signals or barrier semaphores. Data moves between devices by JAX's collectives and lax.ppermute only.
A program may use at most 64 MiB of HBM per device.

v0:
```python
import jax
import jax.numpy as jnp
import numpy as np
from jax import lax
from jax.sharding import PartitionSpec as P

DT2 = 0.003
SIGMA_Y = 1.0
HIGHEST = lax.Precision.HIGHEST


def from_behind(shard, axis, by):
    peers = lax.axis_size(axis)
    return lax.ppermute(shard, axis, [(i, (i + by) % peers) for i in range(peers)])


def gll_tables():
    gll_nodes = np.array([-1.0, -np.sqrt(3.0 / 7.0), 0.0, np.sqrt(3.0 / 7.0), 1.0])
    weights = np.array([0.1, 49.0 / 90.0, 32.0 / 45.0, 49.0 / 90.0, 0.1])
    derivative = np.zeros((5, 5))
    for a in range(5):
        for b in range(5):
            summed = 0.0
            for m in range(5):
                if m == b:
                    continue
                factor = 1.0 / (gll_nodes[b] - gll_nodes[m])
                for k in range(5):
                    if k == b or k == m:
                        continue
                    factor = factor * (gll_nodes[a] - gll_nodes[k]) / (gll_nodes[b] - gll_nodes[k])
                summed = summed + factor
            derivative[a, b] = summed
    return (weights, derivative)


def line_weights(element_count):
    weights, derivative = gll_tables()
    summed = np.zeros(4 * element_count + 1)
    for element in range(element_count):
        summed[4 * element : 4 * element + 5] += weights
    return summed


def loop_weights(element_count):
    summed = line_weights(element_count)
    summed[0] += summed[-1]
    return summed[:-1]


def element_tables(element_count):
    weights, derivative = gll_tables()
    applied = np.zeros((5 * element_count, 4 * element_count + 1))
    picked = np.zeros((5 * element_count, 4 * element_count + 1))
    for element in range(element_count):
        applied[5 * element : 5 * element + 5, 4 * element : 4 * element + 5] = derivative
        picked[5 * element : 5 * element + 5, 4 * element : 4 * element + 5] = np.eye(5)
    node_weights = np.tile(weights, element_count)
    return (
        jnp.asarray(applied, jnp.float32),
        jnp.asarray(picked, jnp.float32),
        jnp.asarray(node_weights, jnp.float32),
    )


def build_tables(count_ext, count_x, count_y, count_z):
    return (
        element_tables(count_ext),
        element_tables(count_y),
        element_tables(count_z),
        jnp.asarray(loop_weights(count_x), jnp.float32),
        jnp.asarray(line_weights(count_y), jnp.float32),
        jnp.asarray(line_weights(count_z), jnp.float32),
    )


def smoothing_tables(columns, points_y):
    offsets = np.arange(3 * columns)[:, None] - columns - np.arange(columns)[None, :]
    sigma_x = columns / 2.0
    gauss_x = np.exp(-0.5 * (offsets / sigma_x) ** 2) * (np.abs(offsets) <= columns)
    normal_x = np.exp(-0.5 * (np.arange(-columns, columns + 1) / sigma_x) ** 2).sum()
    distance = np.arange(points_y)[:, None] - np.arange(points_y)[None, :]
    gauss_y = np.exp(-0.5 * (distance / SIGMA_Y) ** 2)
    gauss_y = gauss_y / gauss_y.sum(axis=1, keepdims=True)
    return (jnp.asarray(gauss_x / normal_x, jnp.float32), jnp.asarray(gauss_y, jnp.float32))


def make_coefs(kappa_grid, kappa_ext, tables):
    table_x, table_y, table_z, weight_x, weight_y, weight_z = tables
    coef_x = jnp.einsum("...p,np->...n", kappa_ext, table_x[1], precision=HIGHEST) * (
        weight_z[:, None, None] * weight_y[None, :, None] * table_x[2][None, None, :]
    )
    coef_y = jnp.einsum("ny,...yx->...nx", table_y[1], kappa_grid, precision=HIGHEST) * (
        weight_z[:, None, None] * table_y[2][None, :, None] * weight_x[None, None, :]
    )
    coef_z = jnp.einsum("nz,...zyx->...nyx", table_z[1], kappa_grid, precision=HIGHEST) * (
        table_z[2][:, None, None] * weight_y[None, :, None] * weight_x[None, None, :]
    )
    return (coef_x, coef_y, coef_z)


def stiffness(wavefield, wavefield_ext, coefficients, tables):
    table_x, table_y, table_z = (tables[0], tables[1], tables[2])
    grad_x = jnp.einsum("...p,np->...n", wavefield_ext, table_x[0], precision=HIGHEST)
    part_x = jnp.einsum("...n,np->...p", coefficients[0] * grad_x, table_x[0], precision=HIGHEST)
    grad_y = jnp.einsum("ny,...yx->...nx", table_y[0], wavefield, precision=HIGHEST)
    part_y = jnp.einsum("ny,...nx->...yx", table_y[0], coefficients[1] * grad_y, precision=HIGHEST)
    grad_z = jnp.einsum("nz,...zyx->...nyx", table_z[0], wavefield, precision=HIGHEST)
    part_z = jnp.einsum(
        "nz,...nyx->...zyx", table_z[0], coefficients[2] * grad_z, precision=HIGHEST
    )
    return (part_x, part_y + part_z)


def reorient(planes, flip_flag):
    return jnp.where(flip_flag != 0, jnp.flip(planes, -2), planes)


def smooth_x(kernel_part, flip_flag, table_x):
    left_part = from_behind(reorient(kernel_part, flip_flag), "cuts", 1)
    right_part = reorient(from_behind(kernel_part, "cuts", -1), flip_flag)
    extended = jnp.concatenate([left_part, kernel_part, right_part], -1)
    return jnp.einsum("...j,ji->...i", extended, table_x, precision=HIGHEST)


def local(
    adjoint_now,
    adjoint_prev,
    backward_now,
    backward_prev,
    kappa,
    density,
    edge_flip,
    receiver_index,
    adjoint_source,
):
    flip_flag = edge_flip[0]
    columns = kappa.shape[-1]
    count_x = columns // 4
    count_y = (kappa.shape[1] - 1) // 4
    count_z = (kappa.shape[0] - 1) // 4
    kappa_right = reorient(from_behind(kappa[:, :, 0:1], "cuts", -1), flip_flag)
    tables = build_tables(count_x, count_x, count_y, count_z)
    kappa_ext = jnp.concatenate([kappa, kappa_right], -1)
    coefficients = make_coefs(kappa, kappa_ext, tables)
    mass_matrix = density * (
        tables[5][:, None, None] * tables[4][None, :, None] * tables[3][None, None, :]
    )
    events = adjoint_now.shape[0]
    adj_now, adj_prev, back_now, back_prev = (
        adjoint_now,
        adjoint_prev,
        backward_now,
        backward_prev,
    )
    kernel = jnp.zeros_like(adj_now)
    for instant in range(adjoint_source.shape[1]):
        forcing = (
            jnp.zeros((events, kappa.size), jnp.float32)
            .at[:, receiver_index]
            .add(adjoint_source[:, instant, :])
        )
        planes = from_behind((adj_now[..., 0:1], back_now[..., 0:1]), "cuts", -1)
        right_adj = reorient(planes[0], flip_flag)
        right_back = reorient(planes[1], flip_flag)
        part_adj, rest_adj = stiffness(
            adj_now, jnp.concatenate([adj_now, right_adj], -1), coefficients, tables
        )
        part_back, rest_back = stiffness(
            back_now, jnp.concatenate([back_now, right_back], -1), coefficients, tables
        )
        returned = from_behind(
            (
                reorient(part_adj[..., columns:], flip_flag),
                reorient(part_back[..., columns:], flip_flag),
            ),
            "cuts",
            1,
        )
        owned_adj = jnp.concatenate(
            [part_adj[..., 0:1] + returned[0], part_adj[..., 1:columns]], -1
        )
        owned_back = jnp.concatenate(
            [part_back[..., 0:1] + returned[1], part_back[..., 1:columns]], -1
        )
        stiff_adj = owned_adj + rest_adj
        stiff_back = owned_back + rest_back
        accel_adj = (forcing.reshape(adj_now.shape) - stiff_adj) / mass_matrix
        accel_back = (0.0 - stiff_back) / mass_matrix
        kernel = kernel + DT2 * back_now * accel_adj
        adj_now, adj_prev = (2.0 * adj_now - adj_prev + DT2 * accel_adj, adj_now)
        back_now, back_prev = (2.0 * back_now - back_prev + DT2 * accel_back, back_now)
    kernel_local = jnp.sum(kernel, axis=0)
    table_x, table_y = smoothing_tables(columns, kappa.shape[1])
    smoothed = smooth_x(lax.psum(kernel_local, "event"), flip_flag, table_x)
    result = jnp.einsum("yv,...vx->...yx", table_y, smoothed, precision=HIGHEST)
    return (adj_now, adj_prev, back_now, back_prev, result)


def solution(mesh):
    placed = (
        P("event", None, None, "cuts"),
        P("event", None, None, "cuts"),
        P("event", None, None, "cuts"),
        P("event", None, None, "cuts"),
        P(None, None, "cuts"),
        P(None, None, "cuts"),
        P("cuts"),
        P("cuts"),
        P("event", None, "cuts"),
    )
    return jax.shard_map(
        local,
        mesh=mesh,
        in_specs=placed,
        out_specs=(
            P("event", None, None, "cuts"),
            P("event", None, None, "cuts"),
            P("event", None, None, "cuts"),
            P("event", None, None, "cuts"),
            P(None, None, "cuts"),
        ),
        check_vma=False,
    )
```

profile of v0, /device:TPU:1, one launch (start us, length us, event | category | flops | bytes accessed | tf_op | source)
XLA Modules:
  0.0 218.3 jit_solution(1065161665501299545)
XLA Ops:
  7.2 8.8 %collective-permute-start = (f32[17,33,1]{2,1,0:T(8,128)}, f32[17,33,1]{2,1,0:T(8,128)S(1)}, u32[]{:S(2)}, u32[]{:S(2)}) collective-permute-start(f32[17,33,1]{2,1,0:T(8,128)} %bitcast.278), channel_id=1, source_target_pairs={{0,504},{8,0},{16,8},{24,16},{32,24},{40,32},{48,40},{56,48},{64,5... | collective-permute-start | bytes 6740 | tf_op jit(solution)/shard_map/ppermute | solution.py:14
  16.0 1.0 copy.159
  17.1 6.5 %collective-permute-start.1 = (f32[1,17,33,1]{3,2,1,0:T(8,128)S(1)}, f32[1,17,33,1]{3,2,1,0:T(8,128)S(1)}, u32[]{:S(2)}, u32[]{:S(2)}) collective-permute-start(f32[1,17,33,1]{3,2,1,0:T(8,128)S(1)} %copy.159), channel_id=1, source_target_pairs={{0,504},{8,0},{16,8},{24,16},{32,24},{40,32},{48,40},{56,48},{64,5... | collective-permute-start | bytes 6740 | tf_op jit(solution)/shard_map/ppermute | solution.py:14
  23.6 0.8 copy.160
  24.4 2.7 %collective-permute-start.5 = (f32[1,17,33,1]{3,2,1,0:T(8,128)}, f32[1,17,33,1]{3,2,1,0:T(8,128)}, u32[]{:S(2)}, u32[]{:S(2)}) collective-permute-start(f32[1,17,33,1]{3,2,1,0:T(8,128)} %copy.160), channel_id=1, source_target_pairs={{0,504},{8,0},{16,8},{24,16},{32,24},{40,32},{48,40},{56,48},{64,5... | collective-permute-start | bytes 6740 | tf_op jit(solution)/shard_map/ppermute | solution.py:14
  29.4 1.3 fusion.74
  31.4 0.6 copy-done.34
  32.1 1.3 fusion.76
  34.1 1.2 fusion.12
  35.3 1.2 fusion.18
  37.1 0.7 scatter_custom_fusion
  37.8 0.8 reshape.203
  38.6 0.7 scatter_custom_fusion.1
  39.3 0.7 reshape.208
  41.3 0.8 copy-done.23
  42.1 0.7 convolution_multiply_fusion.4
  43.1 0.7 convolution_multiply_fusion.3
  43.8 0.7 convolution_bitcast_fusion.3
  44.5 0.8 rev.38
  45.4 0.8 broadcast_select_fusion.8
  46.1 3.9 %collective-permute-start.2 = (f32[1,17,33,1]{3,2,1,0:T(8,128)}, f32[1,17,33,1]{3,2,1,0:T(8,128)}, u32[]{:S(2)}, u32[]{:S(2)}) collective-permute-start(f32[1,17,33,1]{3,2,1,0:T(8,128)} %broadcast_select_fusion.8), channel_id=1, source_target_pairs={{0,8},{8,16},{16,24},{24,32},{32,40},{40,48},{48,56},{56,64},{64,7... | collective-permute-start | bytes 6740 | tf_op jit(solution)/shard_map/ppermute | solution.py:14
  50.1 1.1 rev.41
  51.2 1.0 broadcast_select_fusion.5
  53.1 0.7 convolution_multiply_fusion.1
  53.8 0.7 convolution_bitcast_fusion.1
  54.5 0.8 copy-done.3
  55.4 0.8 rev.42
  56.2 1.1 broadcast_select_fusion.4
  57.7 2.2 %collective-permute-start.6 = (f32[1,17,33,1]{3,2,1,0:T(8,128)S(1)}, f32[1,17,33,1]{3,2,1,0:T(8,128)S(1)}, u32[]{:S(2)}, u32[]{:S(2)}) collective-permute-start(f32[1,17,33,1]{3,2,1,0:T(8,128)S(1)} %broadcast_select_fusion.4), channel_id=1, source_target_pairs={{0,8},{8,16},{16,24},{24,32},{32,40},{40,48},{48,56},{56,64},{64,7... | collective-permute-start | bytes 6740 | tf_op jit(solution)/shard_map/ppermute | solution.py:14
  59.9 1.0 slice_add_fusion.3
  61.0 1.5 fusion.63
  62.5 1.2 fusion.15
  63.6 2.5 %collective-permute-start.3 = (f32[1,17,33,1]{3,2,1,0:T(8,128)S(1)}, f32[1,17,33,1]{3,2,1,0:T(8,128)S(1)}, u32[]{:S(2)}, u32[]{:S(2)}) collective-permute-start(f32[1,17,33,1]{3,2,1,0:T(8,128)S(1)} %bitcast.274), channel_id=1, source_target_pairs={{0,504},{8,0},{16,8},{24,16},{32,24},{40,32},{48,40},{56,48},{64,5... | collective-permute-start | bytes 6740 | tf_op jit(solution)/shard_map/ppermute | solution.py:14
  66.2 1.5 collective-permute-done.6
  67.8 0.7 fusion.54
  68.9 1.9 collective-permute-start.7
  72.4 1.2 fusion.22
  74.4 0.7 convolution_multiply_fusion.2
  75.1 0.7 convolution_bitcast_fusion.2
  75.9 0.8 slice.82
  76.6 1.8 rev.40
  78.4 0.8 broadcast_select_fusion.6
  79.2 5.3 %collective-permute-start.4 = (f32[1,17,33,1]{3,2,1,0:T(8,128)}, f32[1,17,33,1]{3,2,1,0:T(8,128)}, u32[]{:S(2)}, u32[]{:S(2)}) collective-permute-start(f32[1,17,33,1]{3,2,1,0:T(8,128)} %broadcast_select_fusion.6), channel_id=1, source_target_pairs={{0,8},{8,16},{16,24},{24,32},{32,40},{40,48},{48,56},{56,64},{64,7... | collective-permute-start | bytes 6740 | tf_op jit(solution)/shard_map/ppermute | solution.py:14
  84.6 1.8 rev.43
  86.3 1.0 broadcast_select_fusion.3
  87.4 0.7 convolution_multiply_fusion
  88.1 0.7 convolution_bitcast_fusion
  88.8 0.8 slice.90
  89.6 1.8 rev.44
  91.7 2.9 %collective-permute-start.8 = (f32[1,17,33,1]{3,2,1,0:T(8,128)S(1)}, f32[1,17,33,1]{3,2,1,0:T(8,128)S(1)}, u32[]{:S(2)}, u32[]{:S(2)}) collective-permute-start(f32[1,17,33,1]{3,2,1,0:T(8,128)S(1)} %broadcast_select_fusion.2), channel_id=1, source_target_pairs={{0,8},{8,16},{16,24},{24,32},{32,40},{40,48},{48,56},{56,64},{64,7... | collective-permute-start | bytes 6740 | tf_op jit(solution)/shard_map/ppermute | solution.py:14
  94.7 1.1 slice_add_fusion.2
  95.8 3.0 %collective-permute-done.8 = f32[1,17,33,1]{3,2,1,0:T(8,128)S(1)} collective-permute-done((f32[1,17,33,1]{3,2,1,0:T(8,128)S(1)}, f32[1,17,33,1]{3,2,1,0:T(8,128)S(1)}, u32[]{:S(2)}, u32[]{:S(2)}) %collective-permute-start.8) | collective-permute-done | bytes 2276 | tf_op jit(solution)/shard_map/ppermute | solution.py:14
  98.9 1.6 add_bitcast_fusion
  100.6 90.8 %all-reduce.2.cloned.1.call-done = f32[17,33,128]{2,1,0:T(8,128)} async-done(((f32[17,33,128]{2,1,0:T(8,128)}), f32[17,33,128]{2,1,0:T(8,128)}) %all-reduce.2.cloned.1.call-update) | async-done | bytes 287248 | tf_op jit(solution)/shard_map/psum | solution.py:195
  191.4 8.1 %collective-permute-start.10 = (f32[17,33,128]{2,1,0:T(8,128)}, f32[17,33,128]{2,1,0:T(8,128)S(1)}, u32[]{:S(2)}, u32[]{:S(2)}) collective-permute-start(f32[17,33,128]{2,1,0:T(8,128)} %all-reduce.2.cloned.1.call-done), channel_id=1, source_target_pairs={{0,504},{8,0},{16,8},{24,16},{32,24},{40,32},{48,40},{56,48},{64,5... | collective-permute-start | bytes 861704 | tf_op jit(solution)/shard_map/ppermute | solution.py:14
  199.5 1.1 rev.45
  200.7 2.4 %collective-permute-start.9 = (f32[17,33,128]{2,1,0:T(8,128)S(1)}, f32[17,33,128]{2,1,0:T(8,128)S(1)}, u32[]{:S(2)}, u32[]{:S(2)}) collective-permute-start(f32[17,33,128]{2,1,0:T(8,128)S(1)} %broadcast_select_fusion.1), channel_id=1, source_target_pairs={{0,8},{8,16},{16,24},{24,32},{32,40},{40,48},{48,56},{56,64},{64,7... | collective-permute-start | bytes 861704 | tf_op jit(solution)/shard_map/ppermute | solution.py:14
  203.1 1.0 copy.89
  204.1 1.0 copy.91
  205.1 1.0 copy.88
  206.2 1.0 copy.90
  207.3 1.7 collective-permute-done.9
  209.0 1.2 fusion.23
  210.3 1.2 convolution_bitcast_fusion.8
  (113 shorter events, 9.7 us)
Async XLA Ops:
  7.2 184.3 %all-reduce.2.cloned.1.call-start = ((), (), s32[]{:S(2)}) async-start(), calls=%async_computation | async-start | bytes 696320 | tf_op jit(solution)/shard_map/psum | solution.py:195
  7.2 33.9 %collective-permute-start = (f32[17,33,1]{2,1,0:T(8,128)}, f32[17,33,1]{2,1,0:T(8,128)S(1)}, u32[]{:S(2)}, u32[]{:S(2)}) collective-permute-start(f32[17,33,1]{2,1,0:T(8,128)} %bitcast.278), channel_id=1, source_target_pairs={{0,504},{8,0},{16,8},{24,16},{32,24},{40,32},{48,40},{56,48},{64,5... | collective-permute-start | bytes 6740 | tf_op jit(solution)/shard_map/ppermute | solution.py:14
  16.0 7.6 %copy-start = (f32[1,17,33,128]{3,0,2,1:T(1,128)S(1)}, f32[1,17,33,128]{3,0,2,1:T(1,128)}, u32[]{:S(2)}) copy-start(f32[1,17,33,128]{3,0,2,1:T(1,128)} %param.25) | copy-start | bytes 861700
  17.0 10.2 %copy-start.5 = (f32[17,33,128]{2,1,0:T(8,128)S(1)}, f32[17,33,128]{2,1,0:T(8,128)}, u32[]{:S(2)}) copy-start(f32[17,33,128]{2,1,0:T(8,128)} %param.27) | copy-start | bytes 861700
  17.1 23.0 %collective-permute-start.1 = (f32[1,17,33,1]{3,2,1,0:T(8,128)S(1)}, f32[1,17,33,1]{3,2,1,0:T(8,128)S(1)}, u32[]{:S(2)}, u32[]{:S(2)}) collective-permute-start(f32[1,17,33,1]{3,2,1,0:T(8,128)S(1)} %copy.159), channel_id=1, source_target_pairs={{0,504},{8,0},{16,8},{24,16},{32,24},{40,32},{48,40},{56,48},{64,5... | collective-permute-start | bytes 6740 | tf_op jit(solution)/shard_map/ppermute | solution.py:14
  23.6 3.5 %copy-start.28 = (f32[33]{0:T(128)S(1)}, f32[33]{0:T(128)}, u32[]{:S(2)}) copy-start(f32[33]{0:T(128)} %constant.53.clone) | copy-start | bytes 400
  23.6 3.5 %copy-start.32 = (f32[20]{0:T(128)S(1)}, f32[20]{0:T(128)}, u32[]{:S(2)}) copy-start(f32[20]{0:T(128)} %constant.51.clone) | copy-start | bytes 244
  24.4 2.8 %copy-start.26 = (f32[128]{0:T(128)S(1)}, f32[128]{0:T(128)}, u32[]{:S(2)}) copy-start(f32[128]{0:T(128)} %constant.52.clone) | copy-start | bytes 1540
  24.4 2.8 %copy-start.27 = (f32[20,17,1]{1,0,2:T(8,128)S(1)}, f32[20,17,1]{1,0,2:T(8,128)}, u32[]{:S(2)}) copy-start(f32[20,17,1]{1,0,2:T(8,128)} %constant.68) | copy-start | bytes 4084
  24.4 25.7 %collective-permute-start.5 = (f32[1,17,33,1]{3,2,1,0:T(8,128)}, f32[1,17,33,1]{3,2,1,0:T(8,128)}, u32[]{:S(2)}, u32[]{:S(2)}) collective-permute-start(f32[1,17,33,1]{3,2,1,0:T(8,128)} %copy.160), channel_id=1, source_target_pairs={{0,504},{8,0},{16,8},{24,16},{32,24},{40,32},{48,40},{56,48},{64,5... | collective-permute-start | bytes 6740 | tf_op jit(solution)/shard_map/ppermute | solution.py:14
  27.2 1.0 copy-start.1
  27.2 1.0 copy-start.19
  28.7 0.7 copy-start.29
  29.4 1.3 copy-start.33
  30.7 0.7 copy-start.30
  31.4 0.7 copy-start.34
  32.0 1.3 copy-start.25
  33.4 0.7 copy-start.18
  41.2 0.9 copy-start.23
  41.2 0.9 copy-start.31
  42.1 0.9 copy-start.2
  46.1 13.8 %collective-permute-start.2 = (f32[1,17,33,1]{3,2,1,0:T(8,128)}, f32[1,17,33,1]{3,2,1,0:T(8,128)}, u32[]{:S(2)}, u32[]{:S(2)}) collective-permute-start(f32[1,17,33,1]{3,2,1,0:T(8,128)} %broadcast_select_fusion.8), channel_id=1, source_target_pairs={{0,8},{8,16},{16,24},{24,32},{32,40},{40,48},{48,56},{56,64},{64,7... | collective-permute-start | bytes 6740 | tf_op jit(solution)/shard_map/ppermute | solution.py:14
  54.5 0.9 copy-start.3
  56.2 1.2 copy-start.4
  57.5 3.5 %copy-start.11 = (f32[1,17,33,128]{3,2,1,0:T(8,128)S(1)}, f32[1,17,33,128]{3,2,1,0:T(8,128)}, u32[]{:S(2)}) copy-start(f32[1,17,33,128]{3,2,1,0:T(8,128)} %reshape.203) | copy-start | bytes 861700
  57.5 3.5 %copy-start.13 = (f32[17,40,128]{2,1,0:T(8,128)S(1)}, f32[17,40,128]{2,1,0:T(8,128)}, u32[]{:S(2)}) copy-start(f32[17,40,128]{2,1,0:T(8,128)} %fusion.12) | copy-start | bytes 1044484
  57.6 3.3 %copy-start.6 = (f32[17,33,128]{2,1,0:T(8,128)S(1)}, f32[17,33,128]{2,1,0:T(8,128)}, u32[]{:S(2)}) copy-start(f32[17,33,128]{2,1,0:T(8,128)} %param.28) | copy-start | bytes 861700
  57.7 3.3 %copy-start.10 = (f32[33,128,17]{1,2,0:T(8,128)S(1)}, f32[33,128,17]{1,2,0:T(8,128)}, u32[]{:S(2)}) copy-start(f32[33,128,17]{1,2,0:T(8,128)} %fusion.74) | copy-start | bytes 861700
  57.7 3.3 %copy-start.20 = (f32[1,17,33,128]{3,0,2,1:T(1,128)S(1)}, f32[1,17,33,128]{3,0,2,1:T(1,128)}, u32[]{:S(2)}) copy-start(f32[1,17,33,128]{3,0,2,1:T(1,128)} %param.24) | copy-start | bytes 861700
  57.7 10.0 %collective-permute-start.6 = (f32[1,17,33,1]{3,2,1,0:T(8,128)S(1)}, f32[1,17,33,1]{3,2,1,0:T(8,128)S(1)}, u32[]{:S(2)}, u32[]{:S(2)}) collective-permute-start(f32[1,17,33,1]{3,2,1,0:T(8,128)S(1)} %broadcast_select_fusion.4), channel_id=1, source_target_pairs={{0,8},{8,16},{16,24},{24,32},{32,40},{40,48},{48,56},{56,64},{64,7... | collective-permute-start | bytes 6740 | tf_op jit(solution)/shard_map/ppermute | solution.py:14
  63.6 4.1 %copy-start.9 = (f32[33,128,17]{1,2,0:T(8,128)S(1)}, f32[33,128,17]{1,2,0:T(8,128)}, u32[]{:S(2)}) copy-start(f32[33,128,17]{1,2,0:T(8,128)} %fusion.76) | copy-start | bytes 861700
  63.6 4.1 %copy-start.12 = (f32[17,40,128]{2,1,0:T(8,128)S(1)}, f32[17,40,128]{2,1,0:T(8,128)}, u32[]{:S(2)}) copy-start(f32[17,40,128]{2,1,0:T(8,128)} %fusion.18) | copy-start | bytes 1044484
  63.6 4.1 %copy-start.21 = (f32[1,17,33,128]{3,0,2,1:T(1,128)S(1)}, f32[1,17,33,128]{3,0,2,1:T(1,128)}, u32[]{:S(2)}) copy-start(f32[1,17,33,128]{3,0,2,1:T(1,128)} %param.26) | copy-start | bytes 861700
  63.6 10.6 %collective-permute-start.3 = (f32[1,17,33,1]{3,2,1,0:T(8,128)S(1)}, f32[1,17,33,1]{3,2,1,0:T(8,128)S(1)}, u32[]{:S(2)}, u32[]{:S(2)}) collective-permute-start(f32[1,17,33,1]{3,2,1,0:T(8,128)S(1)} %bitcast.274), channel_id=1, source_target_pairs={{0,504},{8,0},{16,8},{24,16},{32,24},{40,32},{48,40},{56,48},{64,5... | collective-permute-start | bytes 6740 | tf_op jit(solution)/shard_map/ppermute | solution.py:14
  68.9 15.7 %collective-permute-start.7 = (f32[1,17,33,1]{3,2,1,0:T(8,128)S(1)}, f32[1,17,33,1]{3,2,1,0:T(8,128)}, u32[]{:S(2)}, u32[]{:S(2)}) collective-permute-start(f32[1,17,33,1]{3,2,1,0:T(8,128)S(1)} %bitcast.276), channel_id=1, source_target_pairs={{0,504},{8,0},{16,8},{24,16},{32,24},{40,32},{48,40},{56,48},{64,5... | collective-permute-start | bytes 6740 | tf_op jit(solution)/shard_map/ppermute | solution.py:14
  79.2 15.4 %collective-permute-start.4 = (f32[1,17,33,1]{3,2,1,0:T(8,128)}, f32[1,17,33,1]{3,2,1,0:T(8,128)}, u32[]{:S(2)}, u32[]{:S(2)}) collective-permute-start(f32[1,17,33,1]{3,2,1,0:T(8,128)} %broadcast_select_fusion.6), channel_id=1, source_target_pairs={{0,8},{8,16},{16,24},{24,32},{32,40},{40,48},{48,56},{56,64},{64,7... | collective-permute-start | bytes 6740 | tf_op jit(solution)/shard_map/ppermute | solution.py:14
  91.7 7.1 %collective-permute-start.8 = (f32[1,17,33,1]{3,2,1,0:T(8,128)S(1)}, f32[1,17,33,1]{3,2,1,0:T(8,128)S(1)}, u32[]{:S(2)}, u32[]{:S(2)}) collective-permute-start(f32[1,17,33,1]{3,2,1,0:T(8,128)S(1)} %broadcast_select_fusion.2), channel_id=1, source_target_pairs={{0,8},{8,16},{16,24},{24,32},{32,40},{40,48},{48,56},{56,64},{64,7... | collective-permute-start | bytes 6740 | tf_op jit(solution)/shard_map/ppermute | solution.py:14
  94.6 4.2 %copy-start.16 = (f32[17,40,128]{2,1,0:T(8,128)S(1)}, f32[17,40,128]{2,1,0:T(8,128)}, u32[]{:S(2)}) copy-start(f32[17,40,128]{2,1,0:T(8,128)} %fusion.15) | copy-start | bytes 1044484
  94.7 4.2 %copy-start.17 = (f32[1,17,33,128]{3,2,1,0:T(8,128)S(1)}, f32[1,17,33,128]{3,2,1,0:T(8,128)}, u32[]{:S(2)}) copy-start(f32[1,17,33,128]{3,2,1,0:T(8,128)} %fusion.22) | copy-start | bytes 861700
  95.8 3.1 %copy-start.7 = (f32[17,33,128]{2,1,0:T(8,128)S(1)}, f32[17,33,128]{2,1,0:T(8,128)}, u32[]{:S(2)}) copy-start(f32[17,33,128]{2,1,0:T(8,128)} %param.28) | copy-start | bytes 861700
  95.8 3.1 %copy-start.14 = (f32[1,17,33,128]{3,2,1,0:T(8,128)S(1)}, f32[1,17,33,128]{3,2,1,0:T(8,128)}, u32[]{:S(2)}) copy-start(f32[1,17,33,128]{3,2,1,0:T(8,128)} %get-tuple-element.21) | copy-start | bytes 861700
  95.8 3.1 %copy-start.15 = (f32[1,17,33,128]{3,2,1,0:T(8,128)S(1)}, f32[1,17,33,128]{3,2,1,0:T(8,128)}, u32[]{:S(2)}) copy-start(f32[1,17,33,128]{3,2,1,0:T(8,128)} %reshape.208) | copy-start | bytes 861700
  191.4 9.2 %copy-start.8 = (f32[17,33,128]{2,1,0:T(8,128)S(1)}, f32[17,33,128]{2,1,0:T(8,128)}, u32[]{:S(2)}) copy-start(f32[17,33,128]{2,1,0:T(8,128)} %all-reduce.2.cloned.1.call-done) | copy-start | bytes 861700
  191.4 15.7 %collective-permute-start.10 = (f32[17,33,128]{2,1,0:T(8,128)}, f32[17,33,128]{2,1,0:T(8,128)S(1)}, u32[]{:S(2)}, u32[]{:S(2)}) collective-permute-start(f32[17,33,128]{2,1,0:T(8,128)} %all-reduce.2.cloned.1.call-done), channel_id=1, source_target_pairs={{0,504},{8,0},{16,8},{24,16},{32,24},{40,32},{48,40},{56,48},{64,5... | collective-permute-start | bytes 861704 | tf_op jit(solution)/shard_map/ppermute | solution.py:14
  200.7 8.3 %collective-permute-start.9 = (f32[17,33,128]{2,1,0:T(8,128)S(1)}, f32[17,33,128]{2,1,0:T(8,128)S(1)}, u32[]{:S(2)}, u32[]{:S(2)}) collective-permute-start(f32[17,33,128]{2,1,0:T(8,128)S(1)} %broadcast_select_fusion.1), channel_id=1, source_target_pairs={{0,8},{8,16},{16,24},{24,32},{32,40},{40,48},{48,56},{56,64},{64,7... | collective-permute-start | bytes 861704 | tf_op jit(solution)/shard_map/ppermute | solution.py:14
  207.3 1.7 copy-start.22
  207.3 2.9 %copy-start.24 = (f32[33,33,1]{1,0,2:T(8,128)S(1)}, f32[33,33,1]{1,0,2:T(8,128)}, u32[]{:S(2)}) copy-start(f32[33,33,1]{1,0,2:T(8,128)} %constant.71) | copy-start | bytes 13072
Sparse Core Ops, SparseCore 0:
  100.7 90.6 all-reduce.1
where the time goes:
time: 219 us; the launch traced here: 218 us
  waiting for transfers between devices  97.1 us (44%)
  starting transfers between devices  47.5 us (22%)
  matrix products  24.5 us (11%)
  local copies, waits for them, and re-layouts  23.8 us (11%)
  between operations  15.5 us (7%)
  other arithmetic  10 us (5%)
    psum x1, waiting for transfers between devices, local(): smoothed = smooth_x(lax.psum(kernel_local, 'event'), flip_flag, table_x)  90.8 us
    ppermute x11, starting transfers between devices, from_behind(): lax.ppermute(shard, axis, [(i, (i + by) % peers) for i in range(peers)])  47.5 us
    unnamed x76, local copies, waits for them, and re-layouts  9.98 us
    rev x11, local copies, waits for them, and re-layouts, reorient(): return jnp.where(flip_flag != 0, jnp.flip(planes, -2), planes)  9.52 us
    ppermute x11, waiting for transfers between devices, from_behind(): lax.ppermute(shard, axis, [(i, (i + by) % peers) for i in range(peers)])  6.25 us
    dot_general x4, matrix products, stiffness(): jnp.einsum('ny,...nx->...yx', table_y[0], coefficients[1] * grad_y, preci...  5.01 us
    select_n x11, other arithmetic, reorient(): return jnp.where(flip_flag != 0, jnp.flip(planes, -2), planes)  4.99 us
  transfers between devices with their start and end apart: 12, of which 4 were waited for; matrix products, arithmetic and copies ran while one was open for 23% of the time, Pallas kernels for 0%

commit v1 on v0

v1 whole, which is shorter than its diff:
```python
import functools

import jax
import jax.numpy as jnp
import numpy as np
from jax import lax
from jax.experimental import pallas as pl
from jax.experimental.pallas import tpu as pltpu
from jax.sharding import PartitionSpec as P

DT2 = 0.003
SIGMA_Y = 1.0
ZP, YP, XL = 17, 33, 128
YPAD = 40
ROWS = ZP * YPAD
HALF = 9
KROWS = 576
VMEM = 48 * 1024 * 1024


def gll_tables():
    nodes = np.array([-1.0, -np.sqrt(3.0 / 7.0), 0.0, np.sqrt(3.0 / 7.0), 1.0])
    weights = np.array([0.1, 49.0 / 90.0, 32.0 / 45.0, 49.0 / 90.0, 0.1])
    deriv = np.zeros((5, 5))
    for a in range(5):
        for b in range(5):
            for m in range(5):
                if m == b:
                    continue
                factor = 1.0 / (nodes[b] - nodes[m])
                for k in range(5):
                    if k == b or k == m:
                        continue
                    factor = factor * (nodes[a] - nodes[k]) / (nodes[b] - nodes[k])
                deriv[a, b] += factor
    return weights, deriv


GW, GD = gll_tables()
SHARED = np.array([0.2, GW[1], GW[2], GW[3], 0.2])
APPLY = GW[:, None] * GD
GATHER = (GD / SHARED[None, :]).T


def split(m):
    hi = np.asarray(m, np.float32).astype(jnp.bfloat16)
    lo = (np.asarray(m, np.float32) - hi.astype(np.float32)).astype(jnp.bfloat16)
    return jnp.asarray(hi), jnp.asarray(lo)


LANE_A, LANE_B, LANE_K, LANE_PA, LANE_CA, LANE_PB, LANE_CB = 0, 13, 26, 39, 44, 52, 57


def x_tables():
    def column(c):
        if 0 <= c < XL:
            return c
        return XL + (c + 8 if c < 0 else 8 + c - XL)

    def node(e, a):
        if 0 <= e < 32:
            return 4 * e + a if a < 4 else XL + e
        return XL + {-1: 32, -2: 37, 32: 42}[e] + a

    grad = np.zeros((2 * XL, 2 * XL))
    back = np.zeros((2 * XL, 2 * XL))
    pick = np.zeros((2 * XL, XL))
    for e in range(-2, 33):
        for a in range(5):
            n = node(e, a)
            for b in range(5):
                c = 4 * e + b
                grad[column(c), n] += APPLY[a, b]
                if -4 <= c <= XL:
                    back[n, column(c)] += GATHER[b, a]
            if n >= XL:
                k = column(4 * e + a)
                pick[k if k < XL else k + LANE_K, n - XL] = 1.0
    return split(grad), split(back), jnp.asarray(pick, jnp.bfloat16)


def smoothing_tables():
    offsets = np.arange(3 * XL)[:, None] - XL - np.arange(XL)[None, :]
    sigma_x = XL / 2.0
    gauss_x = np.exp(-0.5 * (offsets / sigma_x) ** 2) * (np.abs(offsets) <= XL)
    normal_x = np.exp(-0.5 * (np.arange(-XL, XL + 1) / sigma_x) ** 2).sum()
    distance = np.arange(YP)[:, None] - np.arange(YP)[None, :]
    gauss_y = np.exp(-0.5 * (distance / SIGMA_Y) ** 2)
    gauss_y = gauss_y / gauss_y.sum(axis=1, keepdims=True)
    undo = np.zeros((YP, YP))
    for y in range(YP):
        if y == 16:
            undo[y, y] = 1.0
        else:
            undo[y, 32 - y] = 0.5
            undo[y, y] = 0.5 if y < 16 else -0.5
    return gauss_x / normal_x, gauss_y @ undo


def apply5(m, x):
    e0, o0, e1, o1, mid = x[0] + x[4], x[0] - x[4], x[1] + x[3], x[1] - x[3], x[2]
    f = lambda v: np.float32(v)
    odd = [
        f((m[a, 0] + m[a, 4]) / 2) * e0 + f((m[a, 1] + m[a, 3]) / 2) * e1 + f(m[a, 2]) * mid
        for a in (0, 1)
    ]
    even = [
        f((m[a, 0] - m[a, 4]) / 2) * o0 + f((m[a, 1] - m[a, 3]) / 2) * o1 for a in (0, 1, 2)
    ]
    return [even[0] + odd[0], even[1] + odd[1], even[2], even[1] - odd[1], even[0] - odd[0]]


def apply_y(fields, kappa):
    row = lax.broadcasted_iota(jnp.int32, (8, XL), 0)

    def plane(z, carry):
        at = lambda a: pl.ds(a, 8, stride=4)
        k = [kappa[z, at(a), :] for a in range(5)]
        for v, out in fields:
            g = apply5(APPLY, [v[z, at(a), :] for a in range(5)])
            o = apply5(GATHER, [k[a] * g[a] for a in range(5)])
            moved = pltpu.roll(o[4], 1, 0)
            out[z, at(0), :] = jnp.where(row == 0, 2.0 * o[0], o[0] + moved)
            for b in range(1, 4):
                out[z, at(b), :] = o[b]
            out[z, 32:33, :] = 2.0 * moved[0:1]
        return carry

    lax.fori_loop(0, ZP, plane, 0)


def apply_z(fields, kappa, use):
    def block(rows):
        for i, v in enumerate(fields):
            ends = None
            for e in range(4):
                g = apply5(APPLY, [v[4 * e + a, rows, :] for a in range(5)])
                o = apply5(GATHER, [kappa[4 * e + a, rows, :] * g[a] for a in range(5)])
                use(i, 4 * e, rows, 2.0 * o[0] if e == 0 else o[0] + ends)
                for b in range(1, 4):
                    use(i, 4 * e + b, rows, o[b])
                ends = o[4]
            use(i, 16, rows, 2.0 * ends)

    def step(j, carry):
        block(pl.ds(pl.multiple_of(8 * j, 8), 8))
        return carry

    lax.fori_loop(0, 4, step, 0)
    block(pl.ds(32, 1))


def add_forcing(target, c_ref, index, source, instant, iz, iy):
    lane = lax.broadcasted_iota(jnp.int32, (1, XL), 1)
    node = lane % 4
    inv_x = jnp.where(
        node == 0, 1.0 / SHARED[0], jnp.where(node == 2, 1.0 / SHARED[2], 1.0 / SHARED[1])
    ).astype(jnp.float32)

    def one(r, carry):
        point = index[r]
        z = point // (YP * XL)
        rest = point - z * (YP * XL)
        y = rest // XL
        x = rest - y * XL
        amount = source[instant, r] * iz[z] * iy[y]
        at = (pl.ds(z, 1), pl.ds(y, 1), slice(None))
        change = jnp.where(lane == x, inv_x * amount, 0.0)
        target[at] = target[at] + c_ref[at] * change[None]
        return carry

    lax.fori_loop(0, 16, one, 0)


def flip_rows(source, target, flag):
    for y in range(YP):
        to = jnp.where(flag != 0, 32 - y, y)
        target[:, pl.ds(to, 1), :] = source[:, y : y + 1, :]


def pack_kernel(
    flip, index, source, iz, iy, an, ap, bn, bp, ka, de, c_out, f_out, right_out, left_out, pack
):
    lane = lax.broadcasted_iota(jnp.int32, (YP, XL), 1)
    f_out[...] = jnp.zeros_like(f_out)
    for z in range(ZP):
        c_out[z, 0:YP, :] = DT2 / de[z]
    add_forcing(f_out, c_out, index, source, 0, iz, iy)
    for z in range(ZP):
        group = 0 if z < HALF else 64
        a, b, k, c = an[0, z], bn[0, z], ka[z], c_out[z, 0:YP, :]
        pa = 2.0 * a - ap[0, z] + f_out[z, 0:YP, :]
        pb = 2.0 * b - bp[0, z]
        tile = None
        parts = [
            (a, 120, LANE_A), (b, 120, LANE_B), (k, 120, LANE_K), (pa, 124, LANE_PA),
            (c, 124, LANE_CA), (pb, 124, LANE_PB), (c, 124, LANE_CB),
        ]
        for value, first, to in reversed(parts):
            moved = pltpu.roll(value, (group + to - first) % XL, 1)
            if tile is None:
                tile = moved
            else:
                above = group + parts[[p[2] for p in parts].index(to) + 1][2]
                tile = jnp.where(lane < above, moved, tile)
        if group:
            pack[z - HALF, :, :] = jnp.where(lane < 64, pack[z - HALF, :, :], tile)
        else:
            pack[z, :, :] = tile
    left_out[...] = pack[...]
    flip_rows(pack, right_out, flip[0])


def local_kernel(index, source, iz, iy, an, bn, ka, c, f, a_out, b_out, f1_out):
    a, b = an.at[0], bn.at[0]
    apply_y(((a, a_out), (b, b_out)), ka)

    def use(i, z, rows, value):
        out = (a_out, b_out)[i]
        total = c[z, rows, :] * (out[z, rows, :] + value)
        out[z, rows, :] = f[z, rows, :] - total if i == 0 else -total

    apply_z((a, b), ka, use)
    f1_out[...] = jnp.zeros_like(f1_out)
    add_forcing(f1_out, c, index, source, 1, iz, iy)


def halves(x):
    hi = x.astype(jnp.bfloat16)
    return hi, (x - hi.astype(jnp.float32)).astype(jnp.bfloat16)


def dot(a, b):
    return jnp.dot(a, b, preferred_element_type=jnp.float32)


def dot3(x, m_hi, m_lo):
    hi, lo = halves(x)
    return dot(hi, m_hi) + dot(lo, m_hi) + dot(hi, m_lo)


def step_kernel(
    flip, an, ap, bn, bp, ka, c, a0, b0, f1, right_in, left_in,
    g_hi, g_lo, t_hi, t_lo, pick,
    af_out, al_out, bf_out, bl_out, k_out,
    left, u, ku, cu, qu, va, vb, kg, wa, wb, y1, y2,
):
    lane = lax.broadcasted_iota(jnp.int32, (YP, XL), 1)
    flip_rows(left_in, left, flip[0])
    before = None
    for first, n in (
        (LANE_A, 8), (LANE_B, 8), (LANE_K, 8), (LANE_PA, 4), (LANE_CA, 4), (LANE_PB, 4), (LANE_CB, 4)
    ):
        one = ((lane % 64) >= first) & ((lane % 64) < first + n)
        before = one if before is None else before | one
    for z in range(ZP):
        i = z % HALF
        tile = jnp.where(before, right_in[i], left[i])
        if z >= HALF:
            tile = pltpu.roll(tile, 64, 1)
        u[z, 0:YP, :] = tile
        ku[z, 0:YP, :] = jnp.where(
            lane < LANE_B,
            pltpu.roll(tile, XL - LANE_K, 1),
            pltpu.roll(tile, XL - LANE_K + LANE_B, 1),
        )
        qu[z, 0:YP, :] = pltpu.roll(tile, XL - LANE_PA + 4, 1)
        cu[z, 0:YP, :] = pltpu.roll(tile, XL - LANE_CA + 4, 1)
        va[z, 0:YP, :] = an[0, z]
        vb[z, 0:YP, :] = bn[0, z]
        kg[z, 0:YP, 0:XL] = ka[z]
    apply_y(((u, y1),), ku)

    def use(i, z, rows, value):
        qu[z, rows, :] = qu[z, rows, :] - cu[z, rows, :] * (y1[z, rows, :] + value)

    apply_z((u,), ku, use)

    flat = lambda ref: ref[...].reshape(ROWS, ref.shape[-1])
    tall = lambda value: value.reshape(ZP, YPAD, value.shape[-1])
    uf = flat(u)
    chosen = jnp.concatenate([kg[:, :, 0:XL].reshape(ROWS, XL), uf], 1)
    hi, lo = halves(chosen)
    kg[:, :, XL:] = tall(dot(hi, pick[...]) + dot(lo, pick[...]))

    def along_x(v, halo, wide):
        flux = dot3(jnp.concatenate([v, halo], 1), g_hi[...], g_lo[...]) * flat(kg)
        n = 2 * XL if wide else XL
        return dot3(flux, t_hi[:, 0:n], t_lo[:, 0:n])

    xa = along_x(flat(va), uf, True)
    xb = along_x(flat(vb), pltpu.roll(uf, XL - LANE_B, 1), True)
    lane2 = lax.broadcasted_iota(jnp.int32, (ROWS, XL), 1)
    halo = jnp.where(lane2 < LANE_B, xa[:, XL:], pltpu.roll(xb[:, XL:], LANE_B, 1))
    u1 = flat(qu) - flat(cu) * halo
    wa[...] = tall(xa[:, 0:XL])
    wb[...] = tall(xb[:, 0:XL])
    for z in range(ZP):
        cz = c[z, 0:YP, :]
        acc_a = a0[z, 0:YP, :] - cz * wa[z, 0:YP, :]
        acc_b = b0[z, 0:YP, :] - cz * wb[z, 0:YP, :]
        a, b = an[0, z], bn[0, z]
        v1a = 2.0 * a - ap[0, z] + acc_a
        v1b = 2.0 * b - bp[0, z] + acc_b
        al_out[0, z] = v1a
        bl_out[0, z] = v1b
        va[z, 0:YP, :] = v1a
        vb[z, 0:YP, :] = v1b
        ku[z, 0:YP, :] = b * acc_a
    apply_y(((va, y1), (vb, y2)), ka)

    def add(i, z, rows, value):
        out = (y1, y2)[i]
        out[z, rows, :] = out[z, rows, :] + value

    apply_z((va, vb), ka, add)
    xa = along_x(flat(va), u1, False)
    xb = along_x(flat(vb), pltpu.roll(u1, XL - LANE_B, 1), False)
    wa[...] = tall(xa)
    wb[...] = tall(xb)
    for z in range(ZP):
        cz = c[z, 0:YP, :]
        acc_a = f1[z, 0:YP, :] - cz * (wa[z, 0:YP, :] + y1[z, 0:YP, :])
        acc_b = -cz * (wb[z, 0:YP, :] + y2[z, 0:YP, :])
        v1a, v1b = va[z, 0:YP, :], vb[z, 0:YP, :]
        af_out[0, z] = 2.0 * v1a - an[0, z] + acc_a
        bf_out[0, z] = 2.0 * v1b - bn[0, z] + acc_b
        ku[z, 0:YP, :] = ku[z, 0:YP, :] + v1b * acc_a
    for y in range(YP):
        u[:, 32 - y : 33 - y, :] = ku[:, y : y + 1, :]
    row = lax.broadcasted_iota(jnp.int32, (YP, XL), 0)
    sign = jnp.where(row < 16, 1.0, jnp.where(row == 16, 0.0, -1.0)).astype(jnp.float32)
    k_out[ZP * 32 :, :] = jnp.zeros((KROWS - ZP * 32, XL), jnp.float32)
    for z in range(ZP):
        t = u[z, 0:YP, :] + sign * ku[z, 0:YP, :]
        k_out[32 * z : 32 * z + 32, :] = t[0:32]
        k_out[ZP * 32 + z : ZP * 32 + z + 1, :] = t[32:33]


def smooth_kernel(copies, before, own, after, gx_hi, gx_lo, out):
    total = None
    for i, part in enumerate((before, own, after)):
        at = slice(XL * i, XL * (i + 1))
        one = dot3(part[...], gx_hi[at, :], gx_lo[at, :])
        total = one if total is None else total + one
    for i in range(copies):
        out[i] = total


def finish_kernel(t, blocks_hi, blocks_lo, last, out):
    def planes(first, n):
        rows = t[32 * first : 32 * (first + n), :]
        hi, lo = halves(rows)
        m_hi, m_lo = blocks_hi[0 : n * YPAD, 0 : n * 32], blocks_lo[0 : n * YPAD, 0 : n * 32]
        done = dot(m_hi, hi) + dot(m_hi, lo) + dot(m_lo, hi)
        for i in range(n):
            z = first + i
            extra = last[...] * t[ZP * 32 + z : ZP * 32 + z + 1, :]
            out[z] = done[i * YPAD : i * YPAD + YP] + extra[0:YP]

    planes(0, 8)
    planes(8, 8)
    planes(16, 1)


SMEM_SPEC = pl.BlockSpec(memory_space=pltpu.SMEM)
VMEM_SPEC = pl.BlockSpec(memory_space=pltpu.VMEM)


def call(kernel, outs, scalars, arrays, scratch=(), flops=0, moved=0):
    return pl.pallas_call(
        kernel,
        out_shape=[jax.ShapeDtypeStruct(s, jnp.float32) for s in outs],
        in_specs=[SMEM_SPEC] * len(scalars) + [VMEM_SPEC] * len(arrays),
        out_specs=[VMEM_SPEC] * len(outs),
        scratch_shapes=[pltpu.VMEM(s, jnp.float32) for s in scratch],
        compiler_params=pltpu.CompilerParams(vmem_limit_bytes=VMEM),
        cost_estimate=pl.CostEstimate(flops=flops, bytes_accessed=moved, transcendentals=0),
    )(*scalars, *arrays)


def shift(value, axis, by):
    n = lax.axis_size(axis)
    return lax.ppermute(value, axis, [(i, (i + by) % n) for i in range(n)])


def local(an, ap, bn, bp, kappa, density, flip, index, source):
    field, padded, edge = (1, ZP, YP, XL), (ZP, YPAD, XL), (HALF, YP, XL)
    inv_z, inv_y = (np.tile(1.0 / SHARED[:4], n) for n in (4, 8))
    inv_z, inv_y = (np.append(v, v[0] * 2) for v in (inv_z, inv_y))
    inv_z[0] *= 2
    inv_y[0] *= 2
    iz, iy = jnp.asarray(inv_z, jnp.float32), jnp.asarray(inv_y, jnp.float32)
    src = source[0]
    c, f0, to_right, to_left = call(
        pack_kernel,
        [padded, padded, edge, edge],
        [flip, index, src, iz, iy],
        [an, ap, bn, bp, kappa, density],
        [edge],
        moved=3_000_000,
    )
    from_left = shift(to_right, "cuts", 1)
    from_right = shift(to_left, "cuts", -1)
    a0, b0, f1 = call(
        local_kernel,
        [padded, padded, padded],
        [index, src, iz, iy],
        [an, bn, kappa, c, f0],
        flops=20_000_000,
        moved=3_000_000,
    )
    (g_hi, g_lo), (t_hi, t_lo), pick = x_tables()
    wide = (ZP, YPAD, 2 * XL)
    af, al, bf, bl, k = call(
        step_kernel,
        [field, field, field, field, (KROWS, XL)],
        [flip],
        [an, ap, bn, bp, kappa, c, a0, b0, f1, from_left, from_right, g_hi, g_lo, t_hi, t_lo, pick],
        [edge, padded, padded, padded, padded, padded, padded, wide, padded, padded, padded, padded],
        flops=600_000_000,
        moved=6_000_000,
    )
    groups = lax.axis_size("event")
    part = KROWS // groups
    parts = lax.all_to_all(k.reshape(groups, part, XL), "event", 0, 0)
    total = jnp.sum(parts, axis=0)
    row = lax.axis_index("event") * part + jnp.arange(part)
    odd = jnp.where(row < ZP * 32, row % 32 > 16, True)
    sign = jnp.where(odd & (flip[0] != 0), -1.0, 1.0).astype(jnp.float32)[:, None]
    before = shift(total * sign, "cuts", 1)
    after = shift(total, "cuts", -1) * sign
    gauss_x, final_y = smoothing_tables()
    spread = call(
        functools.partial(smooth_kernel, groups),
        [(groups, part, XL)],
        [],
        [before, total, after, *split(gauss_x)],
    )[0]
    whole = lax.all_to_all(spread, "event", 0, 0).reshape(KROWS, XL)
    blocks = np.zeros((8 * YPAD, 256))
    for i in range(8):
        blocks[i * YPAD : i * YPAD + YP, i * 32 : i * 32 + 32] = final_y[:, 0:32]
    last = np.zeros((YPAD, XL))
    last[0:YP] = final_y[:, 32:33]
    smoothed = call(
        finish_kernel, [(ZP, YP, XL)], [], [whole, *split(blocks), jnp.asarray(last, jnp.float32)]
    )[0]
    return af, al, bf, bl, smoothed


def solution(mesh):
    field = P("event", None, None, "cuts")
    grid = P(None, None, "cuts")
    return jax.shard_map(
        local,
        mesh=mesh,
        in_specs=(field,) * 4 + (grid, grid, P("cuts"), P("cuts"), P("event", None, "cuts")),
        out_specs=(field,) * 4 + (grid,),
        check_vma=False,
    )
```

time: 219 us -> 73 us (0.33)
  the two profiles are of different devices: /device:TPU:1 before, /device:TPU:8 now
where the time goes in v1:
time: 73 us; the launch traced here: 72.5 us
  starting transfers between devices  32.5 us (45%)
  waiting for transfers between devices  18.5 us (25%)
  Pallas kernels  12.5 us (17%)
  local copies, waits for them, and re-layouts  7.34 us (10%)
  between operations  1.52 us (2%)
    ppermute x4, starting transfers between devices, shift(): return lax.ppermute(value, axis, [(i, (i + by) % n) for i in range(n)])  20.3 us
    pallas_call x5, Pallas kernels, call(): pl.pallas_call(kernel, out_shape=[jax.ShapeDtypeStruct(s, jnp.float32) fo...  12.5 us
    ppermute x4, waiting for transfers between devices, shift(): return lax.ppermute(value, axis, [(i, (i + by) % n) for i in range(n)])  8.1 us
    unnamed x46, local copies, waits for them, and re-layouts  7.34 us
    all_to_all x1, waiting for transfers between devices, local(): parts = lax.all_to_all(k.reshape(groups, part, XL), 'event', 0, 0)  7.19 us
    all_to_all x1, starting transfers between devices, local(): parts = lax.all_to_all(k.reshape(groups, part, XL), 'event', 0, 0)  7.09 us
    all_to_all x1, starting transfers between devices, local(): whole = lax.all_to_all(spread, 'event', 0, 0).reshape(KROWS, XL)  5.19 us
    all_to_all x1, waiting for transfers between devices, local(): whole = lax.all_to_all(spread, 'event', 0, 0).reshape(KROWS, XL)  3.16 us
  transfers between devices with their start and end apart: 6, of which 5 were waited for; matrix products, arithmetic and copies ran while one was open for 6% of the time, Pallas kernels for 3%

profile of v1, /device:TPU:8, one launch (start us, length us, event | category | flops | bytes accessed | tf_op | source)
XLA Modules:
  0.0 72.5 jit_solution(13174192604843215622)
XLA Ops:
  0.6 0.0 copy-start.16
  0.6 1.0 %copy.32.an = f32[1,17,33,128]{3,2,1,0:T(8,128)S(1)} copy(f32[1,17,33,128]{3,0,2,1:T(1,128)} %param.21) | data formatting | bytes 574464 | tf_op args[0]
  1.7 0.0 copy-done.16
  1.7 0.0 copy-start.17
  2.4 0.2 copy-done.17
  2.7 0.0 copy-start.18
  2.7 0.0 copy-start.1
  2.7 0.9 %copy-done.18 = f32[1,17,33,128]{3,0,2,1:T(1,128)S(1)} copy-done((f32[1,17,33,128]{3,0,2,1:T(1,128)S(1)}, f32[1,17,33,128]{3,0,2,1:T(1,128)}, u32[]{:S(2)}) %copy-start.18) | copy-done | bytes 287256
  3.6 0.0 copy-start
  3.6 0.0 copy-start.14
  3.6 0.0 copy-start.15
  3.7 0.0 copy-start.12
  3.7 0.0 copy-start.13
  3.7 0.1 copy-done.1
  3.7 0.9 %copy-done = f32[17,33,128]{2,1,0:T(8,128)S(1)} copy-done((f32[17,33,128]{2,1,0:T(8,128)S(1)}, f32[17,33,128]{2,1,0:T(8,128)}, u32[]{:S(2)}) %copy-start) | copy-done | bytes 287256
  4.6 0.0 copy-done.14
  4.6 0.0 copy-done.15
  4.6 0.0 copy-done.12
  4.6 0.0 copy-done.13
  4.6 1.9 %shard_map.236 = (f32[17,40,128]{2,1,0:T(8,128)S(1)}, f32[17,40,128]{2,1,0:T(8,128)S(1)}, f32[9,33,128]{2,1,0:T(8,128)S(1)}, f32[9,33,128]{2,1,0:T(8,128)S(1)}) custom-call(s32[1]{0:T(128)S(6)} %copy.40.flip, s32[16]{0:T(128)S(1)} %copy-done.13, f32[2,16]{1,0:T(2,128)S(1)} %bitcast.5, f32[17]{0:T(128)S(1)} %copy-done.14, f32[33]{0:T(128)S(1)} %copy-done.15, ...), custom_call_target="tpu_custom_call" | custom-call | bytes 3000000 | tf_op jit(solution)/shard_map/pallas_call | solution.py:371
  6.5 1.9 %collective-permute-start = (f32[9,33,128]{2,1,0:T(8,128)S(1)}, f32[9,33,128]{2,1,0:T(8,128)S(1)}, u32[]{:S(2)}, u32[]{:S(2)}) collective-permute-start(f32[9,33,128]{2,1,0:T(8,128)S(1)} %get-tuple-element.22), channel_id=1, source_target_pairs={{0,8},{8,16},{16,24},{24,32},{32,40},{40,48},{48,56},{56,64},{64,7... | collective-permute-start | bytes 456200 | tf_op jit(solution)/shard_map/ppermute | solution.py:384
  8.5 11.8 %collective-permute-start.1 = (f32[9,33,128]{2,1,0:T(8,128)S(1)}, f32[9,33,128]{2,1,0:T(8,128)S(1)}, u32[]{:S(2)}, u32[]{:S(2)}) collective-permute-start(f32[9,33,128]{2,1,0:T(8,128)S(1)} %get-tuple-element.23), channel_id=1, source_target_pairs={{0,504},{8,0},{16,8},{24,16},{32,24},{40,32},{48,40},{56,48},{64,5... | collective-permute-start | bytes 456200 | tf_op jit(solution)/shard_map/ppermute | solution.py:384
  20.2 0.0 copy-start.4
  20.2 0.0 copy-start.5
  20.3 0.0 copy-start.6
  20.3 0.0 copy-start.7
  20.3 0.0 copy-start.10
  20.3 1.9 %shard_map.237 = (f32[17,40,128]{2,1,0:T(8,128)S(1)}, f32[17,40,128]{2,1,0:T(8,128)S(1)}, f32[17,40,128]{2,1,0:T(8,128)S(1)}) custom-call(s32[16]{0:T(128)S(1)} %copy-done.13, f32[2,16]{1,0:T(2,128)S(1)} %bitcast.6, f32[17]{0:T(128)S(1)} %copy-done.14, f32[33]{0:T(128)S(1)} %copy-done.15, f32[1,17,33,128]{3,2,1,0:T(8,128)S(1)} %copy.32.an, ...), custom_call_target="tpu_custom_call" | custom-call | flops 20000000 | bytes 3000000 | tf_op jit(solution)/shard_map/pallas_call | solution.py:371
  22.2 0.0 collective-permute-done.right_in
  22.2 1.0 %collective-permute-done.1.left_in = f32[9,33,128]{2,1,0:T(8,128)S(1)} collective-permute-done((f32[9,33,128]{2,1,0:T(8,128)S(1)}, f32[9,33,128]{2,1,0:T(8,128)S(1)}, u32[]{:S(2)}, u32[]{:S(2)}) %collective-permute-start.1) | collective-permute-done | bytes 152096 | tf_op jit(solution)/shard_map/ppermute | solution.py:384
  23.3 0.0 copy-done.4
  23.3 0.0 copy-done.5
  23.3 0.0 copy-done.6
  23.3 0.0 copy-done.7
  23.3 0.0 copy-done.10
  23.3 6.6 %shard_map.238 = (f32[1,17,33,128]{3,2,1,0:T(8,128)S(1)}, f32[1,17,33,128]{3,2,1,0:T(8,128)S(1)}, f32[1,17,33,128]{3,2,1,0:T(8,128)S(1)}, f32[1,17,33,128]{3,2,1,0:T(8,128)S(1)}, f32[576,128]{1,0:T(8,128)}) custom-call(s32[1]{0:T(128)S(6)} %copy.40.flip, f32[1,17,33,128]{3,2,1,0:T(8,128)S(1)} %copy.32.an, f32[1,17,33,128]{3,2,1,0:T(8,128)S(1)} %copy.33.ap, ...), custom_call_target="tpu_custom_call" | custom-call | flops 600000000 | bytes 6000000 | tf_op jit(solution)/shard_map/pallas_call | solution.py:371
  29.9 7.1 %all-to-all-start = ((f32[8,72,128]{2,1,0:T(8,128)}), f32[8,72,128]{2,1,0:T(8,128)S(1)}, u32[]{:S(2)}, u32[]{:S(2)}) async-start(f32[8,72,128]{2,1,0:T(8,128)} %bitcast.1), calls=%async_computation | async-start | bytes 589824 | tf_op jit(solution)/shard_map/all_to_all | solution.py:426
  37.0 7.2 %all-to-all-done = f32[8,72,128]{2,1,0:T(8,128)S(1)} async-done(((f32[8,72,128]{2,1,0:T(8,128)}), f32[8,72,128]{2,1,0:T(8,128)S(1)}, u32[]{:S(2)}, u32[]{:S(2)}) %all-to-all-start) | async-done | bytes 294944 | tf_op jit(solution)/shard_map/all_to_all | solution.py:426
  44.1 0.0 copy-start.9
  44.2 0.0 copy-start.8
  44.2 4.7 %collective-permute-start.3 = (f32[72,128]{1,0:T(8,128)S(1)}, f32[72,128]{1,0:T(8,128)S(1)}, u32[]{:S(2)}, u32[]{:S(2)}) collective-permute-start(f32[72,128]{1,0:T(8,128)S(1)} %reduce_sum.9.own), channel_id=1, source_target_pairs={{0,504},{8,0},{16,8},{24,16},{32,24},{40,32},{48,40},{56,48},{64,5... | collective-permute-start | bytes 110600 | tf_op jit(solution)/shard_map/ppermute | solution.py:384
  48.9 1.6 %collective-permute-done.3 = f32[72,128]{1,0:T(8,128)S(1)} collective-permute-done((f32[72,128]{1,0:T(8,128)S(1)}, f32[72,128]{1,0:T(8,128)S(1)}, u32[]{:S(2)}, u32[]{:S(2)}) %collective-permute-start.3) | collective-permute-done | bytes 36896 | tf_op jit(solution)/shard_map/ppermute | solution.py:384
  50.5 0.1 broadcast_multiply_fusion
  50.6 1.9 %collective-permute-start.2 = (f32[72,128]{1,0:T(8,128)S(1)}, f32[72,128]{1,0:T(8,128)S(1)}, u32[]{:S(2)}, u32[]{:S(2)}) collective-permute-start(f32[72,128]{1,0:T(8,128)S(1)} %get-tuple-element.35), channel_id=1, source_target_pairs={{0,8},{8,16},{16,24},{24,32},{32,40},{40,48},{48,56},{56,64},{64,7... | collective-permute-start | bytes 110600 | tf_op jit(solution)/shard_map/ppermute | solution.py:384
  52.5 5.5 %collective-permute-done.2.before = f32[72,128]{1,0:T(8,128)S(1)} collective-permute-done((f32[72,128]{1,0:T(8,128)S(1)}, f32[72,128]{1,0:T(8,128)S(1)}, u32[]{:S(2)}, u32[]{:S(2)}) %collective-permute-start.2) | collective-permute-done | bytes 36896 | tf_op jit(solution)/shard_map/ppermute | solution.py:384
  57.9 0.0 copy-done.9
  57.9 0.0 copy-done.8
  57.9 1.0 %shard_map.239 = f32[8,72,128]{2,1,0:T(8,128)} custom-call(f32[72,128]{1,0:T(8,128)S(1)} %collective-permute-done.2.before, f32[72,128]{1,0:T(8,128)S(1)} %reduce_sum.9.own, f32[72,128]{1,0:T(8,128)S(1)} %get-tuple-element.34.after, bf16[384,128]{1,0:T(8,128)(2,1)S(1)} %copy-done.8, bf16[384,128]{1,0:T(8,128)(2,1)S(1)} %copy-done.9), custom_call_target="tpu_custom_call" | custom-call | tf_op jit(solution)/shard_map/pallas_call | solution.py:371
  58.9 5.2 %all-to-all-start.1 = ((f32[8,72,128]{2,1,0:T(8,128)}), f32[8,72,128]{2,1,0:T(8,128)S(1)}, u32[]{:S(2)}, u32[]{:S(2)}) async-start(f32[8,72,128]{2,1,0:T(8,128)} %shard_map.239), calls=%async_computation.1 | async-start | bytes 589824 | tf_op jit(solution)/shard_map/all_to_all | solution.py:440
  64.1 1.0 %copy.36 = f32[1,17,33,128]{3,0,2,1:T(1,128)} copy(f32[1,17,33,128]{3,2,1,0:T(8,128)S(1)} %get-tuple-element.29) | data formatting | bytes 574464
  65.1 1.0 %copy.37 = f32[1,17,33,128]{3,0,2,1:T(1,128)} copy(f32[1,17,33,128]{3,2,1,0:T(8,128)S(1)} %get-tuple-element.30) | data formatting | bytes 574464
  66.1 1.0 %copy.38 = f32[1,17,33,128]{3,0,2,1:T(1,128)} copy(f32[1,17,33,128]{3,2,1,0:T(8,128)S(1)} %get-tuple-element.31) | data formatting | bytes 574464
  67.1 0.0 copy-start.2
  67.1 0.0 copy-start.3
  67.1 0.0 copy-start.11
  67.1 1.0 %copy.39 = f32[1,17,33,128]{3,0,2,1:T(1,128)} copy(f32[1,17,33,128]{3,2,1,0:T(8,128)S(1)} %get-tuple-element.32) | data formatting | bytes 574464
  68.1 3.2 %all-to-all-done.1 = f32[8,72,128]{2,1,0:T(8,128)S(1)} async-done(((f32[8,72,128]{2,1,0:T(8,128)}), f32[8,72,128]{2,1,0:T(8,128)S(1)}, u32[]{:S(2)}, u32[]{:S(2)}) %all-to-all-start.1) | async-done | bytes 294944 | tf_op jit(solution)/shard_map/all_to_all | solution.py:440
  71.3 0.0 copy-done.2
  71.3 0.0 copy-done.3
  71.3 0.0 copy-done.11
  71.3 1.2 %shard_map.240 = f32[17,33,128]{2,1,0:T(8,128)} custom-call(f32[576,128]{1,0:T(8,128)S(1)} %bitcast.4, bf16[320,256]{1,0:T(8,128)(2,1)S(1)} %copy-done.2, bf16[320,256]{1,0:T(8,128)(2,1)S(1)} %copy-done.3, f32[40,128]{1,0:T(8,128)S(1)} %copy-done.11), custom_call_target="tpu_custom_call" | custom-call | tf_op jit(solution)/shard_map/pallas_call | solution.py:371
  (5 shorter events, 0.1 us)
Async XLA Ops:
  0.6 1.0 %copy-start.16 = (f32[1,17,33,128]{3,0,2,1:T(1,128)S(1)}, f32[1,17,33,128]{3,0,2,1:T(1,128)}, u32[]{:S(2)}) copy-start(f32[1,17,33,128]{3,0,2,1:T(1,128)} %param.23) | copy-start | bytes 861700
  1.7 1.0 %copy-start.17 = (f32[1,17,33,128]{3,0,2,1:T(1,128)S(1)}, f32[1,17,33,128]{3,0,2,1:T(1,128)}, u32[]{:S(2)}) copy-start(f32[1,17,33,128]{3,0,2,1:T(1,128)} %param.22) | copy-start | bytes 861700
  2.7 1.0 %copy-start.18 = (f32[1,17,33,128]{3,0,2,1:T(1,128)S(1)}, f32[1,17,33,128]{3,0,2,1:T(1,128)}, u32[]{:S(2)}) copy-start(f32[1,17,33,128]{3,0,2,1:T(1,128)} %param.24) | copy-start | bytes 861700
  2.7 1.1 %copy-start.1 = (f32[17,33,128]{2,1,0:T(8,128)S(1)}, f32[17,33,128]{2,1,0:T(8,128)}, u32[]{:S(2)}) copy-start(f32[17,33,128]{2,1,0:T(8,128)} %de.1) | copy-start | bytes 861700
  3.6 1.0 %copy-start = (f32[17,33,128]{2,1,0:T(8,128)S(1)}, f32[17,33,128]{2,1,0:T(8,128)}, u32[]{:S(2)}) copy-start(f32[17,33,128]{2,1,0:T(8,128)} %ka.5) | copy-start | bytes 861700
  3.6 1.0 %copy-start.14 = (f32[17]{0:T(128)S(1)}, f32[17]{0:T(128)}, u32[]{:S(2)}) copy-start(f32[17]{0:T(128)} %constant.60.clone.iz) | copy-start | bytes 208
  3.6 1.0 %copy-start.15 = (f32[33]{0:T(128)S(1)}, f32[33]{0:T(128)}, u32[]{:S(2)}) copy-start(f32[33]{0:T(128)} %constant.61.clone.iy) | copy-start | bytes 400
  3.7 1.0 %copy-start.12 = (f32[1,2,16]{2,1,0:T(2,128)S(1)}, f32[1,2,16]{2,1,0:T(2,128)}, u32[]{:S(2)}) copy-start(f32[1,2,16]{2,1,0:T(2,128)} %param.29) | copy-start | bytes 388
  3.7 1.0 %copy-start.13 = (s32[16]{0:T(128)S(1)}, s32[16]{0:T(128)}, u32[]{:S(2)}) copy-start(s32[16]{0:T(128)} %index.3) | copy-start | bytes 196
  6.5 15.7 %collective-permute-start = (f32[9,33,128]{2,1,0:T(8,128)S(1)}, f32[9,33,128]{2,1,0:T(8,128)S(1)}, u32[]{:S(2)}, u32[]{:S(2)}) collective-permute-start(f32[9,33,128]{2,1,0:T(8,128)S(1)} %get-tuple-element.22), channel_id=1, source_target_pairs={{0,8},{8,16},{16,24},{24,32},{32,40},{40,48},{48,56},{56,64},{64,7... | collective-permute-start | bytes 456200 | tf_op jit(solution)/shard_map/ppermute | solution.py:384
  8.5 14.8 %collective-permute-start.1 = (f32[9,33,128]{2,1,0:T(8,128)S(1)}, f32[9,33,128]{2,1,0:T(8,128)S(1)}, u32[]{:S(2)}, u32[]{:S(2)}) collective-permute-start(f32[9,33,128]{2,1,0:T(8,128)S(1)} %get-tuple-element.23), channel_id=1, source_target_pairs={{0,504},{8,0},{16,8},{24,16},{32,24},{40,32},{48,40},{56,48},{64,5... | collective-permute-start | bytes 456200 | tf_op jit(solution)/shard_map/ppermute | solution.py:384
  20.2 3.0 %copy-start.4 = (bf16[256,256]{1,0:T(8,128)(2,1)S(1)}, bf16[256,256]{1,0:T(8,128)(2,1)}, u32[]{:S(2)}) copy-start(bf16[256,256]{1,0:T(8,128)(2,1)} %constant.62.clone.g_hi) | copy-start | bytes 393220
  20.2 3.0 %copy-start.5 = (bf16[256,256]{1,0:T(8,128)(2,1)S(1)}, bf16[256,256]{1,0:T(8,128)(2,1)}, u32[]{:S(2)}) copy-start(bf16[256,256]{1,0:T(8,128)(2,1)} %constant.63.clone.g_lo) | copy-start | bytes 393220
  20.3 3.0 %copy-start.6 = (bf16[256,256]{1,0:T(8,128)(2,1)S(1)}, bf16[256,256]{1,0:T(8,128)(2,1)}, u32[]{:S(2)}) copy-start(bf16[256,256]{1,0:T(8,128)(2,1)} %constant.64.clone.t_hi) | copy-start | bytes 393220
  20.3 3.0 %copy-start.7 = (bf16[256,256]{1,0:T(8,128)(2,1)S(1)}, bf16[256,256]{1,0:T(8,128)(2,1)}, u32[]{:S(2)}) copy-start(bf16[256,256]{1,0:T(8,128)(2,1)} %constant.65.clone.t_lo) | copy-start | bytes 393220
  20.3 3.0 %copy-start.10 = (bf16[256,128]{1,0:T(8,128)(2,1)S(1)}, bf16[256,128]{1,0:T(8,128)(2,1)}, u32[]{:S(2)}) copy-start(bf16[256,128]{1,0:T(8,128)(2,1)} %constant.66.clone.pick) | copy-start | bytes 196612
  29.9 14.3 %all-to-all-start = ((f32[8,72,128]{2,1,0:T(8,128)}), f32[8,72,128]{2,1,0:T(8,128)S(1)}, u32[]{:S(2)}, u32[]{:S(2)}) async-start(f32[8,72,128]{2,1,0:T(8,128)} %bitcast.1), calls=%async_computation | async-start | bytes 589824 | tf_op jit(solution)/shard_map/all_to_all | solution.py:426
  44.1 13.8 %copy-start.9 = (bf16[384,128]{1,0:T(8,128)(2,1)S(1)}, bf16[384,128]{1,0:T(8,128)(2,1)}, u32[]{:S(2)}) copy-start(bf16[384,128]{1,0:T(8,128)(2,1)} %constant.68.clone.gx_lo) | copy-start | bytes 294916
  44.2 13.8 %copy-start.8 = (bf16[384,128]{1,0:T(8,128)(2,1)S(1)}, bf16[384,128]{1,0:T(8,128)(2,1)}, u32[]{:S(2)}) copy-start(bf16[384,128]{1,0:T(8,128)(2,1)} %constant.67.clone.gx_hi) | copy-start | bytes 294916
  44.2 6.3 %collective-permute-start.3 = (f32[72,128]{1,0:T(8,128)S(1)}, f32[72,128]{1,0:T(8,128)S(1)}, u32[]{:S(2)}, u32[]{:S(2)}) collective-permute-start(f32[72,128]{1,0:T(8,128)S(1)} %reduce_sum.9.own), channel_id=1, source_target_pairs={{0,504},{8,0},{16,8},{24,16},{32,24},{40,32},{48,40},{56,48},{64,5... | collective-permute-start | bytes 110600 | tf_op jit(solution)/shard_map/ppermute | solution.py:384
  50.6 7.4 %collective-permute-start.2 = (f32[72,128]{1,0:T(8,128)S(1)}, f32[72,128]{1,0:T(8,128)S(1)}, u32[]{:S(2)}, u32[]{:S(2)}) collective-permute-start(f32[72,128]{1,0:T(8,128)S(1)} %get-tuple-element.35), channel_id=1, source_target_pairs={{0,8},{8,16},{16,24},{24,32},{32,40},{40,48},{48,56},{56,64},{64,7... | collective-permute-start | bytes 110600 | tf_op jit(solution)/shard_map/ppermute | solution.py:384
  58.9 12.4 %all-to-all-start.1 = ((f32[8,72,128]{2,1,0:T(8,128)}), f32[8,72,128]{2,1,0:T(8,128)S(1)}, u32[]{:S(2)}, u32[]{:S(2)}) async-start(f32[8,72,128]{2,1,0:T(8,128)} %shard_map.239), calls=%async_computation.1 | async-start | bytes 589824 | tf_op jit(solution)/shard_map/all_to_all | solution.py:440
  67.1 4.2 %copy-start.2 = (bf16[320,256]{1,0:T(8,128)(2,1)S(1)}, bf16[320,256]{1,0:T(8,128)(2,1)}, u32[]{:S(2)}) copy-start(bf16[320,256]{1,0:T(8,128)(2,1)} %constant.69.clone.blocks_hi) | copy-start | bytes 491524
  67.1 4.2 %copy-start.3 = (bf16[320,256]{1,0:T(8,128)(2,1)S(1)}, bf16[320,256]{1,0:T(8,128)(2,1)}, u32[]{:S(2)}) copy-start(bf16[320,256]{1,0:T(8,128)(2,1)} %constant.70.clone.blocks_lo) | copy-start | bytes 491524
  67.1 4.2 %copy-start.11 = (f32[40,128]{1,0:T(8,128)S(1)}, f32[40,128]{1,0:T(8,128)}, u32[]{:S(2)}) copy-start(f32[40,128]{1,0:T(8,128)} %constant.71.clone.last) | copy-start | bytes 61444

commit v2 on v1

v2 whole, which is shorter than its diff:
```python
import jax
import jax.numpy as jnp
import numpy as np
from jax import lax
from jax.experimental import pallas as pl
from jax.experimental.pallas import tpu as pltpu
from jax.sharding import PartitionSpec as P

DT2 = 0.003
SIGMA_Y = 1.0
ZP, YP, XL = 17, 33, 128
YPAD = 40
ROWS = ZP * YPAD
HALF = 9
KROWS = 576


def gll_tables():
    nodes = np.array([-1.0, -np.sqrt(3.0 / 7.0), 0.0, np.sqrt(3.0 / 7.0), 1.0])
    weights = np.array([0.1, 49.0 / 90.0, 32.0 / 45.0, 49.0 / 90.0, 0.1])
    deriv = np.zeros((5, 5))
    for a in range(5):
        for b in range(5):
            for m in range(5):
                if m == b:
                    continue
                factor = 1.0 / (nodes[b] - nodes[m])
                for k in range(5):
                    if k == b or k == m:
                        continue
                    factor = factor * (nodes[a] - nodes[k]) / (nodes[b] - nodes[k])
                deriv[a, b] += factor
    return weights, deriv


GW, GD = gll_tables()
SHARED = np.array([0.2, GW[1], GW[2], GW[3], 0.2])
APPLY = GW[:, None] * GD
GATHER = (GD / SHARED[None, :]).T


def split(m):
    hi = np.asarray(m, np.float32).astype(jnp.bfloat16)
    lo = (np.asarray(m, np.float32) - hi.astype(np.float32)).astype(jnp.bfloat16)
    return hi, lo


LANE_A, LANE_B, LANE_K, LANE_PA, LANE_CA, LANE_PB, LANE_CB = 0, 13, 26, 39, 44, 52, 57


def x_tables():
    def node(e, a):
        if 0 <= e < 32:
            return 4 * e + a if a < 4 else XL + e
        return XL + {-1: 32, -2: 37, 32: 42}[e] + a

    def halo(c):
        return c + 8 if c < 0 else 8 + c - XL

    grad, edge = np.zeros((XL, 2 * XL)), np.zeros((XL, 2 * XL))
    back = np.zeros((2 * XL, 2 * XL))
    pick, pick_edge = np.zeros((XL, XL)), np.zeros((XL, XL))
    for e in range(-2, 33):
        for a in range(5):
            n = node(e, a)
            for b in range(5):
                c = 4 * e + b
                own = 0 <= c < XL
                (grad if own else edge)[c if own else halo(c), n] += APPLY[a, b]
                if -4 <= c <= XL:
                    back[n, c if own else XL + halo(c)] += GATHER[b, a]
            if n >= XL:
                c = 4 * e + a
                if 0 <= c < XL:
                    pick[c, n - XL] = 1.0
                else:
                    pick_edge[LANE_K + halo(c), n - XL] = 1.0
    return grad, edge, back, pick, pick_edge


def tables():
    grad, edge, back, pick, pick_edge = x_tables()
    g_hi, g_lo = split(grad)
    e_hi, e_lo = split(edge)
    first = np.zeros((2 * XL, 5 * XL), jnp.bfloat16)
    for i, (part, choose) in enumerate(((e_hi, 1.0), (e_hi, 1.0), (e_lo, 0.0))):
        rows = np.asarray(part)
        first[64 * i : 64 * i + 13, 0 : 2 * XL] = rows[0:13]
        first[64 * i + LANE_B : 64 * i + LANE_B + 13, 2 * XL : 4 * XL] = rows[0:13]
        first[64 * i : 64 * i + 64, 4 * XL :] = (choose * pick_edge[0:64]).astype(jnp.bfloat16)
    second = []
    for at in (LANE_A, LANE_B):
        m = np.zeros((XL, 2 * XL), jnp.bfloat16)
        for i, part in enumerate((e_hi, e_hi, e_lo)):
            m[32 * i + at + 4 : 32 * i + at + 9] = np.asarray(part)[4:9]
        second.append(np.concatenate([np.asarray(g_lo), m], 0))
    t_hi, t_lo = (np.asarray(t) for t in split(back))
    moved = [np.roll(t[:, XL:], LANE_B, 1) for t in (t_hi, t_lo)]
    return dict(
        grad=np.concatenate([np.asarray(g_hi)] * 2, 0),
        grad_lo=np.asarray(g_lo),
        pick=np.concatenate([pick, pick], 0).astype(jnp.bfloat16),
        first=first,
        second_a=second[0],
        second_b=second[1],
        ta_hi=t_hi,
        ta_lo=t_lo,
        tb_hi=np.concatenate([t_hi[:, :XL], moved[0]], 1),
        tb_lo=np.concatenate([t_lo[:, :XL], moved[1]], 1),
        t_both=np.concatenate([t_hi[:, :XL], t_lo[:, :XL]], 1),
    )


def smoothing_tables():
    offsets = np.arange(3 * XL)[:, None] - XL - np.arange(XL)[None, :]
    sigma_x = XL / 2.0
    gauss_x = np.exp(-0.5 * (offsets / sigma_x) ** 2) * (np.abs(offsets) <= XL)
    normal_x = np.exp(-0.5 * (np.arange(-XL, XL + 1) / sigma_x) ** 2).sum()
    distance = np.arange(YP)[:, None] - np.arange(YP)[None, :]
    gauss_y = np.exp(-0.5 * (distance / SIGMA_Y) ** 2)
    gauss_y = gauss_y / gauss_y.sum(axis=1, keepdims=True)
    undo = np.zeros((YP, YP))
    for y in range(YP):
        if y == 16:
            undo[y, y] = 1.0
        else:
            undo[y, 32 - y] = 0.5
            undo[y, y] = 0.5 if y < 16 else -0.5
    return gauss_x / normal_x, gauss_y @ undo


def apply5(m, x):
    e0, o0, e1, o1, mid = x[0] + x[4], x[0] - x[4], x[1] + x[3], x[1] - x[3], x[2]
    f = lambda v: np.float32(v)
    odd = [
        f((m[a, 0] + m[a, 4]) / 2) * e0 + f((m[a, 1] + m[a, 3]) / 2) * e1 + f(m[a, 2]) * mid
        for a in (0, 1)
    ]
    even = [
        f((m[a, 0] - m[a, 4]) / 2) * o0 + f((m[a, 1] - m[a, 3]) / 2) * o1 for a in (0, 1, 2)
    ]
    return [even[0] + odd[0], even[1] + odd[1], even[2], even[1] - odd[1], even[0] - odd[0]]


def apply_y(fields, kappa):
    row = lax.broadcasted_iota(jnp.int32, (8, XL), 0)

    def plane(z, carry):
        at = lambda a: pl.ds(a, 8, stride=4)
        k = [kappa[z, at(a), :] for a in range(5)]
        for v, out in fields:
            g = apply5(APPLY, [v[z, at(a), :] for a in range(5)])
            o = apply5(GATHER, [k[a] * g[a] for a in range(5)])
            moved = pltpu.roll(o[4], 1, 0)
            out[z, at(0), :] = jnp.where(row == 0, 2.0 * o[0], o[0] + moved)
            for b in range(1, 4):
                out[z, at(b), :] = o[b]
            out[z, 32:33, :] = 2.0 * moved[0:1]
        return carry

    lax.fori_loop(0, ZP, plane, 0)


def apply_z(fields, kappa, use):
    def block(rows):
        for i, v in enumerate(fields):
            ends = None
            for e in range(4):
                g = apply5(APPLY, [v[4 * e + a, rows, :] for a in range(5)])
                o = apply5(GATHER, [kappa[4 * e + a, rows, :] * g[a] for a in range(5)])
                use(i, 4 * e, rows, 2.0 * o[0] if e == 0 else o[0] + ends)
                for b in range(1, 4):
                    use(i, 4 * e + b, rows, o[b])
                ends = o[4]
            use(i, 16, rows, 2.0 * ends)

    def step(j, carry):
        block(pl.ds(pl.multiple_of(8 * j, 8), 8))
        return carry

    lax.fori_loop(0, 4, step, 0)
    block(pl.ds(32, 1))


def add_forcing(target, c_ref, index, source, instant, iz, iy):
    lane = lax.broadcasted_iota(jnp.int32, (1, XL), 1)
    node = lane % 4
    inv_x = jnp.where(
        node == 0, 1.0 / SHARED[0], jnp.where(node == 2, 1.0 / SHARED[2], 1.0 / SHARED[1])
    ).astype(jnp.float32)
    for r in range(16):
        point = index[r]
        row = lax.shift_right_logical(point, 7)
        z = lax.shift_right_logical(row * 1986, 16)
        y = row - z * YP
        amount = source[instant, r] * iz[z] * iy[y]
        at = (pl.ds(z, 1), pl.ds(y, 1), slice(None))
        change = jnp.where(lane == (point & (XL - 1)), inv_x * amount, 0.0)
        target[at] = target[at] + c_ref[at] * change[None]


def flip_rows(source, target, flag):
    for y in range(YP):
        to = jnp.where(flag != 0, 32 - y, y)
        target[:, pl.ds(to, 1), :] = source[:, y : y + 1, :]


def pack_kernel(
    flip, index, source, iz, iy, an_in, bn_in, ap_in, bp_in, ka_in, de_in,
    right_out, left_out, an, bn, ap, bp, ka, c_out, f_out, pack, de, sem,
):
    rows = slice(0, YP)
    copies = [
        pltpu.make_async_copy(de_in, de.at[:, rows, :], sem.at[0]),
        pltpu.make_async_copy(ka_in, ka.at[:, rows, :], sem.at[1]),
    ]
    for i, (src, dst) in enumerate(((an_in, an), (bn_in, bn), (ap_in, ap), (bp_in, bp))):
        copies.append(pltpu.make_async_copy(src.at[:, :, 0, :], dst.at[:, rows, :], sem.at[2 + i]))
    for copy in copies:
        copy.start()
    f_out[...] = jnp.zeros_like(f_out)
    lane = lax.broadcasted_iota(jnp.int32, (YP, XL), 1)
    copies[0].wait()
    for z in range(ZP):
        c_out[z, 0:YP, :] = DT2 / de[z, 0:YP, :]
    add_forcing(f_out, c_out, index, source, 0, iz, iy)
    for copy in copies[1:]:
        copy.wait()
    for z in range(ZP):
        group = 0 if z < HALF else 64
        a, b, k, c = an[z, rows, :], bn[z, rows, :], ka[z, rows, :], c_out[z, rows, :]
        pa = 2.0 * a - ap[z, rows, :] + f_out[z, rows, :]
        pb = 2.0 * b - bp[z, rows, :]
        tile = None
        parts = [
            (a, 120, LANE_A), (b, 120, LANE_B), (k, 120, LANE_K), (pa, 124, LANE_PA),
            (c, 124, LANE_CA), (pb, 124, LANE_PB), (c, 124, LANE_CB),
        ]
        above = None
        for value, first, to in reversed(parts):
            moved = pltpu.roll(value, (group + to - first) % XL, 1)
            tile = moved if tile is None else jnp.where(lane < above, moved, tile)
            above = group + to
        if group:
            pack[z - HALF, :, :] = jnp.where(lane < 64, pack[z - HALF, :, :], tile)
        else:
            pack[z, :, :] = tile
    left_out[...] = pack[...]
    flip_rows(pack, right_out, flip[0])


def dot(a, b):
    return jnp.dot(a, b, preferred_element_type=jnp.float32)


def halves(x):
    hi = x.astype(jnp.bfloat16)
    return hi, (x - hi.astype(jnp.float32)).astype(jnp.bfloat16)


def dot3(x, m_hi, m_lo):
    hi, lo = halves(x)
    return dot(hi, m_hi) + dot(lo, m_hi) + dot(hi, m_lo)


def flat(ref):
    return ref[...].reshape(ROWS, ref.shape[-1])


def local_kernel(
    index, source, iz, iy, a, b, ka, c, f, grad, grad_lo, pick,
    a_out, b_out, f1_out, ga_out, gb_out, kg_out,
):
    apply_y(((a, a_out), (b, b_out)), ka)

    def use(i, z, rows, value):
        out = (a_out, b_out)[i]
        total = c[z, rows, :] * (out[z, rows, :] + value)
        out[z, rows, :] = f[z, rows, :] - total if i == 0 else -total

    apply_z((a, b), ka, use)
    f1_out[...] = jnp.zeros_like(f1_out)
    add_forcing(f1_out, c, index, source, 1, iz, iy)
    for field, out in ((a, ga_out), (b, gb_out)):
        hi, lo = halves(flat(field))
        out[...] = dot(jnp.concatenate([hi, lo], 1), grad[...]) + dot(hi, grad_lo[...])
    hi, lo = halves(flat(ka))
    kg_out[...] = dot(jnp.concatenate([hi, lo], 1), pick[...])


def step_kernel(
    flip, an, ap, bn, bp, ka, c, a0, b0, f1, ga, gb, kg0, right_in, left_in,
    first, grad, second_a, ta_hi, ta_lo, tb_hi, tb_lo, t_both,
    k_out, al_out, bl_out, af_out, v1b, u1_out, kg,
    left, u, ku, cu, qu, wa, wb, y1, v1a, k, sem,
):
    lane = lax.broadcasted_iota(jnp.int32, (YP, XL), 1)
    rows = slice(0, YP)
    sent = []

    def send(src, dst, dense):
        if dense:
            src, dst = src.at[:, rows, :], dst.at[:, :, 0, :]
        sent.append(pltpu.make_async_copy(src, dst, sem.at[len(sent)]))
        sent[-1].start()

    flip_rows(left_in, left, flip[0])
    before = None
    for start, n in (
        (LANE_A, 8), (LANE_B, 8), (LANE_K, 8), (LANE_PA, 4), (LANE_CA, 4), (LANE_PB, 4), (LANE_CB, 4)
    ):
        one = ((lane % 64) >= start) & ((lane % 64) < start + n)
        before = one if before is None else before | one
    for z in range(ZP):
        i = z % HALF
        tile = jnp.where(before, right_in[i], left[i])
        if z >= HALF:
            tile = pltpu.roll(tile, 64, 1)
        u[z, rows, :] = tile
        ku[z, rows, :] = jnp.where(
            lane < LANE_B,
            pltpu.roll(tile, XL - LANE_K, 1),
            pltpu.roll(tile, XL - LANE_K + LANE_B, 1),
        )
        qu[z, rows, :] = pltpu.roll(tile, XL - LANE_PA + 4, 1)
        cu[z, rows, :] = pltpu.roll(tile, XL - LANE_CA + 4, 1)
    apply_y(((u, y1),), ku)

    def use(i, z, rows, value):
        qu[z, rows, :] = qu[z, rows, :] - cu[z, rows, :] * (y1[z, rows, :] + value)

    apply_z((u,), ku, use)

    lane2 = lax.broadcasted_iota(jnp.int32, (ROWS, XL), 1)
    tall = lambda value: value.reshape(ZP, YPAD, value.shape[-1])
    hi, lo = halves(flat(u))
    low = pltpu.roll(lo.astype(jnp.float32), 64, 1)
    mixed = jnp.where(lane2 < 64, hi.astype(jnp.float32), low).astype(jnp.bfloat16)
    edge = dot(jnp.concatenate([mixed, hi], 1), first[...])
    kg[...] = jnp.concatenate([flat(ka), kg0[...] + edge[:, 4 * XL :]], 1)
    xa = dot3((ga[...] + edge[:, 0 : 2 * XL]) * kg[...], ta_hi[...], ta_lo[...])
    xb = dot3((gb[...] + edge[:, 2 * XL : 4 * XL]) * kg[...], tb_hi[...], tb_lo[...])
    u1 = flat(qu) - flat(cu) * (xa[:, XL:] + xb[:, XL:])
    hi = u1.astype(jnp.bfloat16).astype(jnp.float32)
    packed = jnp.where(
        lane2 < 32,
        hi,
        jnp.where(lane2 < 64, pltpu.roll(u1 - hi, 32, 1), pltpu.roll(hi, 64, 1)),
    ).astype(jnp.bfloat16)
    u1_out[...] = packed
    wa[...] = tall(xa[:, 0:XL])
    wb[...] = tall(xb[:, 0:XL])
    for z in range(ZP):
        cz = c[z, rows, :]
        acc_a = a0[z, rows, :] - cz * wa[z, rows, :]
        acc_b = b0[z, rows, :] - cz * wb[z, rows, :]
        a, b = an[z, rows, :], bn[z, rows, :]
        v1a[z, rows, :] = 2.0 * a - ap[z, rows, :] + acc_a
        v1b[z, rows, :] = 2.0 * b - bp[z, rows, :] + acc_b
        ku[z, rows, :] = b * acc_a
    send(v1a, al_out, True)
    send(v1b, bl_out, True)
    apply_y(((v1a, y1),), ka)

    def add(i, z, rows, value):
        y1[z, rows, :] = y1[z, rows, :] + value

    apply_z((v1a,), ka, add)
    wa[...] = tall(second_x(v1a, packed, grad, second_a, kg, t_both))
    for z in range(ZP):
        acc_a = f1[z, rows, :] - c[z, rows, :] * (wa[z, rows, :] + y1[z, rows, :])
        ku[z, rows, :] = ku[z, rows, :] + v1b[z, rows, :] * acc_a
        wb[z, rows, :] = 2.0 * v1a[z, rows, :] - an[z, rows, :] + acc_a
    send(wb, af_out, True)
    for y in range(YP):
        u[:, 32 - y : 33 - y, :] = ku[:, y : y + 1, :]
    row = lax.broadcasted_iota(jnp.int32, (YP, XL), 0)
    sign = jnp.where(row < 16, 1.0, jnp.where(row == 16, 0.0, -1.0)).astype(jnp.float32)
    k[ZP * 32 :, :] = jnp.zeros((KROWS - ZP * 32, XL), jnp.float32)
    for z in range(ZP):
        t = u[z, rows, :] + sign * ku[z, rows, :]
        k[32 * z : 32 * z + 32, :] = t[0:32]
        k[ZP * 32 + z : ZP * 32 + z + 1, :] = t[32:33]
        if z in (4, 8, 12):
            at = pl.ds(32 * (z - 4), 128)
            send(k.at[at], k_out.at[at], False)
    at = pl.ds(384, KROWS - 384)
    send(k.at[at], k_out.at[at], False)
    for copy in sent:
        copy.wait()


def second_x(v, packed, grad, second, kg, t_both):
    hi, lo = halves(flat(v))
    g = dot(jnp.concatenate([hi, lo], 1), grad[...])
    g = g + dot(jnp.concatenate([hi, packed], 1), second[...])
    hi, lo = halves(g * kg[...])
    both = dot(hi, t_both[...])
    return both[:, 0:XL] + both[:, XL:] + dot(lo, t_both[:, 0:XL])


def last_kernel(bn, ka, c, v1b, u1, kg, grad, second_b, t_both, bf_out, y1, wb, sem):
    rows = slice(0, YP)
    apply_y(((v1b, y1),), ka)

    def add(i, z, rows, value):
        y1[z, rows, :] = y1[z, rows, :] + value

    apply_z((v1b,), ka, add)
    x = second_x(v1b, u1[...], grad, second_b, kg, t_both)
    wb[...] = x.reshape(ZP, YPAD, XL)
    for z in range(ZP):
        acc = c[z, rows, :] * (wb[z, rows, :] + y1[z, rows, :])
        wb[z, rows, :] = 2.0 * v1b[z, rows, :] - bn[z, rows, :] - acc
    copy = pltpu.make_async_copy(wb.at[:, rows, :], bf_out.at[:, :, 0, :], sem.at[0])
    copy.start()
    copy.wait()


def odd_sign(flip, group, part):
    row = group[0] * part + lax.broadcasted_iota(jnp.int32, (part, XL), 0)
    odd = ((row & 31) > 16) | (row >= ZP * 32)
    return jnp.where(odd & (flip[0] != 0), -1.0, 1.0).astype(jnp.float32)


def sum_kernel(flip, group, parts, total_out, signed_out):
    total = parts[0]
    for i in range(1, parts.shape[0]):
        total = total + parts[i]
    total_out[...] = total
    signed_out[...] = total * odd_sign(flip, group, total.shape[0])


def smooth_kernel(flip, group, before, own, after, gx_hi, gx_lo, out, done, sem):
    sign = odd_sign(flip, group, own.shape[0])
    total = None
    for i, part in enumerate((before[...], own[...], after[...] * sign)):
        at = slice(XL * i, XL * (i + 1))
        one = dot3(part, gx_hi[at, :], gx_lo[at, :])
        total = one if total is None else total + one
    done[...] = total
    copies = [pltpu.make_async_copy(done, out.at[i], sem.at[i]) for i in range(out.shape[0])]
    for copy in copies:
        copy.start()
    for copy in copies:
        copy.wait()


def finish_kernel(t, blocks_hi, blocks_lo, last, out, done_all, sem):
    def planes(first, n):
        rows = t[32 * first : 32 * (first + n), :]
        hi, lo = halves(rows)
        m_hi, m_lo = blocks_hi[0 : n * YPAD, 0 : n * 32], blocks_lo[0 : n * YPAD, 0 : n * 32]
        done = dot(m_hi, hi) + dot(m_hi, lo) + dot(m_lo, hi)
        for i in range(n):
            z = first + i
            extra = last[...] * t[ZP * 32 + z : ZP * 32 + z + 1, :]
            done_all[z] = done[i * YPAD : (i + 1) * YPAD] + extra
        at = pl.ds(first, n)
        copy = pltpu.make_async_copy(done_all.at[at, 0:YP, :], out.at[at], sem.at[first // 8])
        copy.start()
        return copy

    for copy in [planes(0, 8), planes(8, 8), planes(16, 1)]:
        copy.wait()


SMEM_SPEC = pl.BlockSpec(memory_space=pltpu.SMEM)
VMEM_SPEC = pl.BlockSpec(memory_space=pltpu.VMEM)
ANY_SPEC = pl.BlockSpec(memory_space=pl.ANY)


def near(*shape, dtype=jnp.float32):
    return pltpu.VMEM(shape, dtype)


def far(*shape, dtype=jnp.float32):
    return pltpu.HBM(shape, dtype)


def call(kernel, outs, scalars, arrays, scratch=(), far_in=False, flops=0, moved=0, limit=24):
    if far_in:
        arrays = [pltpu.with_memory_space_constraint(v, pltpu.HBM) for v in arrays]
    out_specs = [ANY_SPEC if o.memory_space == pltpu.HBM else VMEM_SPEC for o in outs]
    return pl.pallas_call(
        kernel,
        out_shape=outs,
        in_specs=[SMEM_SPEC] * len(scalars) + [ANY_SPEC if far_in else VMEM_SPEC] * len(arrays),
        out_specs=out_specs,
        scratch_shapes=list(scratch),
        compiler_params=pltpu.CompilerParams(vmem_limit_bytes=limit * 1024 * 1024),
        cost_estimate=pl.CostEstimate(flops=flops, bytes_accessed=moved, transcendentals=0),
    )(*scalars, *arrays)


def shift(value, axis, by):
    n = lax.axis_size(axis)
    return lax.ppermute(value, axis, [(i, (i + by) % n) for i in range(n)])


def local(an, ap, bn, bp, kappa, density, flip, index, source):
    dense, padded, edge = far(ZP, YP, 1, XL), near(ZP, YPAD, XL), near(HALF, YP, XL)
    inv_z, inv_y = (np.tile(1.0 / SHARED[:4], n) for n in (4, 8))
    inv_z, inv_y = (np.append(v, v[0] * 2) for v in (inv_z, inv_y))
    inv_z[0] *= 2
    inv_y[0] *= 2
    iz, iy = jnp.asarray(inv_z, jnp.float32), jnp.asarray(inv_y, jnp.float32)
    src = source[0]
    tab = {name: jnp.asarray(value) for name, value in tables().items()}
    fields = [v.reshape(ZP, YP, 1, XL) for v in (an, bn, ap, bp)]
    dma = pltpu.SemaphoreType.DMA
    to_right, to_left, an, bn, ap, bp, ka, c, f0 = call(
        pack_kernel,
        [edge, edge] + [padded] * 7,
        [flip, index, src, iz, iy],
        [*fields, kappa, density],
        [edge, padded, dma((6,))],
        far_in=True,
        moved=4_000_000,
    )
    from_left = shift(to_right, "cuts", 1)
    from_right = shift(to_left, "cuts", -1)
    wide, narrow = near(ROWS, 2 * XL), near(ROWS, XL)
    a0, b0, f1, ga, gb, kg0 = call(
        local_kernel,
        [padded, padded, padded, wide, wide, narrow],
        [index, src, iz, iy],
        [an, bn, ka, c, f0, tab["grad"], tab["grad_lo"], tab["pick"]],
        flops=300_000_000,
        moved=5_000_000,
    )
    packed = near(ROWS, XL, dtype=jnp.bfloat16)
    k, al, bl, af, v1b, u1, kg = call(
        step_kernel,
        [far(KROWS, XL), dense, dense, dense, padded, packed, wide],
        [flip],
        [an, ap, bn, bp, ka, c, a0, b0, f1, ga, gb, kg0, from_left, from_right]
        + [tab[n] for n in ("first", "grad", "second_a", "ta_hi", "ta_lo", "tb_hi", "tb_lo", "t_both")],
        [edge] + [padded] * 8 + [near(KROWS, XL), dma((7,))],
        flops=600_000_000,
        moved=6_000_000,
    )
    groups = lax.axis_size("event")
    part = KROWS // groups
    parts = lax.all_to_all(k.reshape(groups, part, XL), "event", 0, 0)
    bf = call(
        last_kernel,
        [dense],
        [],
        [bn, ka, c, v1b, u1, kg, tab["grad"], tab["second_b"], tab["t_both"]],
        [padded, padded, dma((1,))],
        flops=300_000_000,
        moved=5_000_000,
    )[0]
    outs = (af, al, bf, bl)
    group = lax.axis_index("event").astype(jnp.int32).reshape(1)
    total, signed = call(sum_kernel, [near(part, XL)] * 2, [flip, group], [parts])
    before = shift(signed, "cuts", 1)
    after = shift(total, "cuts", -1)
    gauss_x, final_y = smoothing_tables()
    spread = call(
        smooth_kernel,
        [far(groups, part, XL)],
        [flip, group],
        [before, total, after, *(jnp.asarray(v) for v in split(gauss_x))],
        [near(part, XL), dma((8,))],
    )[0]
    whole = lax.all_to_all(spread, "event", 0, 0).reshape(KROWS, XL)
    blocks = np.zeros((8 * YPAD, 256))
    for i in range(8):
        blocks[i * YPAD : i * YPAD + YP, i * 32 : i * 32 + 32] = final_y[:, 0:32]
    last = np.zeros((YPAD, XL))
    last[0:YP] = final_y[:, 32:33]
    smoothed = call(
        finish_kernel,
        [far(ZP, YP, XL)],
        [],
        [whole, *(jnp.asarray(v) for v in split(blocks)), jnp.asarray(last, jnp.float32)],
        [near(ZP, YPAD, XL), dma((3,))],
    )[0]
    return *(v.reshape(1, ZP, YP, XL) for v in outs), smoothed


def solution(mesh):
    field = P("event", None, None, "cuts")
    grid = P(None, None, "cuts")
    return jax.shard_map(
        local,
        mesh=mesh,
        in_specs=(field,) * 4 + (grid, grid, P("cuts"), P("cuts"), P("event", None, "cuts")),
        out_specs=(field,) * 4 + (grid,),
        check_vma=False,
    )
```

time: 73 us -> 66.1 us (0.905)
  local copies, waits for them, and re-layouts: 7.34 us -> 0.77 us
  waiting for transfers between devices: 18.5 us -> 14.9 us
  Pallas kernels: 12.5 us -> 14.4 us
  starting transfers between devices: 32.5 us -> 34 us
    unnamed x46 -> x40, local copies, waits for them, and re-layouts: 7.34 us -> 0.77 us
    ppermute x4, waiting for transfers between devices: 8.1 us -> 2.43 us  [shift(): return lax.ppermute(value, axis, [(i, (i + by) % n) for i in range(n)])]
    all_to_all x1, waiting for transfers between devices: 3.16 us -> 5.14 us  [local(): whole = lax.all_to_all(spread, 'event', 0, 0).reshape(KROWS, XL)]
    pallas_call x5 -> x7, Pallas kernels: 12.5 us -> 14.4 us  [call(): pl.pallas_call(kernel, out_shape=outs, in_specs=[SMEM_SPEC] * len(scalars...]
    ppermute x4, starting transfers between devices: 20.3 us -> 21.5 us  [shift(): return lax.ppermute(value, axis, [(i, (i + by) % n) for i in range(n)])]
  transfers between devices with their start and end apart: 6 -> 6, of which waited for: 5 -> 4; matrix products, arithmetic and copies ran while one was open for 6% -> 0% of each run, Pallas kernels for 3% -> 6%
where the time goes in v2:
time: 66.1 us; the launch traced here: 65.6 us
  starting transfers between devices  34 us (51%)
  waiting for transfers between devices  14.9 us (23%)
  Pallas kernels  14.4 us (22%)
  between operations  1.55 us (2%)
  local copies, waits for them, and re-layouts  0.77 us (1%)
    ppermute x4, starting transfers between devices, shift(): return lax.ppermute(value, axis, [(i, (i + by) % n) for i in range(n)])  21.5 us
    pallas_call x7, Pallas kernels, call(): pl.pallas_call(kernel, out_shape=outs, in_specs=[SMEM_SPEC] * len(scalars...  14.4 us
    all_to_all x1, waiting for transfers between devices, local(): parts = lax.all_to_all(k.reshape(groups, part, XL), 'event', 0, 0)  7.31 us
    all_to_all x1, starting transfers between devices, local(): parts = lax.all_to_all(k.reshape(groups, part, XL), 'event', 0, 0)  7.07 us
    all_to_all x1, starting transfers between devices, local(): whole = lax.all_to_all(spread, 'event', 0, 0).reshape(KROWS, XL)  5.44 us
    all_to_all x1, waiting for transfers between devices, local(): whole = lax.all_to_all(spread, 'event', 0, 0).reshape(KROWS, XL)  5.14 us
    ppermute x4, waiting for transfers between devices, shift(): return lax.ppermute(value, axis, [(i, (i + by) % n) for i in range(n)])  2.43 us
  transfers between devices with their start and end apart: 6, of which 4 were waited for; matrix products, arithmetic and copies ran while one was open for 0% of the time, Pallas kernels for 6%

profile of v2, /device:TPU:8, one launch (start us, length us, event | category | flops | bytes accessed | tf_op | source)
XLA Modules:
  0.0 65.6 jit_solution(16751247560647770399)
XLA Ops:
  1.3 0.0 copy-start.18
  1.3 0.0 copy-start.19
  1.3 0.0 copy-start.16
  1.3 0.0 copy-start.17
  1.3 0.6 copy-done.18
  1.9 0.0 copy-done.19
  2.0 0.0 copy-done.16
  2.0 0.0 copy-done.17
  2.0 0.0 copy-start
  2.0 0.0 copy-start.13
  2.0 0.0 copy-start.14
  2.0 2.8 %shard_map.290 = (f32[9,33,128]{2,1,0:T(8,128)S(1)}, f32[9,33,128]{2,1,0:T(8,128)S(1)}, f32[17,40,128]{2,1,0:T(8,128)S(1)}, f32[17,40,128]{2,1,0:T(8,128)S(1)}, ...) custom-call(s32[1]{0:T(128)S(6)} %copy.32.flip, ...), custom_call_target="tpu_custom_call" | custom-call | bytes 4000000 | tf_op jit(solution)/shard_map/pallas_call | solution.py:485
  4.9 1.9 %collective-permute-start = (f32[9,33,128]{2,1,0:T(8,128)S(1)}, f32[9,33,128]{2,1,0:T(8,128)S(1)}, u32[]{:S(2)}, u32[]{:S(2)}) collective-permute-start(f32[9,33,128]{2,1,0:T(8,128)S(1)} %get-tuple-element.42), channel_id=1, source_target_pairs={{0,8},{8,16},{16,24},{24,32},{32,40},{40,48},{48,56},{56,64},{64,7... | collective-permute-start | bytes 456200 | tf_op jit(solution)/shard_map/ppermute | solution.py:498
  6.8 11.8 %collective-permute-start.1 = (f32[9,33,128]{2,1,0:T(8,128)S(1)}, f32[9,33,128]{2,1,0:T(8,128)S(1)}, u32[]{:S(2)}, u32[]{:S(2)}) collective-permute-start(f32[9,33,128]{2,1,0:T(8,128)S(1)} %get-tuple-element.43), channel_id=1, source_target_pairs={{0,504},{8,0},{16,8},{24,16},{32,24},{40,32},{48,40},{56,48},{64,5... | collective-permute-start | bytes 456200 | tf_op jit(solution)/shard_map/ppermute | solution.py:498
  18.6 0.0 copy-done
  18.6 0.0 copy-done.13
  18.6 0.0 copy-done.14
  18.6 0.0 copy-start.1
  18.6 0.0 copy-start.2
  18.6 0.0 copy-start.6
  18.6 0.0 copy-start.7
  18.6 0.0 copy-start.8
  18.6 0.0 copy-start.9
  18.7 0.0 copy-start.10
  18.7 2.1 %shard_map.291 = (f32[17,40,128]{2,1,0:T(8,128)S(1)}, f32[17,40,128]{2,1,0:T(8,128)S(1)}, f32[17,40,128]{2,1,0:T(8,128)S(1)}, f32[680,256]{1,0:T(8,128)S(1)}, f3...) custom-call(s32[16]{0:T(128)S(1)} %copy-done.17, f32[2,16]{1,0:T(2,128)S(1)} %bitcast.14, f32[17]{0:T(128)S(1)} %copy-done.18, ...), custom_call_target="tpu_custom_call" | custom-call | flops 300000000 | bytes 5000000 | tf_op jit(solution)/shard_map/pallas_call | solution.py:485
  20.8 0.0 collective-permute-done.right_in
  20.8 0.8 %collective-permute-done.1.left_in = f32[9,33,128]{2,1,0:T(8,128)S(1)} collective-permute-done((f32[9,33,128]{2,1,0:T(8,128)S(1)}, f32[9,33,128]{2,1,0:T(8,128)S(1)}, u32[]{:S(2)}, u32[]{:S(2)}) %collective-permute-start.1) | collective-permute-done | bytes 152096 | tf_op jit(solution)/shard_map/ppermute | solution.py:498
  21.6 0.0 copy-done.1
  21.6 0.0 copy-done.2
  21.6 0.0 copy-done.6
  21.6 0.0 copy-done.7
  21.6 0.0 copy-done.8
  21.6 0.0 copy-done.9
  21.6 0.0 copy-done.10
  21.6 5.3 %shard_map.292 = (f32[576,128]{1,0:T(8,128)}, f32[17,33,1,128]{3,2,1,0:T(1,128)}, f32[17,33,1,128]{3,2,1,0:T(1,128)}, f32[17,33,1,128]{3,2,1,0:T(1,128)}, f32[17...) custom-call(s32[1]{0:T(128)S(6)} %copy.32.flip, ...), custom_call_target="tpu_custom_call" | custom-call | flops 600000000 | bytes 6000000 | tf_op jit(solution)/shard_map/pallas_call | solution.py:485
  26.9 7.1 %all-to-all-start = ((f32[8,72,128]{2,1,0:T(8,128)}), f32[8,72,128]{2,1,0:T(8,128)S(1)}, u32[]{:S(2)}, u32[]{:S(2)}) async-start(f32[8,72,128]{2,1,0:T(8,128)} %bitcast.15), calls=%async_computation | async-start | bytes 589824 | tf_op jit(solution)/shard_map/all_to_all | solution.py:545
  34.0 7.3 %all-to-all-done.parts = f32[8,72,128]{2,1,0:T(8,128)S(1)} async-done(((f32[8,72,128]{2,1,0:T(8,128)}), f32[8,72,128]{2,1,0:T(8,128)S(1)}, u32[]{:S(2)}, u32[]{:S(2)}) %all-to-all-start) | async-done | bytes 294944 | tf_op jit(solution)/shard_map/all_to_all | solution.py:545
  41.3 0.0 copy-start.11
  41.3 0.0 copy-start.12
  41.3 2.1 %collective-permute-start.2 = (f32[72,128]{1,0:T(8,128)S(1)}, f32[72,128]{1,0:T(8,128)S(1)}, u32[]{:S(2)}, u32[]{:S(2)}) collective-permute-start(f32[72,128]{1,0:T(8,128)S(1)} %get-tuple-element.51), channel_id=1, source_target_pairs={{0,8},{8,16},{16,24},{24,32},{32,40},{40,48},{48,56},{56,64},{64,7... | collective-permute-start | bytes 110600 | tf_op jit(solution)/shard_map/ppermute | solution.py:498
  43.4 5.8 %collective-permute-start.3 = (f32[72,128]{1,0:T(8,128)S(1)}, f32[72,128]{1,0:T(8,128)S(1)}, u32[]{:S(2)}, u32[]{:S(2)}) collective-permute-start(f32[72,128]{1,0:T(8,128)S(1)} %get-tuple-element.52.own), channel_id=1, source_target_pairs={{0,504},{8,0},{16,8},{24,16},{32,24},{40,32},{48,40},{56,48},{64,5... | collective-permute-start | bytes 110600 | tf_op jit(solution)/shard_map/ppermute | solution.py:498
  49.2 0.0 collective-permute-done.2.before
  49.2 1.6 %collective-permute-done.3.after = f32[72,128]{1,0:T(8,128)S(1)} collective-permute-done((f32[72,128]{1,0:T(8,128)S(1)}, f32[72,128]{1,0:T(8,128)S(1)}, u32[]{:S(2)}, u32[]{:S(2)}) %collective-permute-start.3) | collective-permute-done | bytes 36896 | tf_op jit(solution)/shard_map/ppermute | solution.py:498
  50.8 0.0 copy-done.11
  50.8 0.0 copy-done.12
  50.8 1.0 %shard_map.295 = f32[8,72,128]{2,1,0:T(8,128)} custom-call(s32[1]{0:T(128)S(6)} %copy.32.flip, s32[1]{0:T(128)} %bitcast.9.group, f32[72,128]{1,0:T(8,128)S(1)} %collective-permute-done.2.before, f32[72,128]{1,0:T(8,128)S(1)} %get-tuple-element.52.own, f32[72,128]{1,0:T(8,128)S(1)} %collective-permute-done.3.after, bf16[384,128]{1,0:T(8,128)(2,1)S(1)} %copy-done.11, ...), custom_call_target="tpu_custom_call" | custom-call | tf_op jit(solution)/shard_map/pallas_call | solution.py:485
  51.8 0.0 copy-start.5
  51.8 5.4 %all-to-all-start.1 = ((f32[8,72,128]{2,1,0:T(8,128)}), f32[8,72,128]{2,1,0:T(8,128)S(1)}, u32[]{:S(2)}, u32[]{:S(2)}) async-start(f32[8,72,128]{2,1,0:T(8,128)} %shard_map.295), calls=%async_computation.1 | async-start | bytes 589824 | tf_op jit(solution)/shard_map/all_to_all | solution.py:568
  57.3 0.0 copy-done.5
  57.3 0.0 copy-start.3
  57.3 0.0 copy-start.4
  57.3 0.0 copy-start.15
  57.3 2.0 %shard_map.293 = f32[17,33,1,128]{3,2,1,0:T(1,128)} custom-call(f32[17,40,128]{2,1,0:T(8,128)S(1)} %get-tuple-element.31.b.bn, f32[17,40,128]{2,1,0:T(8,128)S(1)} %get-tuple-element.33.ka, f32[17,40,128]{2,1,0:T(8,128)S(1)} %get-tuple-element.34.c, f32[17,40,128]{2,1,0:T(8,128)S(1)} %get-tuple-element.46.v1b, bf16[680,128]{1,0:T(8,128)(2,1)S(1)} %get-tuple-element.47.u1, ...), custom_call_target="tpu_custom_call" | custom-call | flops 300000000 | bytes 5000000 | tf_op jit(solution)/shard_map/pallas_call | solution.py:485
  59.3 5.1 %all-to-all-done.1 = f32[8,72,128]{2,1,0:T(8,128)S(1)} async-done(((f32[8,72,128]{2,1,0:T(8,128)}), f32[8,72,128]{2,1,0:T(8,128)S(1)}, u32[]{:S(2)}, u32[]{:S(2)}) %all-to-all-start.1) | async-done | bytes 294944 | tf_op jit(solution)/shard_map/all_to_all | solution.py:568
  64.5 0.0 copy-done.3
  64.5 0.0 copy-done.4
  64.5 0.0 copy-done.15
  64.5 1.1 %shard_map.296 = f32[17,33,128]{2,1,0:T(8,128)} custom-call(f32[576,128]{1,0:T(8,128)S(1)} %bitcast.12, bf16[320,256]{1,0:T(8,128)(2,1)S(1)} %copy-done.3, bf16[320,256]{1,0:T(8,128)(2,1)S(1)} %copy-done.4, f32[40,128]{1,0:T(8,128)S(1)} %copy-done.15), custom_call_target="tpu_custom_call" | custom-call | tf_op jit(solution)/shard_map/pallas_call | solution.py:485
  (1 shorter events, 0.0 us)
Async XLA Ops:
  1.3 0.7 %copy-start.18 = (f32[17]{0:T(128)S(1)}, f32[17]{0:T(128)}, u32[]{:S(2)}) copy-start(f32[17]{0:T(128)} %constant.40.clone.iz) | copy-start | bytes 208
  1.3 0.7 %copy-start.19 = (f32[33]{0:T(128)S(1)}, f32[33]{0:T(128)}, u32[]{:S(2)}) copy-start(f32[33]{0:T(128)} %constant.41.clone.iy) | copy-start | bytes 400
  1.3 0.7 %copy-start.16 = (f32[1,2,16]{2,1,0:T(2,128)S(1)}, f32[1,2,16]{2,1,0:T(2,128)}, u32[]{:S(2)}) copy-start(f32[1,2,16]{2,1,0:T(2,128)} %param.35) | copy-start | bytes 388
  1.3 0.7 %copy-start.17 = (s32[16]{0:T(128)S(1)}, s32[16]{0:T(128)}, u32[]{:S(2)}) copy-start(s32[16]{0:T(128)} %index.3) | copy-start | bytes 196
  2.0 16.6 %copy-start = (bf16[256,256]{1,0:T(8,128)(2,1)S(1)}, bf16[256,256]{1,0:T(8,128)(2,1)}, u32[]{:S(2)}) copy-start(bf16[256,256]{1,0:T(8,128)(2,1)} %constant.42.clone.grad) | copy-start | bytes 393220
  2.0 16.6 %copy-start.13 = (bf16[128,256]{1,0:T(8,128)(2,1)S(1)}, bf16[128,256]{1,0:T(8,128)(2,1)}, u32[]{:S(2)}) copy-start(bf16[128,256]{1,0:T(8,128)(2,1)} %constant.43.clone.grad_lo) | copy-start | bytes 196612
  2.0 16.6 %copy-start.14 = (bf16[256,128]{1,0:T(8,128)(2,1)S(1)}, bf16[256,128]{1,0:T(8,128)(2,1)}, u32[]{:S(2)}) copy-start(bf16[256,128]{1,0:T(8,128)(2,1)} %constant.44.clone.pick) | copy-start | bytes 196612
  4.9 15.9 %collective-permute-start = (f32[9,33,128]{2,1,0:T(8,128)S(1)}, f32[9,33,128]{2,1,0:T(8,128)S(1)}, u32[]{:S(2)}, u32[]{:S(2)}) collective-permute-start(f32[9,33,128]{2,1,0:T(8,128)S(1)} %get-tuple-element.42), channel_id=1, source_target_pairs={{0,8},{8,16},{16,24},{24,32},{32,40},{40,48},{48,56},{56,64},{64,7... | collective-permute-start | bytes 456200 | tf_op jit(solution)/shard_map/ppermute | solution.py:498
  6.8 14.8 %collective-permute-start.1 = (f32[9,33,128]{2,1,0:T(8,128)S(1)}, f32[9,33,128]{2,1,0:T(8,128)S(1)}, u32[]{:S(2)}, u32[]{:S(2)}) collective-permute-start(f32[9,33,128]{2,1,0:T(8,128)S(1)} %get-tuple-element.43), channel_id=1, source_target_pairs={{0,504},{8,0},{16,8},{24,16},{32,24},{40,32},{48,40},{56,48},{64,5... | collective-permute-start | bytes 456200 | tf_op jit(solution)/shard_map/ppermute | solution.py:498
  18.6 3.0 %copy-start.1 = (bf16[256,256]{1,0:T(8,128)(2,1)S(1)}, bf16[256,256]{1,0:T(8,128)(2,1)}, u32[]{:S(2)}) copy-start(bf16[256,256]{1,0:T(8,128)(2,1)} %constant.52.clone.t_both) | copy-start | bytes 393220
  18.6 3.0 %copy-start.2 = (bf16[256,640]{1,0:T(8,128)(2,1)S(1)}, bf16[256,640]{1,0:T(8,128)(2,1)}, u32[]{:S(2)}) copy-start(bf16[256,640]{1,0:T(8,128)(2,1)} %constant.45.clone.first) | copy-start | bytes 983044
  18.6 3.0 %copy-start.6 = (bf16[256,256]{1,0:T(8,128)(2,1)S(1)}, bf16[256,256]{1,0:T(8,128)(2,1)}, u32[]{:S(2)}) copy-start(bf16[256,256]{1,0:T(8,128)(2,1)} %constant.46.clone.second_a) | copy-start | bytes 393220
  18.6 3.0 %copy-start.7 = (bf16[256,256]{1,0:T(8,128)(2,1)S(1)}, bf16[256,256]{1,0:T(8,128)(2,1)}, u32[]{:S(2)}) copy-start(bf16[256,256]{1,0:T(8,128)(2,1)} %constant.48.clone.ta_hi) | copy-start | bytes 393220
  18.6 3.0 %copy-start.8 = (bf16[256,256]{1,0:T(8,128)(2,1)S(1)}, bf16[256,256]{1,0:T(8,128)(2,1)}, u32[]{:S(2)}) copy-start(bf16[256,256]{1,0:T(8,128)(2,1)} %constant.49.clone.ta_lo) | copy-start | bytes 393220
  18.6 3.0 %copy-start.9 = (bf16[256,256]{1,0:T(8,128)(2,1)S(1)}, bf16[256,256]{1,0:T(8,128)(2,1)}, u32[]{:S(2)}) copy-start(bf16[256,256]{1,0:T(8,128)(2,1)} %constant.50.clone.tb_hi) | copy-start | bytes 393220
  18.7 3.0 %copy-start.10 = (bf16[256,256]{1,0:T(8,128)(2,1)S(1)}, bf16[256,256]{1,0:T(8,128)(2,1)}, u32[]{:S(2)}) copy-start(bf16[256,256]{1,0:T(8,128)(2,1)} %constant.51.clone.tb_lo) | copy-start | bytes 393220
  26.9 14.4 %all-to-all-start = ((f32[8,72,128]{2,1,0:T(8,128)}), f32[8,72,128]{2,1,0:T(8,128)S(1)}, u32[]{:S(2)}, u32[]{:S(2)}) async-start(f32[8,72,128]{2,1,0:T(8,128)} %bitcast.15), calls=%async_computation | async-start | bytes 589824 | tf_op jit(solution)/shard_map/all_to_all | solution.py:545
  41.3 9.5 %copy-start.11 = (bf16[384,128]{1,0:T(8,128)(2,1)S(1)}, bf16[384,128]{1,0:T(8,128)(2,1)}, u32[]{:S(2)}) copy-start(bf16[384,128]{1,0:T(8,128)(2,1)} %constant.53.clone.gx_hi) | copy-start | bytes 294916
  41.3 9.5 %copy-start.12 = (bf16[384,128]{1,0:T(8,128)(2,1)S(1)}, bf16[384,128]{1,0:T(8,128)(2,1)}, u32[]{:S(2)}) copy-start(bf16[384,128]{1,0:T(8,128)(2,1)} %constant.54.clone.gx_lo) | copy-start | bytes 294916
  41.3 7.8 %collective-permute-start.2 = (f32[72,128]{1,0:T(8,128)S(1)}, f32[72,128]{1,0:T(8,128)S(1)}, u32[]{:S(2)}, u32[]{:S(2)}) collective-permute-start(f32[72,128]{1,0:T(8,128)S(1)} %get-tuple-element.51), channel_id=1, source_target_pairs={{0,8},{8,16},{16,24},{24,32},{32,40},{40,48},{48,56},{56,64},{64,7... | collective-permute-start | bytes 110600 | tf_op jit(solution)/shard_map/ppermute | solution.py:498
  43.4 7.4 %collective-permute-start.3 = (f32[72,128]{1,0:T(8,128)S(1)}, f32[72,128]{1,0:T(8,128)S(1)}, u32[]{:S(2)}, u32[]{:S(2)}) collective-permute-start(f32[72,128]{1,0:T(8,128)S(1)} %get-tuple-element.52.own), channel_id=1, source_target_pairs={{0,504},{8,0},{16,8},{24,16},{32,24},{40,32},{48,40},{56,48},{64,5... | collective-permute-start | bytes 110600 | tf_op jit(solution)/shard_map/ppermute | solution.py:498
  51.8 5.5 %copy-start.5 = (bf16[256,256]{1,0:T(8,128)(2,1)S(1)}, bf16[256,256]{1,0:T(8,128)(2,1)}, u32[]{:S(2)}) copy-start(bf16[256,256]{1,0:T(8,128)(2,1)} %constant.47.clone.second_b) | copy-start | bytes 393220
  51.8 12.7 %all-to-all-start.1 = ((f32[8,72,128]{2,1,0:T(8,128)}), f32[8,72,128]{2,1,0:T(8,128)S(1)}, u32[]{:S(2)}, u32[]{:S(2)}) async-start(f32[8,72,128]{2,1,0:T(8,128)} %shard_map.295), calls=%async_computation.1 | async-start | bytes 589824 | tf_op jit(solution)/shard_map/all_to_all | solution.py:568
  57.3 7.2 %copy-start.3 = (bf16[320,256]{1,0:T(8,128)(2,1)S(1)}, bf16[320,256]{1,0:T(8,128)(2,1)}, u32[]{:S(2)}) copy-start(bf16[320,256]{1,0:T(8,128)(2,1)} %constant.55.clone.blocks_hi) | copy-start | bytes 491524
  57.3 7.2 %copy-start.4 = (bf16[320,256]{1,0:T(8,128)(2,1)S(1)}, bf16[320,256]{1,0:T(8,128)(2,1)}, u32[]{:S(2)}) copy-start(bf16[320,256]{1,0:T(8,128)(2,1)} %constant.56.clone.blocks_lo) | copy-start | bytes 491524
  57.3 7.2 %copy-start.15 = (f32[40,128]{1,0:T(8,128)S(1)}, f32[40,128]{1,0:T(8,128)}, u32[]{:S(2)}) copy-start(f32[40,128]{1,0:T(8,128)} %constant.57.clone.last) | copy-start | bytes 61444

commit v3 on v2

v3 whole, which is shorter than its diff:
```python
import jax
import jax.numpy as jnp
import numpy as np
from jax import lax
from jax.experimental import pallas as pl
from jax.experimental.pallas import tpu as pltpu
from jax.sharding import PartitionSpec as P

DT2 = 0.003
SIGMA_Y = 1.0
ZP, YP, XL = 17, 33, 128
YPAD = 40
ROWS = ZP * YPAD
PLANES, GROUP = 6, 42
KROWS = 576
UNROLL_Y, UNROLL_Z = 17, 4


def gll_tables():
    nodes = np.array([-1.0, -np.sqrt(3.0 / 7.0), 0.0, np.sqrt(3.0 / 7.0), 1.0])
    weights = np.array([0.1, 49.0 / 90.0, 32.0 / 45.0, 49.0 / 90.0, 0.1])
    deriv = np.zeros((5, 5))
    for a in range(5):
        for b in range(5):
            for m in range(5):
                if m == b:
                    continue
                factor = 1.0 / (nodes[b] - nodes[m])
                for k in range(5):
                    if k == b or k == m:
                        continue
                    factor = factor * (nodes[a] - nodes[k]) / (nodes[b] - nodes[k])
                deriv[a, b] += factor
    return weights, deriv


GW, GD = gll_tables()
SHARED = np.array([0.2, GW[1], GW[2], GW[3], 0.2])
APPLY = GW[:, None] * GD
GATHER = (GD / SHARED[None, :]).T


def split(m):
    hi = np.asarray(m, np.float32).astype(jnp.bfloat16)
    lo = (np.asarray(m, np.float32) - hi.astype(np.float32)).astype(jnp.bfloat16)
    return hi, lo


LANE_B, LANE_K, LANE_PA, LANE_CA, LANE_PB, LANE_CB = 8, 16, 21, 25, 29, 33
AFTER = 64


def x_tables():
    def node(e, a):
        if 0 <= e < 32:
            return 4 * e + a if a < 4 else XL + e
        return XL + {-1: 32, -2: 37, 32: 42}[e] + a

    def halo(c):
        return c + 8 if c < 0 else AFTER + c - XL

    grad, edge = np.zeros((XL, 2 * XL)), np.zeros((XL, 2 * XL))
    back = np.zeros((2 * XL, 2 * XL))
    pick, pick_edge = np.zeros((XL, XL)), np.zeros((XL, XL))
    for e in range(-2, 33):
        for a in range(5):
            n = node(e, a)
            for b in range(5):
                c = 4 * e + b
                own = 0 <= c < XL
                (grad if own else edge)[c if own else halo(c), n] += APPLY[a, b]
                if -4 <= c <= XL:
                    back[n, c if own else XL + halo(c)] += GATHER[b, a]
            if n >= XL:
                c = 4 * e + a
                if 0 <= c < XL:
                    pick[c, n - XL] = 1.0
                else:
                    pick_edge[LANE_K + halo(c), n - XL] = 1.0
    return grad, edge, back, pick, pick_edge


def tables():
    grad, edge, back, pick, pick_edge = x_tables()
    g_hi, g_lo = split(grad)
    e_hi, e_lo = split(edge)
    high, low = np.zeros((XL, 5 * XL), jnp.bfloat16), np.zeros((XL, 5 * XL), jnp.bfloat16)
    for m, part in ((high, e_hi), (low, e_lo)):
        m[:, 0 : 2 * XL] = part
        m[:, 2 * XL : 4 * XL] = np.roll(part, LANE_B, 0)
    high[:, 4 * XL :] = pick_edge.astype(jnp.bfloat16)
    second = []
    for at in (0, LANE_B):
        m = np.zeros((XL, 2 * XL), jnp.bfloat16)
        for i, part in enumerate((e_hi, e_hi, e_lo)):
            for lane in (4, 5, 6, 7, AFTER):
                m[16 * i + at + lane] = part[lane]
        second.append(np.concatenate([g_lo, m], 0))
    t_hi, t_lo = split(back)
    moved = [np.roll(t[:, XL:], LANE_B, 1) for t in (t_hi, t_lo)]
    return dict(
        grad=np.concatenate([g_hi] * 2, 0),
        grad_lo=g_lo,
        pick=np.concatenate([pick, pick], 0).astype(jnp.bfloat16),
        first=np.concatenate([high, high], 0),
        first_lo=low,
        second_a=second[0],
        second_b=second[1],
        ta_hi=t_hi,
        ta_lo=t_lo,
        tb_hi=np.concatenate([t_hi[:, :XL], moved[0]], 1),
        tb_lo=np.concatenate([t_lo[:, :XL], moved[1]], 1),
        t_both=np.concatenate([t_hi[:, :XL], t_lo[:, :XL]], 1),
    )


def smoothing_tables():
    offsets = np.arange(3 * XL)[:, None] - XL - np.arange(XL)[None, :]
    sigma_x = XL / 2.0
    gauss_x = np.exp(-0.5 * (offsets / sigma_x) ** 2) * (np.abs(offsets) <= XL)
    normal_x = np.exp(-0.5 * (np.arange(-XL, XL + 1) / sigma_x) ** 2).sum()
    distance = np.arange(YP)[:, None] - np.arange(YP)[None, :]
    gauss_y = np.exp(-0.5 * (distance / SIGMA_Y) ** 2)
    gauss_y = gauss_y / gauss_y.sum(axis=1, keepdims=True)
    return gauss_x / normal_x, gauss_y


def apply5(m, x):
    e0, o0, e1, o1, mid = x[0] + x[4], x[0] - x[4], x[1] + x[3], x[1] - x[3], x[2]
    f = lambda v: np.float32(v)
    odd = [
        f((m[a, 0] + m[a, 4]) / 2) * e0 + f((m[a, 1] + m[a, 3]) / 2) * e1 + f(m[a, 2]) * mid
        for a in (0, 1)
    ]
    even = [
        f((m[a, 0] - m[a, 4]) / 2) * o0 + f((m[a, 1] - m[a, 3]) / 2) * o1 for a in (0, 1, 2)
    ]
    return [even[0] + odd[0], even[1] + odd[1], even[2], even[1] - odd[1], even[0] - odd[0]]


def apply_y(fields, kappa):
    row = lax.broadcasted_iota(jnp.int32, (8, XL), 0)

    def plane(z, carry):
        at = lambda a: pl.ds(a, 8, stride=4)
        k = [kappa[z, at(a), :] for a in range(5)]
        for v, out in fields:
            g = apply5(APPLY, [v[z, at(a), :] for a in range(5)])
            o = apply5(GATHER, [k[a] * g[a] for a in range(5)])
            moved = pltpu.roll(o[4], 1, 0)
            out[z, at(0), :] = jnp.where(row == 0, 2.0 * o[0], o[0] + moved)
            for b in range(1, 4):
                out[z, at(b), :] = o[b]
            out[z, 32:33, :] = 2.0 * moved[0:1]
        return carry

    lax.fori_loop(0, ZP, plane, 0, unroll=UNROLL_Y)


def apply_z(fields, kappa, use):
    def block(rows):
        for i, v in enumerate(fields):
            ends = None
            for e in range(4):
                g = apply5(APPLY, [v[4 * e + a, rows, :] for a in range(5)])
                o = apply5(GATHER, [kappa[4 * e + a, rows, :] * g[a] for a in range(5)])
                use(i, 4 * e, rows, 2.0 * o[0] if e == 0 else o[0] + ends)
                for b in range(1, 4):
                    use(i, 4 * e + b, rows, o[b])
                ends = o[4]
            use(i, 16, rows, 2.0 * ends)

    def step(j, carry):
        block(pl.ds(pl.multiple_of(8 * j, 8), 8))
        return carry

    lax.fori_loop(0, 4, step, 0, unroll=UNROLL_Z)
    block(pl.ds(32, 1))


def inverse_weight(i, last):
    node = i & 3
    end = (i == 0) | (i == last)
    inner = jnp.where(node == 2, np.float32(1.0 / SHARED[2]), np.float32(1.0 / SHARED[1]))
    shared = jnp.where(end, np.float32(2.0 / SHARED[0]), np.float32(1.0 / SHARED[0]))
    return jnp.where(node == 0, shared, inner)


def add_forcing(target, c_ref, index, source, instant):
    lane = lax.broadcasted_iota(jnp.int32, (1, XL), 1)
    node = lane % 4
    inv_x = jnp.where(
        node == 0, 1.0 / SHARED[0], jnp.where(node == 2, 1.0 / SHARED[2], 1.0 / SHARED[1])
    ).astype(jnp.float32)
    for r in range(16):
        point = index[r]
        row = lax.shift_right_logical(point, 7)
        z = lax.shift_right_logical(row * 1986, 16)
        y = row - z * YP
        amount = source[instant, r] * inverse_weight(z, ZP - 1) * inverse_weight(y, YP - 1)
        at = (pl.ds(z, 1), pl.ds(y, 1), slice(None))
        change = jnp.where(lane == (point & (XL - 1)), inv_x * amount, 0.0)
        target[at] = target[at] + c_ref[at] * change[None]


def flip_rows(source, target, flag):
    for y in range(YP):
        to = jnp.where(flag != 0, 32 - y, y)
        target[:, pl.ds(to, 1), :] = source[:, y : y + 1, :]


def pack_edges(a, b, ka, ap, bp, c, f, edges):
    rows = slice(0, YP)
    lane = lax.broadcasted_iota(jnp.int32, (YP, XL), 1)
    first = (0, LANE_B, LANE_K, LANE_PA, LANE_CA, LANE_PB, LANE_CB)
    for i in range(PLANES):
        whole = [None] * len(edges)
        for g in range(3):
            z = PLANES * g + i
            if z >= ZP:
                continue
            av, bv, k, cv = a[z, rows, :], b[z, rows, :], ka[z, rows, :], c[z, rows, :]
            pa = 2.0 * av - ap[z, rows, :] + f[z, rows, :]
            pb = 2.0 * bv - bp[z, rows, :]
            for n, (to_after, _) in enumerate(edges):
                tile = None
                for j, value in reversed(list(enumerate((av, bv, k, pa, cv, pb, cv)))):
                    moved = pltpu.roll(value, first[j] + 8 * to_after + GROUP * g, 1)
                    if tile is None:
                        tile = moved
                    else:
                        above = first[j + 1] + (4 * to_after if j + 1 > 2 else 0)
                        tile = jnp.where(lane < GROUP * g + above, moved, tile)
                whole[n] = tile if g == 0 else jnp.where(lane < GROUP * g, whole[n], tile)
        for n, (_, pack) in enumerate(edges):
            pack[i, :, :] = whole[n]


def pack_kernel(
    flip, odd, an_in, bn_in, ap_in, bp_in, ka_in, de_in, index_in, source_in,
    far_out, near_out, an, bn, ap, bp, ka, c_out, f_out, de, far_pack, near_pack, index, source, sem,
):
    rows = slice(0, YP)
    scalars = []
    for i, (src, dst) in enumerate(((index_in, index), (source_in, source))):
        scalars.append(pltpu.make_async_copy(src, dst, sem.at[6 + i]))
        scalars[-1].start()
    copies = [
        pltpu.make_async_copy(de_in, de.at[:, rows, :], sem.at[0]),
        pltpu.make_async_copy(ka_in, ka.at[:, rows, :], sem.at[1]),
    ]
    for i, (src, dst) in enumerate(((an_in, an), (bn_in, bn), (ap_in, ap), (bp_in, bp))):
        copies.append(pltpu.make_async_copy(src.at[:, :, 0, :], dst.at[:, rows, :], sem.at[2 + i]))
    for copy in copies:
        copy.start()
    f_out[...] = jnp.zeros_like(f_out)
    for copy in scalars:
        copy.wait()
    copies[0].wait()
    for z in range(ZP):
        c_out[z, 0:YP, :] = DT2 / de[z, 0:YP, :]
    add_forcing(f_out, c_out, index, source, 0)
    for copy in copies[1:]:
        copy.wait()
    edges = [(odd[0], far_pack), (1 - odd[0], near_pack)]
    pack_edges(an, bn, ka, ap, bp, c_out, f_out, edges)
    flip_rows(far_pack, far_out, flip[0] * odd[0])
    flip_rows(near_pack, near_out, flip[0] * (1 - odd[0]))


def dot(a, b):
    return jnp.dot(a, b, preferred_element_type=jnp.float32)


def halves(x):
    hi = x.astype(jnp.bfloat16)
    return hi, (x - hi.astype(jnp.float32)).astype(jnp.bfloat16)


def dot3(x, m_hi, m_lo):
    hi, lo = halves(x)
    return dot(hi, m_hi) + dot(lo, m_hi) + dot(hi, m_lo)


def flat(ref):
    return ref[...].reshape(ROWS, ref.shape[-1])


def local_kernel(
    a, b, ka, c, f, grad, grad_lo, pick, index_in, source_in,
    a_out, b_out, f1_out, ga_out, gb_out, kg_out, index, source, sem,
):
    scalars = []
    for i, (src, dst) in enumerate(((index_in, index), (source_in, source))):
        scalars.append(pltpu.make_async_copy(src, dst, sem.at[i]))
        scalars[-1].start()
    apply_y(((a, a_out), (b, b_out)), ka)

    def use(i, z, rows, value):
        out = (a_out, b_out)[i]
        total = c[z, rows, :] * (out[z, rows, :] + value)
        out[z, rows, :] = f[z, rows, :] - total if i == 0 else -total

    apply_z((a, b), ka, use)
    f1_out[...] = jnp.zeros_like(f1_out)
    for copy in scalars:
        copy.wait()
    add_forcing(f1_out, c, index, source, 1)
    for field, out in ((a, ga_out), (b, gb_out)):
        hi, lo = halves(flat(field))
        out[...] = dot(jnp.concatenate([hi, lo], 1), grad[...]) + dot(hi, grad_lo[...])
    hi, lo = halves(flat(ka))
    kg_out[...] = dot(jnp.concatenate([hi, lo], 1), pick[...])


def step_kernel(
    flip, odd, an, ap, bn, bp, ka, c, a0, b0, f1, ga, gb, kg0, far_in, near_in,
    first, first_lo, grad, second_a, ta_hi, ta_lo, tb_hi, tb_lo, t_both,
    k_out, al_out, bl_out, v2a, v1b, u1_out, kg,
    left, raw, u, ku, cu, qu, wa, wb, y1, v1a, k, sem,
):
    lane = lax.broadcasted_iota(jnp.int32, (YP, XL), 1)
    rows = slice(0, YP)
    sent = []

    def send(src, dst, dense):
        if dense:
            src, dst = src.at[:, rows, :], dst.at[:, :, 0, :]
        sent.append(pltpu.make_async_copy(src, dst, sem.at[len(sent)]))
        sent[-1].start()

    is_odd = odd[0] != 0
    raw[...] = jnp.where(is_odd, far_in[...], near_in[...])
    flip_rows(raw, left, flip[0])
    own_a = (lane & 63) < LANE_B
    for z in range(ZP):
        i, at = z % PLANES, GROUP * (z // PLANES)
        before = jnp.where(is_odd, near_in[i], far_in[i])
        if at:
            before = pltpu.roll(before, XL - at, 1)
        tile = jnp.where(lane < AFTER, before, pltpu.roll(left[i], (AFTER - at) % XL, 1))
        u[z, rows, :] = tile
        ku[z, rows, :] = jnp.where(
            own_a, pltpu.roll(tile, XL - LANE_K, 1), pltpu.roll(tile, XL - LANE_K + LANE_B, 1)
        )
        qu[z, rows, :] = pltpu.roll(tile, XL - LANE_PA, 1)
        cu[z, rows, :] = pltpu.roll(tile, XL - LANE_CA, 1)
    apply_y(((u, y1),), ku)

    def use(i, z, rows, value):
        qu[z, rows, :] = qu[z, rows, :] - cu[z, rows, :] * (y1[z, rows, :] + value)

    apply_z((u,), ku, use)

    lane2 = lax.broadcasted_iota(jnp.int32, (ROWS, XL), 1)
    tall = lambda value: value.reshape(ZP, YPAD, value.shape[-1])
    hi, lo = halves(flat(u))
    edge = dot(jnp.concatenate([hi, lo], 1), first[...]) + dot(hi, first_lo[...])
    kg[...] = jnp.concatenate([flat(ka), kg0[...] + edge[:, 4 * XL :]], 1)
    xa = dot3((ga[...] + edge[:, 0 : 2 * XL]) * kg[...], ta_hi[...], ta_lo[...])
    xb = dot3((gb[...] + edge[:, 2 * XL : 4 * XL]) * kg[...], tb_hi[...], tb_lo[...])
    u1 = flat(qu) - flat(cu) * (xa[:, XL:] + xb[:, XL:])
    hi = u1.astype(jnp.bfloat16).astype(jnp.float32)
    packed = jnp.where(
        (lane2 & 63) < 16,
        hi,
        jnp.where((lane2 & 63) < 32, pltpu.roll(u1 - hi, 16, 1), pltpu.roll(hi, 32, 1)),
    ).astype(jnp.bfloat16)
    u1_out[...] = packed
    wa[...] = tall(xa[:, 0:XL])
    wb[...] = tall(xb[:, 0:XL])
    for z in range(ZP):
        cz = c[z, rows, :]
        acc_a = a0[z, rows, :] - cz * wa[z, rows, :]
        acc_b = b0[z, rows, :] - cz * wb[z, rows, :]
        a, b = an[z, rows, :], bn[z, rows, :]
        v1a[z, rows, :] = 2.0 * a - ap[z, rows, :] + acc_a
        v1b[z, rows, :] = 2.0 * b - bp[z, rows, :] + acc_b
        ku[z, rows, :] = b * acc_a
    send(v1a, al_out, True)
    send(v1b, bl_out, True)
    apply_y(((v1a, y1),), ka)

    def add(i, z, rows, value):
        y1[z, rows, :] = y1[z, rows, :] + value

    apply_z((v1a,), ka, add)
    wa[...] = tall(second_x(v1a, packed, grad, second_a, kg, t_both))
    for i in (6, 7):
        k[72 * i + 64 : 72 * i + 72, :] = jnp.zeros((8, XL), jnp.float32)
    for z in (ZP - 1, *range(ZP - 1)):
        acc_a = f1[z, rows, :] - c[z, rows, :] * (wa[z, rows, :] + y1[z, rows, :])
        v2a[z, rows, :] = 2.0 * v1a[z, rows, :] - an[z, rows, :] + acc_a
        t = ku[z, rows, :] + v1b[z, rows, :] * acc_a
        if z < ZP - 1:
            at = 72 * (z // 2) + 32 * (z % 2)
            k[at : at + 8, :] = t[0:8]
            k[at + 8 : at + 16, :] = t[25:33]
            k[at + 16 : at + 24, :] = t[8:16]
            k[at + 24 : at + 32, :] = t[17:25]
        else:
            for i in range(4):
                at = 72 * i + 64
                k[at : at + 4, :] = t[4 * i : 4 * i + 4]
                k[at + 4 : at + 8, :] = t[29 - 4 * i : 33 - 4 * i]
        at = 72 * (4 + z // 8) + 64 + z % 8
        k[at : at + 1, :] = t[16:17]
        for j in {1: [0], 3: [1], 5: [2], 7: [3], 9: [4], 13: [6], 15: [5, 7]}.get(z, []):
            at = pl.ds(72 * j, 72)
            send(k.at[at], k_out.at[at], False)
    for copy in sent:
        copy.wait()


def second_x(v, packed, grad, second, kg, t_both):
    hi, lo = halves(flat(v))
    g = dot(jnp.concatenate([hi, lo], 1), grad[...])
    g = g + dot(jnp.concatenate([hi, packed], 1), second[...])
    hi, lo = halves(g * kg[...])
    both = dot(hi, t_both[...])
    return both[:, 0:XL] + both[:, XL:] + dot(lo, t_both[:, 0:XL])


def last_kernel(bn, ka, c, v1b, v2a, u1, kg, grad, second_b, t_both, af_out, bf_out, y1, wb, sem):
    rows = slice(0, YP)
    first = pltpu.make_async_copy(v2a.at[:, rows, :], af_out.at[:, :, 0, :], sem.at[1])
    first.start()
    apply_y(((v1b, y1),), ka)

    def add(i, z, rows, value):
        y1[z, rows, :] = y1[z, rows, :] + value

    apply_z((v1b,), ka, add)
    x = second_x(v1b, u1[...], grad, second_b, kg, t_both)
    wb[...] = x.reshape(ZP, YPAD, XL)
    for z in range(ZP):
        acc = c[z, rows, :] * (wb[z, rows, :] + y1[z, rows, :])
        wb[z, rows, :] = 2.0 * v1b[z, rows, :] - bn[z, rows, :] - acc
    copy = pltpu.make_async_copy(wb.at[:, rows, :], bf_out.at[:, :, 0, :], sem.at[0])
    copy.start()
    first.wait()
    copy.wait()


def turn(part, whole, flipped):
    for i in range(part // 72):
        for r in range(8):
            for j in range(9):
                at = 72 * i + 8 * (j ^ 1 if j < 8 else j) + 7 - r
                flipped[72 * i + 8 * j + r : 72 * i + 8 * j + r + 1, :] = whole[at : at + 1, :]


def turned_part(group, value, flipped):
    row = lax.broadcasted_iota(jnp.int32, value.shape, 0)
    stays = (row % 72 >= 64) & (row // 72 + group[0] * (value.shape[0] // 72) >= 4)
    return jnp.where(stays, value, flipped[...])


def sum_kernel(flip, group, odd, parts, far_out, near_out, own_out, flipped):
    total = parts[0]
    for i in range(1, parts.shape[0]):
        total = total + parts[i]
    own_out[...] = total
    turn(total.shape[0], own_out, flipped)
    other = turned_part(group, total, flipped)
    turned = flip[0] != 0
    far_out[...] = jnp.where(turned & (odd[0] != 0), other, total)
    near_out[...] = jnp.where(turned & (odd[0] == 0), other, total)


def smooth_kernel(flip, group, odd, far_in, own, near_in, gx_hi, gx_lo, out, done, flipped, sem):
    is_odd = odd[0] != 0
    before = jnp.where(is_odd, near_in[...], far_in[...])
    after = jnp.where(is_odd, far_in[...], near_in[...])
    done[...] = after
    turn(after.shape[0], done, flipped)
    after = jnp.where(flip[0] != 0, turned_part(group, after, flipped), after)
    total = None
    for i, part in enumerate((before, own[...], after)):
        at = slice(XL * i, XL * (i + 1))
        one = dot3(part, gx_hi[at, :], gx_lo[at, :])
        total = one if total is None else total + one
    done[...] = total
    copies = [pltpu.make_async_copy(done, out.at[i], sem.at[i]) for i in range(out.shape[0])]
    for copy in copies:
        copy.start()
    for copy in copies:
        copy.wait()


def finish_kernel(t, blocks_hi, blocks_lo, end_hi, end_lo, middle, out, rows, done_all, sem):
    def planes(first, n, m_hi, m_lo):
        if n > 1:
            for i in range(n):
                at = 72 * ((first + i) // 2) + 32 * (i % 2)
                rows[32 * i : 32 * i + 32, :] = t[at : at + 32, :]
        else:
            for i in range(4):
                rows[8 * i : 8 * i + 8, :] = t[72 * i + 64 : 72 * i + 72, :]
        hi, lo = halves(rows[0 : 32 * n, :])
        done = dot(m_hi[...], hi) + dot(m_hi[...], lo) + dot(m_lo[...], hi)
        for i in range(n):
            z = first + i
            at = 72 * (4 + z // 8) + 64 + z % 8
            done_all[z] = done[i * YPAD : (i + 1) * YPAD] + middle[...] * t[at : at + 1, :]
        at = pl.ds(first, n)
        copy = pltpu.make_async_copy(done_all.at[at, 0:YP, :], out.at[at], sem.at[first // 8])
        copy.start()
        return copy

    copies = [planes(0, 8, blocks_hi, blocks_lo), planes(8, 8, blocks_hi, blocks_lo), planes(16, 1, end_hi, end_lo)]
    for copy in copies:
        copy.wait()


SMEM_SPEC = pl.BlockSpec(memory_space=pltpu.SMEM)
VMEM_SPEC = pl.BlockSpec(memory_space=pltpu.VMEM)
ANY_SPEC = pl.BlockSpec(memory_space=pl.ANY)


def near(*shape, dtype=jnp.float32):
    return pltpu.VMEM(shape, dtype)


def distant(*shape, dtype=jnp.float32):
    return pltpu.HBM(shape, dtype)


def call(kernel, outs, scalars, arrays, scratch=(), far=(), flops=0, moved=0, limit=24):
    far = [pltpu.with_memory_space_constraint(v, pltpu.HBM) for v in far]
    out_specs = [ANY_SPEC if o.memory_space == pltpu.HBM else VMEM_SPEC for o in outs]
    return pl.pallas_call(
        kernel,
        out_shape=outs,
        in_specs=[SMEM_SPEC] * len(scalars) + [VMEM_SPEC] * len(arrays) + [ANY_SPEC] * len(far),
        out_specs=out_specs,
        scratch_shapes=list(scratch),
        compiler_params=pltpu.CompilerParams(vmem_limit_bytes=limit * 1024 * 1024),
        cost_estimate=pl.CostEstimate(flops=flops, bytes_accessed=moved, transcendentals=0),
    )(*scalars, *arrays, *far)


def swap(value, odd):
    n = lax.axis_size("cuts")
    return lax.ppermute(value, "cuts", [(i, (i + 1 if i % 2 == odd else i - 1) % n) for i in range(n)])


def local(an, ap, bn, bp, kappa, density, flip, index, source):
    dense, padded, edge = distant(ZP, YP, 1, XL), near(ZP, YPAD, XL), near(PLANES, YP, XL)
    odd = (lax.axis_index("cuts").astype(jnp.int32) % 2).reshape(1)
    src = source[0]
    tab = {name: jnp.asarray(value) for name, value in tables().items()}
    fields = [v.reshape(ZP, YP, 1, XL) for v in (an, bn, ap, bp)]
    dma = pltpu.SemaphoreType.DMA
    receivers = [pltpu.SMEM(v.shape, v.dtype) for v in (index, src)]
    to_far, to_near, an, bn, ap, bp, ka, c, f0 = call(
        pack_kernel,
        [edge, edge] + [padded] * 7,
        [flip, odd],
        [],
        [padded, edge, edge, *receivers, dma((8,))],
        far=[*fields, kappa, density, index, src],
        moved=4_000_000,
    )
    from_far = swap(to_far, 1)
    wide, narrow = near(ROWS, 2 * XL), near(ROWS, XL)
    from_near = swap(to_near, 0)
    a0, b0, f1, ga, gb, kg0 = call(
        local_kernel,
        [padded, padded, padded, wide, wide, narrow],
        [],
        [an, bn, ka, c, f0, tab["grad"], tab["grad_lo"], tab["pick"]],
        [*receivers, dma((2,))],
        far=[index, src],
        flops=300_000_000,
        moved=5_000_000,
    )
    packed = near(ROWS, XL, dtype=jnp.bfloat16)
    k, al, bl, v2a, v1b, u1, kg = call(
        step_kernel,
        [distant(KROWS, XL), dense, dense, padded, padded, packed, wide],
        [flip, odd],
        [an, ap, bn, bp, ka, c, a0, b0, f1, ga, gb, kg0, from_far, from_near]
        + [tab[n] for n in ("first", "first_lo", "grad", "second_a", "ta_hi", "ta_lo", "tb_hi", "tb_lo", "t_both")],
        [edge, edge] + [padded] * 8 + [near(KROWS, XL), dma((10,))],
        flops=600_000_000,
        moved=6_000_000,
    )
    groups = lax.axis_size("event")
    part = KROWS // groups
    parts = lax.all_to_all(k.reshape(groups, part, XL), "event", 0, 0)
    af, bf = call(
        last_kernel,
        [dense, dense],
        [],
        [bn, ka, c, v1b, v2a, u1, kg, tab["grad"], tab["second_b"], tab["t_both"]],
        [padded, padded, dma((2,))],
        flops=300_000_000,
        moved=5_000_000,
    )
    outs = (af, al, bf, bl)
    group = lax.axis_index("event").astype(jnp.int32).reshape(1)
    place = [flip, group, odd]
    to_far, to_near, total = call(sum_kernel, [near(part, XL)] * 3, place, [parts], [near(part, XL)])
    from_near = swap(to_near, 0)
    from_far = swap(to_far, 1)
    gauss_x, gauss_y = smoothing_tables()
    gauss = [jnp.asarray(v) for v in split(gauss_x)]
    spread = call(
        smooth_kernel,
        [distant(groups, part, XL)],
        place,
        [from_far, total, from_near, *gauss],
        [near(part, XL), near(part, XL), dma((8,))],
    )[0]
    whole = lax.all_to_all(spread, "event", 0, 0).reshape(KROWS, XL)
    order = [*range(0, 8), *range(25, 33), *range(8, 16), *range(17, 25)]
    blocks, end, middle = np.zeros((8 * YPAD, 256)), np.zeros((YPAD, 32)), np.zeros((YPAD, XL))
    for i in range(8):
        blocks[i * YPAD : i * YPAD + YP, i * 32 : i * 32 + 32] = gauss_y[:, order]
    end[0:YP] = gauss_y[:, [y for i in range(0, 16, 4) for y in (*range(i, i + 4), *range(29 - i, 33 - i))]]
    middle[0:YP] = gauss_y[:, 16:17]
    smoothed = call(
        finish_kernel,
        [distant(ZP, YP, XL)],
        [],
        [whole, *(jnp.asarray(v) for v in (*split(blocks), *split(end))), jnp.asarray(middle, jnp.float32)],
        [near(256, XL), near(ZP, YPAD, XL), dma((3,))],
    )[0]
    return *(v.reshape(1, ZP, YP, XL) for v in outs), smoothed


def solution(mesh):
    field = P("event", None, None, "cuts")
    grid = P(None, None, "cuts")
    return jax.shard_map(
        local,
        mesh=mesh,
        in_specs=(field,) * 4 + (grid, grid, P("cuts"), P("cuts"), P("event", None, "cuts")),
        out_specs=(field,) * 4 + (grid,),
        check_vma=False,
    )
```

time: 66.1 us -> 61.8 us (0.935)
  starting transfers between devices: 34 us -> 30.4 us
  Pallas kernels: 14.4 us -> 12.4 us
  waiting for transfers between devices: 14.9 us -> 15.9 us
    ppermute x4, starting transfers between devices: 21.5 us -> 18 us  [swap(): lax.ppermute(value, 'cuts', [(i, (i + 1 if i % 2 == odd else i - 1) % n)...]
    pallas_call x7, Pallas kernels: 14.4 us -> 12.4 us  [call(): pl.pallas_call(kernel, out_shape=outs, in_specs=[SMEM_SPEC] * len(scalars...]
    all_to_all x1, waiting for transfers between devices: 7.31 us -> 8.25 us  [local(): parts = lax.all_to_all(k.reshape(groups, part, XL), 'event', 0, 0)]
    ppermute x4, waiting for transfers between devices: 2.43 us -> 3.17 us  [swap(): lax.ppermute(value, 'cuts', [(i, (i + 1 if i % 2 == odd else i - 1) % n)...]
  transfers between devices with their start and end apart: 6 -> 6, of which waited for: 4 -> 3; matrix products, arithmetic and copies ran while one was open for 0% -> 0% of each run, Pallas kernels for 6% -> 5%
where the time goes in v3:
time: 61.8 us; the launch traced here: 61.3 us
  starting transfers between devices  30.4 us (49%)
  waiting for transfers between devices  15.9 us (26%)
  Pallas kernels  12.4 us (20%)
  between operations  1.6 us (3%)
  local copies, waits for them, and re-layouts  1.01 us (2%)
    ppermute x4, starting transfers between devices, swap(): lax.ppermute(value, 'cuts', [(i, (i + 1 if i % 2 == odd else i - 1) % n)...  18 us
    pallas_call x7, Pallas kernels, call(): pl.pallas_call(kernel, out_shape=outs, in_specs=[SMEM_SPEC] * len(scalars...  12.4 us
    all_to_all x1, waiting for transfers between devices, local(): parts = lax.all_to_all(k.reshape(groups, part, XL), 'event', 0, 0)  8.25 us
    all_to_all x1, starting transfers between devices, local(): parts = lax.all_to_all(k.reshape(groups, part, XL), 'event', 0, 0)  7.09 us
    all_to_all x1, starting transfers between devices, local(): whole = lax.all_to_all(spread, 'event', 0, 0).reshape(KROWS, XL)  5.28 us
    all_to_all x1, waiting for transfers between devices, local(): whole = lax.all_to_all(spread, 'event', 0, 0).reshape(KROWS, XL)  4.49 us
    ppermute x4, waiting for transfers between devices, swap(): lax.ppermute(value, 'cuts', [(i, (i + 1 if i % 2 == odd else i - 1) % n)...  3.17 us
  transfers between devices with their start and end apart: 6, of which 3 were waited for; matrix products, arithmetic and copies ran while one was open for 0% of the time, Pallas kernels for 5%

profile of v3, /device:TPU:8, one launch (start us, length us, event | category | flops | bytes accessed | tf_op | source)
XLA Modules:
  0.0 61.3 jit_solution(18147859207530271577)
XLA Ops:
  1.3 0.0 copy-start
  1.3 0.0 copy-start.14
  1.3 0.0 copy-start.15
  1.3 3.0 %shard_map.299 = (f32[6,33,128]{2,1,0:T(8,128)S(1)}, f32[6,33,128]{2,1,0:T(8,128)S(1)}, f32[17,40,128]{2,1,0:T(8,128)S(1)}, f32[17,40,128]{2,1,0:T(8,128)S(1)}, ...) custom-call(s32[1]{0:T(128)S(6)} %copy.33.flip, ...), custom_call_target="tpu_custom_call" | custom-call | bytes 4000000 | tf_op jit(solution)/shard_map/pallas_call | solution.py:532
  4.4 11.8 %collective-permute-start = (f32[6,33,128]{2,1,0:T(8,128)S(1)}, f32[6,33,128]{2,1,0:T(8,128)S(1)}, u32[]{:S(2)}, u32[]{:S(2)}) collective-permute-start(f32[6,33,128]{2,1,0:T(8,128)S(1)} %get-tuple-element.45), channel_id=1, source_target_pairs={{0,504},{8,16},{16,8},{24,32},{32,24},{40,48},{48,40},{56,64},{64,... | collective-permute-start | bytes 304136 | tf_op jit(solution)/shard_map/ppermute | solution.py:545
  16.1 1.9 %collective-permute-start.1 = (f32[6,33,128]{2,1,0:T(8,128)S(1)}, f32[6,33,128]{2,1,0:T(8,128)S(1)}, u32[]{:S(2)}, u32[]{:S(2)}) collective-permute-start(f32[6,33,128]{2,1,0:T(8,128)S(1)} %get-tuple-element.46), channel_id=1, source_target_pairs={{0,8},{8,0},{16,24},{24,16},{32,40},{40,32},{48,56},{56,48},{64,72... | collective-permute-start | bytes 304136 | tf_op jit(solution)/shard_map/ppermute | solution.py:545
  18.1 0.0 copy-done
  18.1 0.0 copy-done.14
  18.1 0.0 copy-done.15
  18.1 0.0 copy-start.1
  18.1 0.0 copy-start.2
  18.1 0.0 copy-start.3
  18.1 0.0 copy-start.7
  18.2 0.0 copy-start.8
  18.2 0.0 copy-start.9
  18.2 0.0 copy-start.10
  18.2 0.0 copy-start.11
  18.2 1.5 %shard_map.300 = (f32[17,40,128]{2,1,0:T(8,128)S(1)}, f32[17,40,128]{2,1,0:T(8,128)S(1)}, f32[17,40,128]{2,1,0:T(8,128)S(1)}, f32[680,256]{1,0:T(8,128)S(1)}, f3...) custom-call(f32[17,40,128]{2,1,0:T(8,128)S(1)} %get-tuple-element.35.a.an, f32[17,40,128]{2,1,0:T(8,128)S(1)} %get-tuple-element.32.b.bn, ...), custom_call_target="tpu_custom_call" | custom-call | flops 300000000 | bytes 5000000 | tf_op jit(solution)/shard_map/pallas_call | solution.py:532
  19.7 0.0 collective-permute-done.far_in
  19.7 0.0 collective-permute-done.1.near_in
  19.7 0.0 copy-done.1
  19.7 0.0 copy-done.2
  19.7 0.0 copy-done.3
  19.7 0.0 copy-done.7
  19.8 0.0 copy-done.8
  19.8 0.0 copy-done.9
  19.8 0.0 copy-done.10
  19.8 0.0 copy-done.11
  19.8 3.9 %shard_map.301 = (f32[576,128]{1,0:T(8,128)}, f32[17,33,1,128]{3,2,1,0:T(1,128)}, f32[17,33,1,128]{3,2,1,0:T(1,128)}, f32[17,40,128]{2,1,0:T(8,128)S(1)}, f32[17...) custom-call(s32[1]{0:T(128)S(6)} %copy.33.flip, s32[1]{0:T(128)} %bitcast.odd, ...), custom_call_target="tpu_custom_call" | custom-call | flops 600000000 | bytes 6000000 | tf_op jit(solution)/shard_map/pallas_call | solution.py:532
  23.7 7.1 %all-to-all-start = ((f32[8,72,128]{2,1,0:T(8,128)}), f32[8,72,128]{2,1,0:T(8,128)S(1)}, u32[]{:S(2)}, u32[]{:S(2)}) async-start(f32[8,72,128]{2,1,0:T(8,128)} %bitcast.14), calls=%async_computation | async-start | bytes 589824 | tf_op jit(solution)/shard_map/all_to_all | solution.py:591
  30.8 8.2 %all-to-all-done.parts = f32[8,72,128]{2,1,0:T(8,128)S(1)} async-done(((f32[8,72,128]{2,1,0:T(8,128)}), f32[8,72,128]{2,1,0:T(8,128)S(1)}, u32[]{:S(2)}, u32[]{:S(2)}) %all-to-all-start) | async-done | bytes 294944 | tf_op jit(solution)/shard_map/all_to_all | solution.py:591
  39.0 0.0 copy-start.12
  39.0 0.0 copy-start.13
  39.0 0.1 shard_map.303
  39.1 2.4 %collective-permute-start.2 = (f32[72,128]{1,0:T(8,128)S(1)}, f32[72,128]{1,0:T(8,128)S(1)}, u32[]{:S(2)}, u32[]{:S(2)}) collective-permute-start(f32[72,128]{1,0:T(8,128)S(1)} %get-tuple-element.56), channel_id=1, source_target_pairs={{0,504},{8,16},{16,8},{24,32},{32,24},{40,48},{48,40},{56,64},{64,... | collective-permute-start | bytes 110600 | tf_op jit(solution)/shard_map/ppermute | solution.py:545
  41.5 1.9 %collective-permute-start.3 = (f32[72,128]{1,0:T(8,128)S(1)}, f32[72,128]{1,0:T(8,128)S(1)}, u32[]{:S(2)}, u32[]{:S(2)}) collective-permute-start(f32[72,128]{1,0:T(8,128)S(1)} %get-tuple-element.58), channel_id=1, source_target_pairs={{0,8},{8,0},{16,24},{24,16},{32,40},{40,32},{48,56},{56,48},{64,72... | collective-permute-start | bytes 110600 | tf_op jit(solution)/shard_map/ppermute | solution.py:545
  43.5 3.2 %collective-permute-done.2.far_in = f32[72,128]{1,0:T(8,128)S(1)} collective-permute-done((f32[72,128]{1,0:T(8,128)S(1)}, f32[72,128]{1,0:T(8,128)S(1)}, u32[]{:S(2)}, u32[]{:S(2)}) %collective-permute-start.2) | collective-permute-done | bytes 36896 | tf_op jit(solution)/shard_map/ppermute | solution.py:545
  46.6 0.0 collective-permute-done.3.near_in
  46.6 0.0 copy-done.12
  46.6 0.0 copy-done.13
  46.6 1.0 %shard_map.304 = f32[8,72,128]{2,1,0:T(8,128)} custom-call(s32[1]{0:T(128)S(6)} %copy.33.flip, s32[1]{0:T(128)} %bitcast.10.group, s32[1]{0:T(128)} %bitcast.odd, f32[72,128]{1,0:T(8,128)S(1)} %collective-permute-done.2.far_in, f32[72,128]{1,0:T(8,128)S(1)} %get-tuple-element.57.own, f32[72,128]{1,0:T(8,128)S(1)} %collective-permute-done.3.near_in, ...), custom_call_target="tpu_custom_call" | custom-call | tf_op jit(solution)/shard_map/pallas_call | solution.py:532
  47.7 5.3 %all-to-all-start.1 = ((f32[8,72,128]{2,1,0:T(8,128)}), f32[8,72,128]{2,1,0:T(8,128)S(1)}, u32[]{:S(2)}, u32[]{:S(2)}) async-start(f32[8,72,128]{2,1,0:T(8,128)} %shard_map.304), calls=%async_computation.1 | async-start | bytes 589824 | tf_op jit(solution)/shard_map/all_to_all | solution.py:616
  52.9 0.0 copy-start.6
  52.9 0.9 %copy-done.6 = bf16[256,256]{1,0:T(8,128)(2,1)S(1)} copy-done((bf16[256,256]{1,0:T(8,128)(2,1)S(1)}, bf16[256,256]{1,0:T(8,128)(2,1)}, u32[]{:S(2)}) %copy-start.6) | copy-done | bytes 131096
  53.8 0.0 copy-start.4
  53.8 0.0 copy-start.5
  53.9 0.0 copy-start.16
  53.9 0.0 copy-start.17
  53.9 0.0 copy-start.18
  53.9 1.8 %shard_map.302 = (f32[17,33,1,128]{3,2,1,0:T(1,128)}, f32[17,33,1,128]{3,2,1,0:T(1,128)}) custom-call(f32[17,40,128]{2,1,0:T(8,128)S(1)} %get-tuple-element.32.b.bn, f32[17,40,128]{2,1,0:T(8,128)S(1)} %get-tuple-element.33.ka, f32[17,40,128]{2,1,0:T(8,128)S(1)} %get-tuple-element.34.c, f32[17,40,128]{2,1,0:T(8,128)S(1)} %get-tuple-element.47.v1b, ...), custom_call_target="tpu_custom_call" | custom-call | flops 300000000 | bytes 5000000 | tf_op jit(solution)/shard_map/pallas_call | solution.py:532
  55.7 4.5 %all-to-all-done.1 = f32[8,72,128]{2,1,0:T(8,128)S(1)} async-done(((f32[8,72,128]{2,1,0:T(8,128)}), f32[8,72,128]{2,1,0:T(8,128)S(1)}, u32[]{:S(2)}, u32[]{:S(2)}) %all-to-all-start.1) | async-done | bytes 294944 | tf_op jit(solution)/shard_map/all_to_all | solution.py:616
  60.2 0.0 copy-done.4
  60.2 0.0 copy-done.5
  60.2 0.0 copy-done.16
  60.2 0.0 copy-done.17
  60.2 0.0 copy-done.18
  60.2 1.1 %shard_map.305 = f32[17,33,128]{2,1,0:T(8,128)} custom-call(f32[576,128]{1,0:T(8,128)S(1)} %bitcast.13, bf16[320,256]{1,0:T(8,128)(2,1)S(1)} %copy-done.5, bf16[320,256]{1,0:T(8,128)(2,1)S(1)} %copy-done.4, bf16[40,32]{1,0:T(8,128)(2,1)S(1)} %copy-done.18, bf16[40,32]{1,0:T(8,128)(2,1)S(1)} %copy-done.17, f32[40,128]{1,0:T(8,128)S(1)} %copy-done.16), custom_call_target="tpu_custom_call" | custom-call | tf_op jit(solution)/shard_map/pallas_call | solution.py:532
Async XLA Ops:
  1.3 16.8 %copy-start = (bf16[256,256]{1,0:T(8,128)(2,1)S(1)}, bf16[256,256]{1,0:T(8,128)(2,1)}, u32[]{:S(2)}) copy-start(bf16[256,256]{1,0:T(8,128)(2,1)} %constant.60.clone.grad) | copy-start | bytes 393220
  1.3 16.8 %copy-start.14 = (bf16[256,128]{1,0:T(8,128)(2,1)S(1)}, bf16[256,128]{1,0:T(8,128)(2,1)}, u32[]{:S(2)}) copy-start(bf16[256,128]{1,0:T(8,128)(2,1)} %constant.62.clone.pick) | copy-start | bytes 196612
  1.3 16.8 %copy-start.15 = (bf16[128,256]{1,0:T(8,128)(2,1)S(1)}, bf16[128,256]{1,0:T(8,128)(2,1)}, u32[]{:S(2)}) copy-start(bf16[128,256]{1,0:T(8,128)(2,1)} %constant.61.clone.grad_lo) | copy-start | bytes 196612
  4.4 15.3 %collective-permute-start = (f32[6,33,128]{2,1,0:T(8,128)S(1)}, f32[6,33,128]{2,1,0:T(8,128)S(1)}, u32[]{:S(2)}, u32[]{:S(2)}) collective-permute-start(f32[6,33,128]{2,1,0:T(8,128)S(1)} %get-tuple-element.45), channel_id=1, source_target_pairs={{0,504},{8,16},{16,8},{24,32},{32,24},{40,48},{48,40},{56,64},{64,... | collective-permute-start | bytes 304136 | tf_op jit(solution)/shard_map/ppermute | solution.py:545
  16.1 3.6 %collective-permute-start.1 = (f32[6,33,128]{2,1,0:T(8,128)S(1)}, f32[6,33,128]{2,1,0:T(8,128)S(1)}, u32[]{:S(2)}, u32[]{:S(2)}) collective-permute-start(f32[6,33,128]{2,1,0:T(8,128)S(1)} %get-tuple-element.46), channel_id=1, source_target_pairs={{0,8},{8,0},{16,24},{24,16},{32,40},{40,32},{48,56},{56,48},{64,72... | collective-permute-start | bytes 304136 | tf_op jit(solution)/shard_map/ppermute | solution.py:545
  18.1 1.6 %copy-start.1 = (bf16[256,256]{1,0:T(8,128)(2,1)S(1)}, bf16[256,256]{1,0:T(8,128)(2,1)}, u32[]{:S(2)}) copy-start(bf16[256,256]{1,0:T(8,128)(2,1)} %constant.71.clone.t_both) | copy-start | bytes 393220
  18.1 1.6 %copy-start.2 = (bf16[256,640]{1,0:T(8,128)(2,1)S(1)}, bf16[256,640]{1,0:T(8,128)(2,1)}, u32[]{:S(2)}) copy-start(bf16[256,640]{1,0:T(8,128)(2,1)} %constant.63.clone.first) | copy-start | bytes 983044
  18.1 1.6 %copy-start.3 = (bf16[128,640]{1,0:T(8,128)(2,1)S(1)}, bf16[128,640]{1,0:T(8,128)(2,1)}, u32[]{:S(2)}) copy-start(bf16[128,640]{1,0:T(8,128)(2,1)} %constant.64.clone.first_lo) | copy-start | bytes 491524
  18.1 1.6 %copy-start.7 = (bf16[256,256]{1,0:T(8,128)(2,1)S(1)}, bf16[256,256]{1,0:T(8,128)(2,1)}, u32[]{:S(2)}) copy-start(bf16[256,256]{1,0:T(8,128)(2,1)} %constant.70.clone.tb_lo) | copy-start | bytes 393220
  18.2 1.6 %copy-start.8 = (bf16[256,256]{1,0:T(8,128)(2,1)S(1)}, bf16[256,256]{1,0:T(8,128)(2,1)}, u32[]{:S(2)}) copy-start(bf16[256,256]{1,0:T(8,128)(2,1)} %constant.69.clone.tb_hi) | copy-start | bytes 393220
  18.2 1.6 %copy-start.9 = (bf16[256,256]{1,0:T(8,128)(2,1)S(1)}, bf16[256,256]{1,0:T(8,128)(2,1)}, u32[]{:S(2)}) copy-start(bf16[256,256]{1,0:T(8,128)(2,1)} %constant.68.clone.ta_lo) | copy-start | bytes 393220
  18.2 1.6 %copy-start.10 = (bf16[256,256]{1,0:T(8,128)(2,1)S(1)}, bf16[256,256]{1,0:T(8,128)(2,1)}, u32[]{:S(2)}) copy-start(bf16[256,256]{1,0:T(8,128)(2,1)} %constant.67.clone.ta_hi) | copy-start | bytes 393220
  18.2 1.6 %copy-start.11 = (bf16[256,256]{1,0:T(8,128)(2,1)S(1)}, bf16[256,256]{1,0:T(8,128)(2,1)}, u32[]{:S(2)}) copy-start(bf16[256,256]{1,0:T(8,128)(2,1)} %constant.65.clone.second_a) | copy-start | bytes 393220
  23.7 15.3 %all-to-all-start = ((f32[8,72,128]{2,1,0:T(8,128)}), f32[8,72,128]{2,1,0:T(8,128)S(1)}, u32[]{:S(2)}, u32[]{:S(2)}) async-start(f32[8,72,128]{2,1,0:T(8,128)} %bitcast.14), calls=%async_computation | async-start | bytes 589824 | tf_op jit(solution)/shard_map/all_to_all | solution.py:591
  39.0 7.6 %copy-start.12 = (bf16[384,128]{1,0:T(8,128)(2,1)S(1)}, bf16[384,128]{1,0:T(8,128)(2,1)}, u32[]{:S(2)}) copy-start(bf16[384,128]{1,0:T(8,128)(2,1)} %constant.73.clone.gx_lo) | copy-start | bytes 294916
  39.0 7.6 %copy-start.13 = (bf16[384,128]{1,0:T(8,128)(2,1)S(1)}, bf16[384,128]{1,0:T(8,128)(2,1)}, u32[]{:S(2)}) copy-start(bf16[384,128]{1,0:T(8,128)(2,1)} %constant.72.clone.gx_hi) | copy-start | bytes 294916
  39.1 7.5 %collective-permute-start.2 = (f32[72,128]{1,0:T(8,128)S(1)}, f32[72,128]{1,0:T(8,128)S(1)}, u32[]{:S(2)}, u32[]{:S(2)}) collective-permute-start(f32[72,128]{1,0:T(8,128)S(1)} %get-tuple-element.56), channel_id=1, source_target_pairs={{0,504},{8,16},{16,8},{24,32},{32,24},{40,48},{48,40},{56,64},{64,... | collective-permute-start | bytes 110600 | tf_op jit(solution)/shard_map/ppermute | solution.py:545
  41.5 5.1 %collective-permute-start.3 = (f32[72,128]{1,0:T(8,128)S(1)}, f32[72,128]{1,0:T(8,128)S(1)}, u32[]{:S(2)}, u32[]{:S(2)}) collective-permute-start(f32[72,128]{1,0:T(8,128)S(1)} %get-tuple-element.58), channel_id=1, source_target_pairs={{0,8},{8,0},{16,24},{24,16},{32,40},{40,32},{48,56},{56,48},{64,72... | collective-permute-start | bytes 110600 | tf_op jit(solution)/shard_map/ppermute | solution.py:545
  47.7 12.5 %all-to-all-start.1 = ((f32[8,72,128]{2,1,0:T(8,128)}), f32[8,72,128]{2,1,0:T(8,128)S(1)}, u32[]{:S(2)}, u32[]{:S(2)}) async-start(f32[8,72,128]{2,1,0:T(8,128)} %shard_map.304), calls=%async_computation.1 | async-start | bytes 589824 | tf_op jit(solution)/shard_map/all_to_all | solution.py:616
  52.9 0.9 %copy-start.6 = (bf16[256,256]{1,0:T(8,128)(2,1)S(1)}, bf16[256,256]{1,0:T(8,128)(2,1)}, u32[]{:S(2)}) copy-start(bf16[256,256]{1,0:T(8,128)(2,1)} %constant.66.clone.second_b) | copy-start | bytes 393220
  53.8 6.3 %copy-start.4 = (bf16[320,256]{1,0:T(8,128)(2,1)S(1)}, bf16[320,256]{1,0:T(8,128)(2,1)}, u32[]{:S(2)}) copy-start(bf16[320,256]{1,0:T(8,128)(2,1)} %constant.75.clone.blocks_lo) | copy-start | bytes 491524
  53.8 6.3 %copy-start.5 = (bf16[320,256]{1,0:T(8,128)(2,1)S(1)}, bf16[320,256]{1,0:T(8,128)(2,1)}, u32[]{:S(2)}) copy-start(bf16[320,256]{1,0:T(8,128)(2,1)} %constant.74.clone.blocks_hi) | copy-start | bytes 491524
  53.9 6.3 %copy-start.16 = (f32[40,128]{1,0:T(8,128)S(1)}, f32[40,128]{1,0:T(8,128)}, u32[]{:S(2)}) copy-start(f32[40,128]{1,0:T(8,128)} %constant.78.clone.middle) | copy-start | bytes 61444
  53.9 6.3 %copy-start.17 = (bf16[40,32]{1,0:T(8,128)(2,1)S(1)}, bf16[40,32]{1,0:T(8,128)(2,1)}, u32[]{:S(2)}) copy-start(bf16[40,32]{1,0:T(8,128)(2,1)} %constant.77.clone.end_lo) | copy-start | bytes 7684
  53.9 6.3 %copy-start.18 = (bf16[40,32]{1,0:T(8,128)(2,1)S(1)}, bf16[40,32]{1,0:T(8,128)(2,1)}, u32[]{:S(2)}) copy-start(bf16[40,32]{1,0:T(8,128)(2,1)} %constant.76.clone.end_hi) | copy-start | bytes 7684

commit v4 on v3

--- a/solution.py
+++ b/solution.py
@@ -209,31 +209,37 @@
         target[:, pl.ds(to, 1), :] = source[:, y : y + 1, :]
 
 
-def pack_edges(a, b, ka, ap, bp, c, f, edges):
+def pack_edges(a, b, ka, ap, bp, c, f, is_odd, far_pack, near_pack):
     rows = slice(0, YP)
     lane = lax.broadcasted_iota(jnp.int32, (YP, XL), 1)
     first = (0, LANE_B, LANE_K, LANE_PA, LANE_CA, LANE_PB, LANE_CB)
     for i in range(PLANES):
-        whole = [None] * len(edges)
+        before = after = None
         for g in range(3):
-            z = PLANES * g + i
+            z, base = PLANES * g + i, GROUP * g
             if z >= ZP:
                 continue
             av, bv, k, cv = a[z, rows, :], b[z, rows, :], ka[z, rows, :], c[z, rows, :]
             pa = 2.0 * av - ap[z, rows, :] + f[z, rows, :]
             pb = 2.0 * bv - bp[z, rows, :]
-            for n, (to_after, _) in enumerate(edges):
-                tile = None
-                for j, value in reversed(list(enumerate((av, bv, k, pa, cv, pb, cv)))):
-                    moved = pltpu.roll(value, first[j] + 8 * to_after + GROUP * g, 1)
-                    if tile is None:
-                        tile = moved
-                    else:
-                        above = first[j + 1] + (4 * to_after if j + 1 > 2 else 0)
-                        tile = jnp.where(lane < GROUP * g + above, moved, tile)
-                whole[n] = tile if g == 0 else jnp.where(lane < GROUP * g, whole[n], tile)
-        for n, (_, pack) in enumerate(edges):
-            pack[i, :, :] = whole[n]
+            moved = [
+                pltpu.roll(v, at + base, 1) if at + base else v
+                for v, at in zip((av, bv, k, pa, cv, pb, cv), first)
+            ]
+            to_before = to_after = moved[6]
+            for j in reversed(range(6)):
+                to_before = jnp.where(lane < base + first[j + 1], moved[j], to_before)
+                above = base + first[j + 1] - (4 if j >= 2 else 8)
+                covered = lane < above if above else lane >= XL - 8
+                to_after = jnp.where(covered, moved[j], to_after)
+            if g == 0:
+                before, after = to_before, to_after
+            else:
+                before = jnp.where(lane < base, before, to_before)
+                after = jnp.where((lane < base - 8) | (lane >= XL - 8), after, to_after)
+        after = pltpu.roll(after, 8, 1)
+        far_pack[i, :, :] = jnp.where(is_odd, after, before)
+        near_pack[i, :, :] = jnp.where(is_odd, before, after)
 
 
 def pack_kernel(
@@ -262,8 +268,7 @@
     add_forcing(f_out, c_out, index, source, 0)
     for copy in copies[1:]:
         copy.wait()
-    edges = [(odd[0], far_pack), (1 - odd[0], near_pack)]
-    pack_edges(an, bn, ka, ap, bp, c_out, f_out, edges)
+    pack_edges(an, bn, ka, ap, bp, c_out, f_out, odd[0] != 0, far_pack, near_pack)
     flip_rows(far_pack, far_out, flip[0] * odd[0])
     flip_rows(near_pack, near_out, flip[0] * (1 - odd[0]))
 

time: 61.8 us -> 61.6 us (level)
  no operation moved by 1% of the time
where the time goes in v4:
time: 61.6 us; the launch traced here: 61.1 us
  starting transfers between devices  30.4 us (49%)
  waiting for transfers between devices  15.9 us (26%)
  Pallas kernels  12.2 us (20%)
  between operations  1.6 us (3%)
  local copies, waits for them, and re-layouts  1.01 us (2%)
    ppermute x4, starting transfers between devices, swap(): lax.ppermute(value, 'cuts', [(i, (i + 1 if i % 2 == odd else i - 1) % n)...  18 us
    pallas_call x7, Pallas kernels, call(): pl.pallas_call(kernel, out_shape=outs, in_specs=[SMEM_SPEC] * len(scalars...  12.2 us
    all_to_all x1, waiting for transfers between devices, local(): parts = lax.all_to_all(k.reshape(groups, part, XL), 'event', 0, 0)  8.25 us
    all_to_all x1, starting transfers between devices, local(): parts = lax.all_to_all(k.reshape(groups, part, XL), 'event', 0, 0)  7.11 us
    all_to_all x1, starting transfers between devices, local(): whole = lax.all_to_all(spread, 'event', 0, 0).reshape(KROWS, XL)  5.29 us
    all_to_all x1, waiting for transfers between devices, local(): whole = lax.all_to_all(spread, 'event', 0, 0).reshape(KROWS, XL)  4.49 us
    ppermute x4, waiting for transfers between devices, swap(): lax.ppermute(value, 'cuts', [(i, (i + 1 if i % 2 == odd else i - 1) % n)...  3.2 us
  transfers between devices with their start and end apart: 6, of which 3 were waited for; matrix products, arithmetic and copies ran while one was open for 0% of the time, Pallas kernels for 5%

profile of v4, /device:TPU:8, one launch (start us, length us, event | category | flops | bytes accessed | tf_op | source)
XLA Modules:
  0.0 61.1 jit_solution(16666974126132097745)
XLA Ops:
  1.3 0.0 copy-start
  1.3 0.0 copy-start.14
  1.3 0.0 copy-start.15
  1.3 2.8 %shard_map.299 = (f32[6,33,128]{2,1,0:T(8,128)S(1)}, f32[6,33,128]{2,1,0:T(8,128)S(1)}, f32[17,40,128]{2,1,0:T(8,128)S(1)}, f32[17,40,128]{2,1,0:T(8,128)S(1)}, ...) custom-call(s32[1]{0:T(128)S(6)} %copy.33.flip, ...), custom_call_target="tpu_custom_call" | custom-call | bytes 4000000 | tf_op jit(solution)/shard_map/pallas_call | solution.py:537
  4.1 11.8 %collective-permute-start = (f32[6,33,128]{2,1,0:T(8,128)S(1)}, f32[6,33,128]{2,1,0:T(8,128)S(1)}, u32[]{:S(2)}, u32[]{:S(2)}) collective-permute-start(f32[6,33,128]{2,1,0:T(8,128)S(1)} %get-tuple-element.45), channel_id=1, source_target_pairs={{0,504},{8,16},{16,8},{24,32},{32,24},{40,48},{48,40},{56,64},{64,... | collective-permute-start | bytes 304136 | tf_op jit(solution)/shard_map/ppermute | solution.py:550
  15.9 1.9 %collective-permute-start.1 = (f32[6,33,128]{2,1,0:T(8,128)S(1)}, f32[6,33,128]{2,1,0:T(8,128)S(1)}, u32[]{:S(2)}, u32[]{:S(2)}) collective-permute-start(f32[6,33,128]{2,1,0:T(8,128)S(1)} %get-tuple-element.46), channel_id=1, source_target_pairs={{0,8},{8,0},{16,24},{24,16},{32,40},{40,32},{48,56},{56,48},{64,72... | collective-permute-start | bytes 304136 | tf_op jit(solution)/shard_map/ppermute | solution.py:550
  17.8 0.0 copy-done
  17.8 0.0 copy-done.14
  17.9 0.0 copy-done.15
  17.9 0.0 copy-start.1
  17.9 0.0 copy-start.2
  17.9 0.0 copy-start.3
  17.9 0.0 copy-start.7
  17.9 0.0 copy-start.8
  17.9 0.0 copy-start.9
  17.9 0.0 copy-start.10
  17.9 0.0 copy-start.11
  18.0 1.5 %shard_map.300 = (f32[17,40,128]{2,1,0:T(8,128)S(1)}, f32[17,40,128]{2,1,0:T(8,128)S(1)}, f32[17,40,128]{2,1,0:T(8,128)S(1)}, f32[680,256]{1,0:T(8,128)S(1)}, f3...) custom-call(f32[17,40,128]{2,1,0:T(8,128)S(1)} %get-tuple-element.35.a.an, f32[17,40,128]{2,1,0:T(8,128)S(1)} %get-tuple-element.32.b.bn, ...), custom_call_target="tpu_custom_call" | custom-call | flops 300000000 | bytes 5000000 | tf_op jit(solution)/shard_map/pallas_call | solution.py:537
  19.5 0.0 collective-permute-done.far_in
  19.5 0.0 collective-permute-done.1.near_in
  19.5 0.0 copy-done.1
  19.5 0.0 copy-done.2
  19.5 0.0 copy-done.3
  19.5 0.0 copy-done.7
  19.5 0.0 copy-done.8
  19.5 0.0 copy-done.9
  19.5 0.0 copy-done.10
  19.6 0.0 copy-done.11
  19.6 3.9 %shard_map.301 = (f32[576,128]{1,0:T(8,128)}, f32[17,33,1,128]{3,2,1,0:T(1,128)}, f32[17,33,1,128]{3,2,1,0:T(1,128)}, f32[17,40,128]{2,1,0:T(8,128)S(1)}, f32[17...) custom-call(s32[1]{0:T(128)S(6)} %copy.33.flip, s32[1]{0:T(128)} %bitcast.odd, ...), custom_call_target="tpu_custom_call" | custom-call | flops 600000000 | bytes 6000000 | tf_op jit(solution)/shard_map/pallas_call | solution.py:537
  23.4 7.1 %all-to-all-start = ((f32[8,72,128]{2,1,0:T(8,128)}), f32[8,72,128]{2,1,0:T(8,128)S(1)}, u32[]{:S(2)}, u32[]{:S(2)}) async-start(f32[8,72,128]{2,1,0:T(8,128)} %bitcast.14), calls=%async_computation | async-start | bytes 589824 | tf_op jit(solution)/shard_map/all_to_all | solution.py:596
  30.6 8.2 %all-to-all-done.parts = f32[8,72,128]{2,1,0:T(8,128)S(1)} async-done(((f32[8,72,128]{2,1,0:T(8,128)}), f32[8,72,128]{2,1,0:T(8,128)S(1)}, u32[]{:S(2)}, u32[]{:S(2)}) %all-to-all-start) | async-done | bytes 294944 | tf_op jit(solution)/shard_map/all_to_all | solution.py:596
  38.8 0.0 copy-start.12
  38.8 0.0 copy-start.13
  38.8 0.1 shard_map.303
  38.9 2.4 %collective-permute-start.2 = (f32[72,128]{1,0:T(8,128)S(1)}, f32[72,128]{1,0:T(8,128)S(1)}, u32[]{:S(2)}, u32[]{:S(2)}) collective-permute-start(f32[72,128]{1,0:T(8,128)S(1)} %get-tuple-element.56), channel_id=1, source_target_pairs={{0,504},{8,16},{16,8},{24,32},{32,24},{40,48},{48,40},{56,64},{64,... | collective-permute-start | bytes 110600 | tf_op jit(solution)/shard_map/ppermute | solution.py:550
  41.3 1.9 %collective-permute-start.3 = (f32[72,128]{1,0:T(8,128)S(1)}, f32[72,128]{1,0:T(8,128)S(1)}, u32[]{:S(2)}, u32[]{:S(2)}) collective-permute-start(f32[72,128]{1,0:T(8,128)S(1)} %get-tuple-element.58), channel_id=1, source_target_pairs={{0,8},{8,0},{16,24},{24,16},{32,40},{40,32},{48,56},{56,48},{64,72... | collective-permute-start | bytes 110600 | tf_op jit(solution)/shard_map/ppermute | solution.py:550
  43.2 3.2 %collective-permute-done.2.far_in = f32[72,128]{1,0:T(8,128)S(1)} collective-permute-done((f32[72,128]{1,0:T(8,128)S(1)}, f32[72,128]{1,0:T(8,128)S(1)}, u32[]{:S(2)}, u32[]{:S(2)}) %collective-permute-start.2) | collective-permute-done | bytes 36896 | tf_op jit(solution)/shard_map/ppermute | solution.py:550
  46.4 0.0 collective-permute-done.3.near_in
  46.4 0.0 copy-done.12
  46.4 0.0 copy-done.13
  46.4 1.0 %shard_map.304 = f32[8,72,128]{2,1,0:T(8,128)} custom-call(s32[1]{0:T(128)S(6)} %copy.33.flip, s32[1]{0:T(128)} %bitcast.10.group, s32[1]{0:T(128)} %bitcast.odd, f32[72,128]{1,0:T(8,128)S(1)} %collective-permute-done.2.far_in, f32[72,128]{1,0:T(8,128)S(1)} %get-tuple-element.57.own, f32[72,128]{1,0:T(8,128)S(1)} %collective-permute-done.3.near_in, ...), custom_call_target="tpu_custom_call" | custom-call | tf_op jit(solution)/shard_map/pallas_call | solution.py:537
  47.4 5.3 %all-to-all-start.1 = ((f32[8,72,128]{2,1,0:T(8,128)}), f32[8,72,128]{2,1,0:T(8,128)S(1)}, u32[]{:S(2)}, u32[]{:S(2)}) async-start(f32[8,72,128]{2,1,0:T(8,128)} %shard_map.304), calls=%async_computation.1 | async-start | bytes 589824 | tf_op jit(solution)/shard_map/all_to_all | solution.py:621
  52.7 0.0 copy-start.6
  52.7 0.9 %copy-done.6 = bf16[256,256]{1,0:T(8,128)(2,1)S(1)} copy-done((bf16[256,256]{1,0:T(8,128)(2,1)S(1)}, bf16[256,256]{1,0:T(8,128)(2,1)}, u32[]{:S(2)}) %copy-start.6) | copy-done | bytes 131096
  53.6 0.0 copy-start.4
  53.6 0.0 copy-start.5
  53.6 0.0 copy-start.16
  53.6 0.0 copy-start.17
  53.6 0.0 copy-start.18
  53.7 1.8 %shard_map.302 = (f32[17,33,1,128]{3,2,1,0:T(1,128)}, f32[17,33,1,128]{3,2,1,0:T(1,128)}) custom-call(f32[17,40,128]{2,1,0:T(8,128)S(1)} %get-tuple-element.32.b.bn, f32[17,40,128]{2,1,0:T(8,128)S(1)} %get-tuple-element.33.ka, f32[17,40,128]{2,1,0:T(8,128)S(1)} %get-tuple-element.34.c, f32[17,40,128]{2,1,0:T(8,128)S(1)} %get-tuple-element.47.v1b, ...), custom_call_target="tpu_custom_call" | custom-call | flops 300000000 | bytes 5000000 | tf_op jit(solution)/shard_map/pallas_call | solution.py:537
  55.5 4.5 %all-to-all-done.1 = f32[8,72,128]{2,1,0:T(8,128)S(1)} async-done(((f32[8,72,128]{2,1,0:T(8,128)}), f32[8,72,128]{2,1,0:T(8,128)S(1)}, u32[]{:S(2)}, u32[]{:S(2)}) %all-to-all-start.1) | async-done | bytes 294944 | tf_op jit(solution)/shard_map/all_to_all | solution.py:621
  59.9 0.0 copy-done.4
  59.9 0.0 copy-done.5
  60.0 0.0 copy-done.16
  60.0 0.0 copy-done.17
  60.0 0.0 copy-done.18
  60.0 1.1 %shard_map.305 = f32[17,33,128]{2,1,0:T(8,128)} custom-call(f32[576,128]{1,0:T(8,128)S(1)} %bitcast.13, bf16[320,256]{1,0:T(8,128)(2,1)S(1)} %copy-done.5, bf16[320,256]{1,0:T(8,128)(2,1)S(1)} %copy-done.4, bf16[40,32]{1,0:T(8,128)(2,1)S(1)} %copy-done.18, bf16[40,32]{1,0:T(8,128)(2,1)S(1)} %copy-done.17, f32[40,128]{1,0:T(8,128)S(1)} %copy-done.16), custom_call_target="tpu_custom_call" | custom-call | tf_op jit(solution)/shard_map/pallas_call | solution.py:537
Async XLA Ops:
  1.3 16.5 %copy-start = (bf16[256,256]{1,0:T(8,128)(2,1)S(1)}, bf16[256,256]{1,0:T(8,128)(2,1)}, u32[]{:S(2)}) copy-start(bf16[256,256]{1,0:T(8,128)(2,1)} %constant.60.clone.grad) | copy-start | bytes 393220
  1.3 16.5 %copy-start.14 = (bf16[256,128]{1,0:T(8,128)(2,1)S(1)}, bf16[256,128]{1,0:T(8,128)(2,1)}, u32[]{:S(2)}) copy-start(bf16[256,128]{1,0:T(8,128)(2,1)} %constant.62.clone.pick) | copy-start | bytes 196612
  1.3 16.5 %copy-start.15 = (bf16[128,256]{1,0:T(8,128)(2,1)S(1)}, bf16[128,256]{1,0:T(8,128)(2,1)}, u32[]{:S(2)}) copy-start(bf16[128,256]{1,0:T(8,128)(2,1)} %constant.61.clone.grad_lo) | copy-start | bytes 196612
  4.1 15.3 %collective-permute-start = (f32[6,33,128]{2,1,0:T(8,128)S(1)}, f32[6,33,128]{2,1,0:T(8,128)S(1)}, u32[]{:S(2)}, u32[]{:S(2)}) collective-permute-start(f32[6,33,128]{2,1,0:T(8,128)S(1)} %get-tuple-element.45), channel_id=1, source_target_pairs={{0,504},{8,16},{16,8},{24,32},{32,24},{40,48},{48,40},{56,64},{64,... | collective-permute-start | bytes 304136 | tf_op jit(solution)/shard_map/ppermute | solution.py:550
  15.9 3.6 %collective-permute-start.1 = (f32[6,33,128]{2,1,0:T(8,128)S(1)}, f32[6,33,128]{2,1,0:T(8,128)S(1)}, u32[]{:S(2)}, u32[]{:S(2)}) collective-permute-start(f32[6,33,128]{2,1,0:T(8,128)S(1)} %get-tuple-element.46), channel_id=1, source_target_pairs={{0,8},{8,0},{16,24},{24,16},{32,40},{40,32},{48,56},{56,48},{64,72... | collective-permute-start | bytes 304136 | tf_op jit(solution)/shard_map/ppermute | solution.py:550
  17.9 1.6 %copy-start.1 = (bf16[256,256]{1,0:T(8,128)(2,1)S(1)}, bf16[256,256]{1,0:T(8,128)(2,1)}, u32[]{:S(2)}) copy-start(bf16[256,256]{1,0:T(8,128)(2,1)} %constant.71.clone.t_both) | copy-start | bytes 393220
  17.9 1.6 %copy-start.2 = (bf16[256,640]{1,0:T(8,128)(2,1)S(1)}, bf16[256,640]{1,0:T(8,128)(2,1)}, u32[]{:S(2)}) copy-start(bf16[256,640]{1,0:T(8,128)(2,1)} %constant.63.clone.first) | copy-start | bytes 983044
  17.9 1.6 %copy-start.3 = (bf16[128,640]{1,0:T(8,128)(2,1)S(1)}, bf16[128,640]{1,0:T(8,128)(2,1)}, u32[]{:S(2)}) copy-start(bf16[128,640]{1,0:T(8,128)(2,1)} %constant.64.clone.first_lo) | copy-start | bytes 491524
  17.9 1.6 %copy-start.7 = (bf16[256,256]{1,0:T(8,128)(2,1)S(1)}, bf16[256,256]{1,0:T(8,128)(2,1)}, u32[]{:S(2)}) copy-start(bf16[256,256]{1,0:T(8,128)(2,1)} %constant.70.clone.tb_lo) | copy-start | bytes 393220
  17.9 1.6 %copy-start.8 = (bf16[256,256]{1,0:T(8,128)(2,1)S(1)}, bf16[256,256]{1,0:T(8,128)(2,1)}, u32[]{:S(2)}) copy-start(bf16[256,256]{1,0:T(8,128)(2,1)} %constant.69.clone.tb_hi) | copy-start | bytes 393220
  17.9 1.6 %copy-start.9 = (bf16[256,256]{1,0:T(8,128)(2,1)S(1)}, bf16[256,256]{1,0:T(8,128)(2,1)}, u32[]{:S(2)}) copy-start(bf16[256,256]{1,0:T(8,128)(2,1)} %constant.68.clone.ta_lo) | copy-start | bytes 393220
  17.9 1.6 %copy-start.10 = (bf16[256,256]{1,0:T(8,128)(2,1)S(1)}, bf16[256,256]{1,0:T(8,128)(2,1)}, u32[]{:S(2)}) copy-start(bf16[256,256]{1,0:T(8,128)(2,1)} %constant.67.clone.ta_hi) | copy-start | bytes 393220
  17.9 1.6 %copy-start.11 = (bf16[256,256]{1,0:T(8,128)(2,1)S(1)}, bf16[256,256]{1,0:T(8,128)(2,1)}, u32[]{:S(2)}) copy-start(bf16[256,256]{1,0:T(8,128)(2,1)} %constant.65.clone.second_a) | copy-start | bytes 393220
  23.4 15.4 %all-to-all-start = ((f32[8,72,128]{2,1,0:T(8,128)}), f32[8,72,128]{2,1,0:T(8,128)S(1)}, u32[]{:S(2)}, u32[]{:S(2)}) async-start(f32[8,72,128]{2,1,0:T(8,128)} %bitcast.14), calls=%async_computation | async-start | bytes 589824 | tf_op jit(solution)/shard_map/all_to_all | solution.py:596
  38.8 7.6 %copy-start.12 = (bf16[384,128]{1,0:T(8,128)(2,1)S(1)}, bf16[384,128]{1,0:T(8,128)(2,1)}, u32[]{:S(2)}) copy-start(bf16[384,128]{1,0:T(8,128)(2,1)} %constant.73.clone.gx_lo) | copy-start | bytes 294916
  38.8 7.6 %copy-start.13 = (bf16[384,128]{1,0:T(8,128)(2,1)S(1)}, bf16[384,128]{1,0:T(8,128)(2,1)}, u32[]{:S(2)}) copy-start(bf16[384,128]{1,0:T(8,128)(2,1)} %constant.72.clone.gx_hi) | copy-start | bytes 294916
  38.9 7.5 %collective-permute-start.2 = (f32[72,128]{1,0:T(8,128)S(1)}, f32[72,128]{1,0:T(8,128)S(1)}, u32[]{:S(2)}, u32[]{:S(2)}) collective-permute-start(f32[72,128]{1,0:T(8,128)S(1)} %get-tuple-element.56), channel_id=1, source_target_pairs={{0,504},{8,16},{16,8},{24,32},{32,24},{40,48},{48,40},{56,64},{64,... | collective-permute-start | bytes 110600 | tf_op jit(solution)/shard_map/ppermute | solution.py:550
  41.3 5.1 %collective-permute-start.3 = (f32[72,128]{1,0:T(8,128)S(1)}, f32[72,128]{1,0:T(8,128)S(1)}, u32[]{:S(2)}, u32[]{:S(2)}) collective-permute-start(f32[72,128]{1,0:T(8,128)S(1)} %get-tuple-element.58), channel_id=1, source_target_pairs={{0,8},{8,0},{16,24},{24,16},{32,40},{40,32},{48,56},{56,48},{64,72... | collective-permute-start | bytes 110600 | tf_op jit(solution)/shard_map/ppermute | solution.py:550
  47.4 12.5 %all-to-all-start.1 = ((f32[8,72,128]{2,1,0:T(8,128)}), f32[8,72,128]{2,1,0:T(8,128)S(1)}, u32[]{:S(2)}, u32[]{:S(2)}) async-start(f32[8,72,128]{2,1,0:T(8,128)} %shard_map.304), calls=%async_computation.1 | async-start | bytes 589824 | tf_op jit(solution)/shard_map/all_to_all | solution.py:621
  52.7 0.9 %copy-start.6 = (bf16[256,256]{1,0:T(8,128)(2,1)S(1)}, bf16[256,256]{1,0:T(8,128)(2,1)}, u32[]{:S(2)}) copy-start(bf16[256,256]{1,0:T(8,128)(2,1)} %constant.66.clone.second_b) | copy-start | bytes 393220
  53.6 6.3 %copy-start.4 = (bf16[320,256]{1,0:T(8,128)(2,1)S(1)}, bf16[320,256]{1,0:T(8,128)(2,1)}, u32[]{:S(2)}) copy-start(bf16[320,256]{1,0:T(8,128)(2,1)} %constant.75.clone.blocks_lo) | copy-start | bytes 491524
  53.6 6.3 %copy-start.5 = (bf16[320,256]{1,0:T(8,128)(2,1)S(1)}, bf16[320,256]{1,0:T(8,128)(2,1)}, u32[]{:S(2)}) copy-start(bf16[320,256]{1,0:T(8,128)(2,1)} %constant.74.clone.blocks_hi) | copy-start | bytes 491524
  53.6 6.3 %copy-start.16 = (f32[40,128]{1,0:T(8,128)S(1)}, f32[40,128]{1,0:T(8,128)}, u32[]{:S(2)}) copy-start(f32[40,128]{1,0:T(8,128)} %constant.78.clone.middle) | copy-start | bytes 61444
  53.6 6.3 %copy-start.17 = (bf16[40,32]{1,0:T(8,128)(2,1)S(1)}, bf16[40,32]{1,0:T(8,128)(2,1)}, u32[]{:S(2)}) copy-start(bf16[40,32]{1,0:T(8,128)(2,1)} %constant.77.clone.end_lo) | copy-start | bytes 7684
  53.6 6.3 %copy-start.18 = (bf16[40,32]{1,0:T(8,128)(2,1)S(1)}, bf16[40,32]{1,0:T(8,128)(2,1)}, u32[]{:S(2)}) copy-start(bf16[40,32]{1,0:T(8,128)(2,1)} %constant.76.clone.end_hi) | copy-start | bytes 7684
